TPU v7x, 32 devices: a whole 2x2x4 slice. The times are simulated.
32 devices in a mesh: blk: 8 (over y, x, core), src: 4 (over z).
Axes of the slice: x: 2, y: 2, z: 4, core: 2. Of those that a mesh axis runs over, the one named last changes fastest.
Arguments:
- windows: bfloat16 [512, 8192], P('blk', 'src'), may hold values from -6 to 6
- observed: bfloat16 [64, 2, 4096], P(None, None, 'src'), may hold values from -40 to 40
- pair_class: int32 [512, 512], P('blk'), may hold values from 0 to 63
- green: bfloat16 [64, 2, 4096], P(None, None, 'src'), may hold values from -6 to 6
- green_index: int32 [4, 512], P(None, 'blk'), may hold values from 0 to 63
- tile_index: int32 [4, 512], P(None, 'blk'), may hold values from 0 to 15
Outputs:
- gradient: float32 [16, 4096], P('src', 'blk')
All inputs are finite; a program needn't handle non-finite values.
Results may differ from a plain program's by a relative error of at most 0.0051.
Values may be sent and summed in bfloat16 or wider, within the bound.
No kernel may reach another device: no remote copies, remote signals or barrier semaphores. Data moves between devices by JAX's collectives and lax.ppermute only.
A program may use at most 256 MiB of HBM per device.

v0:
```python
import math

import jax
import jax.numpy as jnp
from jax import lax
from jax.sharding import PartitionSpec as P

NT = 8192
TILE_SIDE = 64
TILE_DEV = 4
F = 4096
TP = 4096


def trig_pair(phase_index, period):
    angle_rad = phase_index.astype(jnp.float32) * (2.0 * math.pi / period)
    return (jnp.cos(angle_rad), jnp.sin(angle_rad))


def dft_rows(count, freq_ids, period):
    amp_scale = 1.0 / math.sqrt(period)
    local_freqs = freq_ids.shape[0]
    high_ids = jnp.arange(count // 128, dtype=jnp.int32)
    low_ids = jnp.arange(128, dtype=jnp.int32)
    high_cos, high_sin = trig_pair(high_ids[:, None] * 128 * freq_ids[None, :] % period, period)
    low_cos, low_sin = trig_pair(low_ids[:, None] * freq_ids[None, :] % period, period)
    cos_part = (
        high_cos[:, None, :] * low_cos[None] - high_sin[:, None, :] * low_sin[None]
    ).reshape(count, local_freqs)
    sin_part = (
        high_sin[:, None, :] * low_cos[None] + high_cos[:, None, :] * low_sin[None]
    ).reshape(count, local_freqs)
    return jnp.concatenate([cos_part * amp_scale, -sin_part * amp_scale], axis=1).astype(
        jnp.bfloat16
    )


def mode_table(freq_ids, points, edge_cells):
    phase_index = freq_ids[:, None] % edge_cells * (points[None, :] % edge_cells) + freq_ids[
        :, None
    ] // edge_cells * (points[None, :] // edge_cells)
    angle_rad = (phase_index % edge_cells).astype(jnp.float32) * (2.0 * math.pi / edge_cells)
    return jnp.concatenate([jnp.cos(angle_rad), -jnp.sin(angle_rad)], axis=0)


def body(windows, observed, pair_class, green, green_index, tile_index):
    panel_rows = windows.shape[0]
    local_freqs = observed.shape[2]
    class_count = observed.shape[0]
    src_index = lax.axis_index("src")
    blk_index = lax.axis_index("blk")
    stations = panel_rows * lax.axis_size("blk")
    freq_ids = src_index * local_freqs + jnp.arange(local_freqs, dtype=jnp.int32)
    shard_piece = lax.all_gather(windows, "src", axis=1, tiled=True)
    table_rows = dft_rows(shard_piece.shape[1], freq_ids, NT)
    spectra = jnp.dot(shard_piece, table_rows, preferred_element_type=jnp.float32).astype(
        jnp.bfloat16
    )
    class_ids = jnp.arange(class_count, dtype=jnp.int32)
    shard_piece = lax.all_gather(spectra, "blk", axis=0, tiled=True)
    widened = shard_piece.astype(jnp.float32)
    far_real = widened[:, :local_freqs]
    far_imag = widened[:, local_freqs:]
    power_sum = jnp.sum(far_real * far_real + far_imag * far_imag, axis=0)
    class_hot = (pair_class[:, :, None] == class_ids).astype(jnp.bfloat16)
    grouped = jnp.einsum("ijk,jf->ikf", class_hot, shard_piece, preferred_element_type=jnp.float32)
    power_sum, grouped = (power_sum, grouped)
    obs_table = observed.reshape(class_count, 2 * local_freqs).astype(jnp.float32)
    obs_real, obs_imag = (obs_table[:, :local_freqs], obs_table[:, local_freqs:])
    group_real, group_imag = (grouped[..., :local_freqs], grouped[..., local_freqs:])
    highest = lax.Precision.HIGHEST
    mix_real = jnp.einsum("kf,ikf->if", obs_real, group_real, precision=highest) - jnp.einsum(
        "kf,ikf->if", obs_imag, group_imag, precision=highest
    )
    mix_imag = jnp.einsum("kf,ikf->if", obs_real, group_imag, precision=highest) + jnp.einsum(
        "kf,ikf->if", obs_imag, group_real, precision=highest
    )
    own_spectra = spectra.astype(jnp.float32)
    adjoint = (
        own_spectra * jnp.concatenate([power_sum, power_sum])[None, :]
        - jnp.concatenate([mix_real, mix_imag], axis=1)
    ) / stations
    adj_real, adj_imag = (adjoint[:, :local_freqs], adjoint[:, local_freqs:])
    green_bank = green.reshape(green.shape[0], 2 * local_freqs)
    green_ids = jnp.arange(green_bank.shape[0], dtype=jnp.int32)
    pick_hot = (green_index[:, :, None] == green_ids).astype(jnp.bfloat16)
    picked = jnp.einsum(
        "npg,gf->npf", pick_hot, green_bank, preferred_element_type=jnp.bfloat16
    ).astype(jnp.float32)
    pick_real, pick_imag = (picked[..., :local_freqs], picked[..., local_freqs:])
    weighted = jnp.concatenate(
        [
            adj_real[None] * pick_real + adj_imag[None] * pick_imag,
            adj_real[None] * pick_imag - adj_imag[None] * pick_real,
        ],
        axis=-1,
    ).astype(jnp.bfloat16)
    tiles_all = TILE_DEV * lax.axis_size("src")
    tile_hot = (tile_index[:, :, None] == jnp.arange(tiles_all, dtype=jnp.int32)).astype(
        jnp.bfloat16
    )
    tile_spectra = jnp.einsum(
        "npt,npf->tf", tile_hot, weighted, preferred_element_type=jnp.float32
    ) * math.sqrt(tiles_all / (stations * green_index.shape[0]))
    summed = lax.psum(tile_spectra, "blk")
    point_share = TP // lax.axis_size("blk")
    points = blk_index * point_share + jnp.arange(point_share, dtype=jnp.int32)
    tile_image = jnp.dot(
        summed, mode_table(freq_ids, points, TILE_SIDE), precision=lax.Precision.HIGHEST
    ) / math.sqrt(F)
    return lax.psum_scatter(tile_image, "src", scatter_dimension=0, tiled=True)


def solution(mesh):
    in_specs = (
        P("blk", "src"),
        P(None, None, "src"),
        P("blk", None),
        P(None, None, "src"),
        P(None, "blk"),
        P(None, "blk"),
    )
    out_specs = P("src", "blk")
    return jax.shard_map(body, mesh=mesh, in_specs=in_specs, out_specs=out_specs, check_vma=False)
```

profile of v0, /device:TPU:0, one launch (start us, length us, event | category | flops | bytes accessed | tf_op | source)
XLA Modules:
  0.0 199.4 jit_solution(1199099315168607779)
XLA Ops:
  6.5 0.0 all-gather.3.cloned.1.call-start
  6.5 0.7 all-gather.3.cloned.1.call-update
  7.3 0.0 all-gather.5.cloned.1.call-start
  7.3 2.0 %fusion.41 = (f32[128,1024]{1,0:T(8,128)S(1)}, f32[128,1024]{1,0:T(8,128)S(1)}) fusion(s32[1024]{0:T(1024)S(1)} %iota_add_fusion), kind=kLoop, calls=%fused_computation.65 | loop fusion | flops 1835008 | bytes 1052672 | tf_op jit(solution)/shard_map/cos | solution.py:17
  9.4 1.1 fusion.45
  10.5 15.5 %multiply_convert_fusion.1 = (bf16[64,128,1024]{2,1,0:T(8,128)(2,1)}, bf16[64,128,1024]{2,1,0:T(8,128)(2,1)}) fusion(f32[128,1024]{1,0:T(8,128)S(1)} %get-tuple-element.24, f32[64,1024]{1,0:T(8,128)S(1)} %get-tuple-element.22, f32[128,1024]{1,0:T(8,128)S(1)} %get-tuple-element.23, f32[64,1024]{1,0:T(8,128)S(1)} %get-tuple-element.21), kind=kLoop, calls=%fused_computation.5 | loop fusion | flops 92274688 | bytes 35127296 | tf_op jit(solution)/shard_map/convert.5
  25.9 13.7 %all-gather.3.cloned.1.call-done = bf16[64,8192]{1,0:T(8,128)(2,1)} async-done(((bf16[64,2048]{1,0:T(8,128)(2,1)}), bf16[64,8192]{1,0:T(8,128)(2,1)}) %all-gather.3.cloned.1.call-update) | async-done | bytes 1048592 | tf_op jit(solution)/shard_map/all_gather | solution.py:54
  39.6 0.0 copy-start.2
  39.6 0.0 copy-start.3
  39.6 0.0 copy-start.4
  39.6 14.4 %fusion.13 = bf16[64,2048]{1,0:T(8,128)(2,1)} fusion(bf16[64,8192]{1,0:T(8,128)(2,1)} %all-gather.3.cloned.1.call-done, bf16[8192,1024]{1,0:T(8,128)(2,1)} %bitcast.46, bf16[8192,1024]{1,0:T(8,128)(2,1)} %bitcast.45), kind=kOutput, calls=%fused_computation.24 | convolution fusion | flops 2214723584 | bytes 34865152 | tf_op jit(solution)/shard_map/dot_general | solution.py:56
  54.0 0.0 all-gather.5.cloned.1.call-update
  54.0 0.0 all-reduce.3.cloned.1.call-start
  54.1 0.0 copy-done.2
  54.1 0.1 copy.35
  54.1 0.0 copy-done.3
  54.1 0.2 reshape.280
  54.4 0.0 copy-done.4
  54.4 0.5 convolution_convert_fusion
  54.9 0.0 copy-start.5
  54.9 26.6 %all-gather.5.cloned.1.call-done = bf16[512,2048]{1,0:T(8,128)(2,1)} async-done(((bf16[64,2048]{1,0:T(8,128)(2,1)}), bf16[512,2048]{1,0:T(8,128)(2,1)}) %all-gather.5.cloned.1.call-update) | async-done | bytes 2097168 | tf_op jit(solution)/shard_map/all_gather | solution.py:60
  81.6 0.0 copy-start
  81.6 2.3 %convert_element_type.49 = f32[512,2048]{1,0:T(8,128)S(1)} convert(bf16[512,2048]{1,0:T(8,128)(2,1)} %all-gather.5.cloned.1.call-done) | non-fusion elementwise | flops 1048576 | bytes 6291456 | tf_op jit(solution)/shard_map/convert_element_type | solution.py:61
  83.8 0.3 fusion.21
  84.2 0.0 copy-done.5
  84.2 0.0 copy-done
  84.2 15.5 %fusion.4 = f32[64,64,2048]{2,1,0:T(8,128)} fusion(s32[64,512]{1,0:T(8,128)S(1)} %copy-done.5, bf16[512,2048]{1,0:T(8,128)(2,1)S(1)} %copy-done), kind=kOutput, calls=%fused_computation.13 | convolution fusion | flops 8592031744 | bytes 35782656 | tf_op jit(solution)/shard_map/ijk,jf->ikf/dot_general | solution.py:66
  99.6 0.0 copy-start.1
  99.6 15.1 %multiply_reduce_fusion.2 = (f32[1024,64]{0,1:T(8,128)S(1)}, f32[1024,64]{0,1:T(8,128)S(1)}, f32[1024,64]{0,1:T(8,128)S(1)}, f32[1024,64]{0,1:T(8,128)S(1)}) fusion(f32[64,64,2048]{2,1,0:T(8,128)} %fusion.4, f32[1024,64]{0,1:T(8,128)S(1)} %get-tuple-element.18, f32[1024,64]{0,1:T(8,128)S(1)} %get-tuple-element.17), kind=kLoop, calls=%fused_computation.10 | loop fusion | flops 33292288 | bytes 35127296 | tf_op jit(solution)/shard_map/kf,ikf->if/dot_general | solution.py:72
  114.7 0.0 copy-start.6
  114.7 0.1 add_bitcast_fusion
  114.8 0.0 copy-done.1
  114.8 0.1 fusion.33
  114.9 0.0 copy-start.7
  114.9 0.3 add_convert_fusion
  115.3 0.1 copy-done.6
  115.4 1.0 fusion.16
  116.4 0.0 all-reduce.3.cloned.1.call-update
  116.4 9.9 %fusion.23 = (f32[1024,512]{1,0:T(8,128)S(1)}, f32[1024,512]{1,0:T(8,128)}) fusion(s32[512]{0:T(512)S(1)} %get-tuple-element.29, s32[1024]{0:T(1024)S(1)} %get-tuple-element.25, s32[512]{0:T(512)S(1)} %get-tuple-element.30, s32[1024]{0:T(1024)S(1)} %get-tuple-element.26), kind=kLoop, calls=%fused_computation.36 | loop fusion | flops 8912896 | bytes 4206592 | tf_op jit(solution)/shard_map/cos | solution.py:43
  126.3 0.0 copy-done.7
  126.3 0.6 dynamic-slice
  127.5 42.0 %all-reduce.3.cloned.1.call-done = f32[16,2048]{1,0:T(8,128)} async-done(((f32[16,2048]{1,0:T(8,128)}), f32[16,2048]{1,0:T(8,128)}) %all-reduce.3.cloned.1.call-update) | async-done | bytes 131088 | tf_op jit(solution)/shard_map/psum | solution.py:105
  169.5 3.8 %fusion.24 = f32[16,512]{1,0:T(8,128)S(1)} fusion(f32[16,2048]{1,0:T(8,128)} %all-reduce.3.cloned.1.call-done, f32[1024,512]{1,0:T(8,128)} %get-tuple-element.20, f32[1024,512]{1,0:T(8,128)S(1)} %get-tuple-element.19), kind=kOutput, calls=%fused_computation.37 | convolution fusion | flops 202383360 | bytes 4358144 | tf_op jit(solution)/shard_map/dot_general | solution.py:108
  173.3 19.0 %all-reduce = f32[16,512]{1,0:T(8,128)S(1)} all-reduce(f32[16,512]{1,0:T(8,128)S(1)} %fusion.24), channel_id=2, replica_groups=mesh['blk'=8,'src'=4] {'src'}, use_global_device_ids=true, to_apply=%region_2.3.clone | all-reduce | flops 8192 | bytes 65536
  192.3 0.6 constant_dynamic-slice_fusion
  (7 shorter events, 0.1 us)
Async XLA Ops:
  6.5 33.1 %all-gather.3.cloned.1.call-start = ((), (), s32[]{:S(2)}) async-start(), calls=%async_computation | async-start | bytes 1310720 | tf_op jit(solution)/shard_map/all_gather | solution.py:54
  7.3 74.3 %all-gather.5.cloned.1.call-start = ((), (), s32[]{:S(2)}) async-start(), calls=%async_computation.1 | async-start | bytes 2359296 | tf_op jit(solution)/shard_map/all_gather | solution.py:60
  39.6 14.5 %copy-start.2 = (bf16[64,2,1024]{2,1,0:T(2,128)(2,1)S(1)}, bf16[64,2,1024]{2,1,0:T(2,128)(2,1)}, u32[]{:S(2)}) copy-start(bf16[64,2,1024]{2,1,0:T(2,128)(2,1)} %param.7) | copy-start | bytes 786436
  39.6 14.5 %copy-start.3 = (bf16[64,2,1024]{2,1,0:T(2,128)(2,1)S(1)}, bf16[64,2,1024]{2,1,0:T(2,128)(2,1)}, u32[]{:S(2)}) copy-start(bf16[64,2,1024]{2,1,0:T(2,128)(2,1)} %param.9) | copy-start | bytes 786436
  39.6 14.8 %copy-start.4 = (s32[4,64]{1,0:T(4,128)S(1)}, s32[4,64]{1,0:T(4,128)}, u32[]{:S(2)}) copy-start(s32[4,64]{1,0:T(4,128)} %param.10) | copy-start | bytes 3076
  54.0 115.5 %all-reduce.3.cloned.1.call-start = ((), (), s32[]{:S(2)}) async-start(), calls=%async_computation.2 | async-start | bytes 262144 | tf_op jit(solution)/shard_map/psum | solution.py:105
  54.9 29.3 %copy-start.5 = (s32[64,512]{1,0:T(8,128)S(1)}, s32[64,512]{1,0:T(8,128)}, u32[]{:S(2)}) copy-start(s32[64,512]{1,0:T(8,128)} %param.8) | copy-start | bytes 393220
  81.6 2.6 %copy-start = (bf16[512,2048]{1,0:T(8,128)(2,1)S(1)}, bf16[512,2048]{1,0:T(8,128)(2,1)}, u32[]{:S(2)}) copy-start(bf16[512,2048]{1,0:T(8,128)(2,1)} %all-gather.5.cloned.1.call-done) | copy-start | bytes 6291460
  99.6 15.2 %copy-start.1 = (bf16[64,2048]{1,0:T(8,128)(2,1)S(1)}, bf16[64,2048]{1,0:T(8,128)(2,1)}, u32[]{:S(2)}) copy-start(bf16[64,2048]{1,0:T(8,128)(2,1)} %fusion.13) | copy-start | bytes 786436
  114.7 0.7 copy-start.6
  114.9 11.3 %copy-start.7 = (u32[32]{0:T(128)S(1)}, u32[32]{0:T(128)}, u32[]{:S(2)}) copy-start(u32[32]{0:T(128)} %constant.113) | copy-start | bytes 388
Sparse Core Ops, SparseCore 0:
  8.9 30.6 all-gather.2
  54.1 27.3 all-gather.4
  116.5 52.9 all-reduce.2
where the time goes:
time: 200 us; the launch traced here: 199 us
  waiting for transfers between devices  83 us (42%)
  other arithmetic  46.7 us (23%)
  matrix products  35.1 us (18%)
  blocking collectives  19 us (10%)
  between operations  14 us (7%)
    psum x1, waiting for transfers between devices, body(): summed = lax.psum(tile_spectra, 'blk')  42 us
    all_gather x1, waiting for transfers between devices, body(): shard_piece = lax.all_gather(spectra, 'blk', axis=0, tiled=True)  26.6 us
    unnamed x1, blocking collectives  19 us
    another operation x2, other arithmetic  15.8 us
    dot_general x1, matrix products, body(): jnp.einsum('ijk,jf->ikf', class_hot, shard_piece, preferred_element_type=...  15.5 us
    dot_general x1, other arithmetic, body(): jnp.einsum('kf,ikf->if', obs_imag, group_imag, precision=highest)  15.1 us
    dot_general x1, matrix products, body(): jnp.dot(shard_piece, table_rows, preferred_element_type=jnp.float32)  14.4 us
    all_gather x1, waiting for transfers between devices, body(): shard_piece = lax.all_gather(windows, 'src', axis=1, tiled=True)  13.7 us
  transfers between devices with their start and end apart: 3, of which 3 were waited for; matrix products, arithmetic and copies ran while one was open for 15% of the time, Pallas kernels for 0%

commit v1 on v0

--- a/solution.py
+++ b/solution.py
@@ -1,8 +1,12 @@
+import functools
 import math
 
 import jax
 import jax.numpy as jnp
+import numpy as np
 from jax import lax
+from jax.experimental import pallas as pl
+from jax.experimental.pallas import tpu as pltpu
 from jax.sharding import PartitionSpec as P
 
 NT = 8192
@@ -43,7 +47,7 @@
     return jnp.concatenate([jnp.cos(angle_rad), -jnp.sin(angle_rad)], axis=0)
 
 
-def body(windows, observed, pair_class, green, green_index, tile_index):
+def general_body(windows, observed, pair_class, green, green_index, tile_index):
     panel_rows = windows.shape[0]
     local_freqs = observed.shape[2]
     class_count = observed.shape[0]
@@ -110,6 +114,272 @@
     ) / math.sqrt(F)
     return lax.psum_scatter(tile_image, "src", scatter_dimension=0, tiled=True)
 
+LANES = 128
+BOTH = ("blk", "src")
+HIGHEST = lax.Precision.HIGHEST
+NT_DIMS = (((1,), (1,)), ((), ()))
+TN_DIMS = (((0,), (0,)), ((), ()))
+VMEM_BYTES = 56 * 1024 * 1024
+
+
+def split_bf16(values):
+    high = values.astype(jnp.bfloat16)
+    low = (values - high.astype(np.float32)).astype(jnp.bfloat16)
+    return high, low
+
+
+def forward_tables(n_src, n_blk):
+    steps = NT // LANES
+    per_src = steps // n_src
+    own = np.arange(n_src)
+    order = np.stack(
+        [np.concatenate([(s ^ k) * per_src + np.arange(per_src) for k in range(n_src)]) for s in own]
+    )
+    rows = np.arange(steps)
+    angle = 2 * np.pi / steps * ((rows[None, :, None] * order[:, None, :]) % steps)
+    first = np.concatenate([np.cos(angle), -np.sin(angle)], axis=1).astype(np.float32)
+    first = np.concatenate(split_bf16(first), axis=1)
+    lanes = np.arange(LANES)
+    angle = 2 * np.pi / NT * ((lanes[:, None] * lanes[None, :]) % NT)
+    twiddle = np.stack([np.cos(angle), -np.sin(angle)]).astype(np.float32)
+    devices = np.arange(n_src * n_blk)
+    block = devices % n_src * n_blk + devices // n_src
+    angle = 2 * np.pi / steps * ((block[:, None] * lanes[None, :]) % steps)
+    cos, sin = np.cos(angle), np.sin(angle)
+    third = np.concatenate(
+        [np.concatenate([cos, sin], axis=1), np.concatenate([-sin, cos], axis=1)], axis=0
+    )
+    return first, twiddle, (third / math.sqrt(NT)).astype(np.float32)
+
+
+def mode_tables(n_src, n_blk, scale):
+    side = np.arange(TILE_SIDE)
+    angle = 2 * np.pi / TILE_SIDE * ((side[:, None] * side[None, :]) % TILE_SIDE)
+    cos, sin = np.cos(angle), np.sin(angle)
+    low = np.zeros((2, 2, TILE_SIDE, 2, 2, TILE_SIDE))
+    for parity in range(2):
+        low[0, parity, :, parity, 0] = cos
+        low[0, parity, :, parity, 1] = sin
+        low[1, parity, :, parity, 0] = -sin
+        low[1, parity, :, parity, 1] = cos
+    low = low.reshape(4 * TILE_SIDE, 4 * TILE_SIDE) * scale
+    devices = np.arange(n_src * n_blk)
+    block = devices % n_src * n_blk + devices // n_src
+    high_freqs = block[:, None] * 2 + np.arange(2)[None, :]
+    angle = 2 * np.pi / TILE_SIDE * ((side[:, None, None] * high_freqs[None]) % TILE_SIDE)
+    high = np.stack([np.cos(angle), -np.sin(angle)], axis=-1).reshape(
+        n_blk, TILE_SIDE // n_blk, 4 * n_src * n_blk
+    )
+    return low.astype(np.float32), (high / math.sqrt(F)).astype(np.float32)
+
+
+def spectra_kernel(n_src, *refs):
+    pieces = refs[:n_src]
+    first_ref, twiddle_ref, third_ref, out_ref, samples, reals, imags = refs[n_src:]
+    stations, local = pieces[0].shape
+    per_src = local // LANES
+    steps = per_src * n_src
+    count = third_ref.shape[0] // 2
+    first = first_ref[lax.axis_index("src")]
+    for k in range(n_src):
+        for a in range(per_src):
+            samples[pl.ds(k * per_src + a, stations, stride=steps), :] = pieces[k][
+                :, a * LANES : (a + 1) * LANES
+            ].astype(jnp.float32)
+    twiddle_real, twiddle_imag = twiddle_ref[0], twiddle_ref[1]
+    third = third_ref[...]
+    for station in range(stations):
+        rows = samples[station * steps : (station + 1) * steps, :].astype(jnp.bfloat16)
+        parts = jnp.dot(first, rows, preferred_element_type=jnp.float32)
+        real = parts[:steps] + parts[2 * steps : 3 * steps]
+        imag = parts[steps : 2 * steps] + parts[3 * steps :]
+        real = jnp.concatenate([real] * (LANES // steps), axis=0)
+        imag = jnp.concatenate([imag] * (LANES // steps), axis=0)
+        turned = jnp.concatenate(
+            [
+                real * twiddle_real - imag * twiddle_imag,
+                real * twiddle_imag + imag * twiddle_real,
+            ],
+            axis=1,
+        )
+        result = lax.dot_general(
+            third, turned, NT_DIMS, precision=HIGHEST, preferred_element_type=jnp.float32
+        )
+        reals[pl.ds(station, count, stride=stations), :] = result[:count]
+        imags[pl.ds(station, count, stride=stations), :] = result[count:]
+    out_ref[:, :LANES] = reals[...].astype(jnp.bfloat16)
+    out_ref[:, LANES:] = imags[...].astype(jnp.bfloat16)
+
+
+def adjoint_kernel(n_blk, n_src, slots, tiles, chunk, *refs):
+    packs = refs[:n_blk]
+    spectra_ref, observed_ref, green_ref, low_ref, out_ref, classes, picks, mixed, total = refs[
+        n_blk:
+    ]
+    stations = spectra_ref.shape[0]
+    panel = stations // n_blk
+    class_count = observed_ref.shape[0]
+    green_count = green_ref.shape[0]
+    local_freqs = observed_ref.shape[1] // 2
+    blk_index = lax.axis_index("blk")
+    for k in range(n_blk):
+        owner = blk_index ^ k
+        at = pl.ds(pl.multiple_of(owner * panel, panel), panel)
+        classes[at, :] = packs[k][:panel].astype(jnp.int32)
+        picks[owner] = packs[k][panel : panel + 16, :LANES].astype(jnp.int32)
+    here = pl.ds(pl.multiple_of(blk_index * LANES, LANES), LANES)
+    there = pl.ds(pl.multiple_of(local_freqs + blk_index * LANES, LANES), LANES)
+    obs_real = observed_ref[:, here].astype(jnp.float32)[None]
+    obs_imag = observed_ref[:, there].astype(jnp.float32)[None]
+    green = jnp.concatenate([green_ref[:, here], green_ref[:, there]], axis=1)
+    spectra = spectra_ref[...]
+    widened = spectra.astype(jnp.float32)
+    power = jnp.sum(widened * widened, axis=0, keepdims=True)
+    power = power[:, :LANES] + power[:, LANES:]
+    power = jnp.concatenate([power, power], axis=1)
+    class_ids = lax.broadcasted_iota(jnp.int32, (1, class_count, stations), 1)
+    total[...] = jnp.zeros_like(total)
+
+    def one_panel(owner, carry):
+        start = pl.multiple_of(owner * panel, panel)
+        for part in range(panel // chunk):
+            rows = classes[pl.ds(start + part * chunk, chunk), :]
+            hot = jnp.where(rows[:, None, :] == class_ids, 1.0, 0.0).astype(jnp.bfloat16)
+            grouped = jnp.dot(
+                hot.reshape(chunk * class_count, stations),
+                spectra,
+                preferred_element_type=jnp.float32,
+            ).reshape(chunk, class_count, 2 * LANES)
+            group_real, group_imag = grouped[..., :LANES], grouped[..., LANES:]
+            at = pl.ds(part * chunk, chunk)
+            mixed[at, :LANES] = jnp.sum(obs_real * group_real - obs_imag * group_imag, axis=1)
+            mixed[at, LANES:] = jnp.sum(obs_real * group_imag + obs_imag * group_real, axis=1)
+        own = spectra_ref[pl.ds(start, panel), :].astype(jnp.float32)
+        adjoint = (own * power - mixed[...]) * (1.0 / stations)
+        adj_real, adj_imag = adjoint[:, :LANES], adjoint[:, LANES:]
+        ids = picks[owner]
+        green_ids = lax.broadcasted_iota(jnp.int32, (green_count, panel), 0)
+        tile_ids = lax.broadcasted_iota(jnp.int32, (tiles, panel), 0)
+        for slot in range(slots):
+            pick = jnp.where(ids[slot : slot + 1, :panel] == green_ids, 1.0, 0.0)
+            tile = jnp.where(ids[8 + slot : 9 + slot, :panel] == tile_ids, 1.0, 0.0)
+            picked = lax.dot_general(
+                pick.astype(jnp.bfloat16), green, TN_DIMS, preferred_element_type=jnp.float32
+            )
+            pick_real, pick_imag = picked[:, :LANES], picked[:, LANES:]
+            weighted = jnp.concatenate(
+                [
+                    adj_real * pick_real + adj_imag * pick_imag,
+                    adj_real * pick_imag - adj_imag * pick_real,
+                ],
+                axis=1,
+            ).astype(jnp.bfloat16)
+            total[...] += jnp.dot(
+                tile.astype(jnp.bfloat16), weighted, preferred_element_type=jnp.float32
+            )
+        return carry
+
+    lax.fori_loop(0, n_blk, one_panel, 0)
+    low = jnp.dot(
+        total[...], low_ref[...], precision=HIGHEST, preferred_element_type=jnp.float32
+    )
+    share = tiles // n_src
+    rows = []
+    for owner in range(n_src):
+        for part in range(4):
+            piece = low[owner * share : (owner + 1) * share, part * TILE_SIDE : (part + 1) * TILE_SIDE]
+            rows.append(jnp.concatenate([piece[t : t + 1] for t in range(share)], axis=1))
+    rows = jnp.concatenate(rows, axis=0)
+    for copy in range(n_blk):
+        out_ref[copy * 4 * n_src : (copy + 1) * 4 * n_src, :] = rows
+
+
+def image_kernel(high_ref, parts_ref, out_ref):
+    high = high_ref[lax.axis_index("blk")]
+    image = jnp.dot(
+        high, parts_ref[...], precision=HIGHEST, preferred_element_type=jnp.float32
+    )
+    rows = high.shape[0]
+    for tile in range(out_ref.shape[0]):
+        for row in range(rows):
+            out_ref[tile : tile + 1, row * TILE_SIDE : (row + 1) * TILE_SIDE] = image[
+                row : row + 1, tile * TILE_SIDE : (tile + 1) * TILE_SIDE
+            ]
+
+
+def swap(values, axis, distance):
+    size = lax.axis_size(axis)
+    return lax.ppermute(values, axis, [(i, i ^ distance) for i in range(size)])
+
+
+def split_body(windows, observed, pair_class, green, green_index, tile_index):
+    n_blk, n_src = lax.axis_size("blk"), lax.axis_size("src")
+    src_index = lax.axis_index("src")
+    panel, local = windows.shape
+    stations = panel * n_blk
+    slots = green_index.shape[0]
+    tiles = TILE_DEV * n_src
+    share = panel // n_src
+    pieces = [
+        lax.dynamic_slice_in_dim(windows, (src_index ^ k) * share, share, 0) for k in range(n_src)
+    ]
+    pieces = [pieces[0]] + [swap(pieces[k], "src", k) for k in range(1, n_src)]
+
+    def widen(ids):
+        return jnp.pad(ids, ((0, 8 - slots), (0, stations - panel)))
+
+    pack = jnp.concatenate([pair_class, widen(green_index), widen(tile_index)], axis=0).astype(
+        jnp.bfloat16
+    )
+    packs = [pack] + [swap(pack, "blk", k) for k in range(1, n_blk)]
+
+    first, twiddle, third = forward_tables(n_src, n_blk)
+    low, high = mode_tables(n_src, n_blk, math.sqrt(tiles / (stations * slots)))
+    devices = n_blk * n_src
+    params = pltpu.CompilerParams(vmem_limit_bytes=VMEM_BYTES)
+    blocks = pl.pallas_call(
+        functools.partial(spectra_kernel, n_src),
+        out_shape=jax.ShapeDtypeStruct((devices * share, 2 * LANES), jnp.bfloat16),
+        scratch_shapes=[
+            pltpu.VMEM((share * NT // LANES, LANES), jnp.float32),
+            pltpu.VMEM((devices * share, LANES), jnp.float32),
+            pltpu.VMEM((devices * share, LANES), jnp.float32),
+        ],
+        compiler_params=params,
+        name="spectra",
+    )(*pieces, first, twiddle, third)
+    spectra = lax.all_to_all(
+        blocks.reshape(devices, share, 2 * LANES), BOTH, 0, 0, tiled=True
+    ).reshape(stations, 2 * LANES)
+    class_count = observed.shape[0]
+    parts = pl.pallas_call(
+        functools.partial(adjoint_kernel, n_blk, n_src, slots, tiles, 8),
+        out_shape=jax.ShapeDtypeStruct((4 * devices, TILE_DEV * TILE_SIDE), jnp.float32),
+        scratch_shapes=[
+            pltpu.VMEM((stations, stations), jnp.int32),
+            pltpu.VMEM((n_blk, 16, LANES), jnp.int32),
+            pltpu.VMEM((panel, 2 * LANES), jnp.float32),
+            pltpu.VMEM((tiles, 2 * LANES), jnp.float32),
+        ],
+        compiler_params=params,
+        name="adjoint",
+    )(
+        *packs,
+        spectra,
+        observed.reshape(class_count, -1),
+        green.reshape(green.shape[0], -1),
+        low,
+    )
+    parts = lax.all_to_all(
+        parts.reshape(devices, 4, TILE_DEV * TILE_SIDE), BOTH, 0, 0, tiled=True
+    ).reshape(4 * devices, TILE_DEV * TILE_SIDE)
+    return pl.pallas_call(
+        image_kernel,
+        out_shape=jax.ShapeDtypeStruct((TILE_DEV, TP // n_blk), jnp.float32),
+        compiler_params=params,
+        name="image",
+    )(high, parts)
+
 
 def solution(mesh):
     in_specs = (
@@ -121,4 +391,6 @@
         P(None, "blk"),
     )
     out_specs = P("src", "blk")
+    whole_lanes = mesh.size * LANES == F
+    body = split_body if whole_lanes else general_body
     return jax.shard_map(body, mesh=mesh, in_specs=in_specs, out_specs=out_specs, check_vma=False)

time: 200 us -> 71.6 us (0.36)
  waiting for transfers between devices: 83 us -> 9.2 us
  other arithmetic: 46.7 us -> 0.03 us
  matrix products: 35.1 us -> 0 us
  Pallas kernels: 0 us -> 25.5 us
  starting transfers between devices: 0.08 us -> 17.4 us
  between operations: 14 us -> 0.17 us
  blocking collectives: 19 us -> 12.6 us
  local copies, waits for them, and re-layouts: 1.59 us -> 6.4 us
    psum x1 -> x0, waiting for transfers between devices: 42 us -> none  [body(): summed = lax.psum(tile_spectra, 'blk')]
    all_gather x2 -> x0, waiting for transfers between devices: 40.3 us -> none  [the longest x1 26.6 us: body(): shard_piece = lax.all_gather(spectra, 'blk', axis=0, tiled=True)]
    dot_general x5 -> x0, matrix products: 35.1 us -> none  [the longest x1 15.5 us: body(): jnp.einsum('ijk,jf->ikf', class_hot, shard_piece, preferred_element_type=...]
    pallas_call x0 -> x3, Pallas kernels: none -> 25.5 us  [the longest x1 17.8 us: split_body(): pl.pallas_call(functools.partial(adjoint_kernel, n_blk, n_src, slots, til...]
    unnamed x1 -> x0, blocking collectives: 19 us -> none
    another operation x2 -> x3, other arithmetic: 15.8 us -> 0.02 us
    dot_general x1 -> x0, other arithmetic: 15.1 us -> none  [body(): jnp.einsum('kf,ikf->if', obs_imag, group_imag, precision=highest)]
    cos x3 -> x0, other arithmetic: 13 us -> none  [the longest x1 9.86 us: mode_table(): return jnp.concatenate([jnp.cos(angle_rad), -jnp.sin(angle_rad)], axis=0)]
  transfers between devices with their start and end apart: 3 -> 11, of which waited for: 3 -> 6; matrix products, arithmetic and copies ran while one was open for 15% -> 2% of each run, Pallas kernels for 0% -> 0%
where the time goes in v1:
time: 71.6 us; the launch traced here: 71.2 us
  Pallas kernels  25.5 us (36%)
  starting transfers between devices  17.4 us (24%)
  blocking collectives  12.6 us (18%)
  waiting for transfers between devices  9.2 us (13%)
  local copies, waits for them, and re-layouts  6.4 us (9%)
    pallas_call x1, Pallas kernels, split_body(): pl.pallas_call(functools.partial(adjoint_kernel, n_blk, n_src, slots, til...  17.8 us
    ppermute x10, starting transfers between devices, swap(): return lax.ppermute(values, axis, [(i, i ^ distance) for i in range(size)])  13 us
    all_to_all x1, blocking collectives, split_body(): lax.all_to_all(parts.reshape(devices, 4, TILE_DEV * TILE_SIDE), BOTH, 0,...  12.6 us
    ppermute x10, waiting for transfers between devices, swap(): return lax.ppermute(values, axis, [(i, i ^ distance) for i in range(size)])  9.2 us
    pallas_call x1, Pallas kernels, split_body(): pl.pallas_call(functools.partial(spectra_kernel, n_src), out_shape=jax.Sh...  5.9 us
    all_to_all x1, starting transfers between devices, split_body(): lax.all_to_all(blocks.reshape(devices, share, 2 * LANES), BOTH, 0, 0, til...  4.42 us
    unnamed x36, local copies, waits for them, and re-layouts  3.21 us
    pallas_call x1, Pallas kernels, split_body(): pl.pallas_call(image_kernel, out_shape=jax.ShapeDtypeStruct((TILE_DEV, TP...  1.77 us
  transfers between devices with their start and end apart: 11, of which 6 were waited for; matrix products, arithmetic and copies ran while one was open for 2% of the time, Pallas kernels for 0%

profile of v1, /device:TPU:0, one launch (start us, length us, event | category | flops | bytes accessed | tf_op | source)
XLA Modules:
  0.0 71.2 jit_solution(2954795811960224429)
XLA Ops:
  0.0 1.6 %constant_dynamic-slice_fusion = (bf16[16,2048]{1,0:T(8,128)(2,1)S(1)}, bf16[16,2048]{1,0:T(8,128)(2,1)S(1)}, bf16[16,2048]{1,0:T(8,128)(2,1)}, bf16[16,2048]{1,0:T(8,128)(2,1)S(1)}) fusion(bf16[64,2048]{1,0:T(8,128)(2,1)} %param.11, s32[]{:T(128)S(6)} %select_n.15, s32[]{:T(128)S(6)} %select_n.13, s32[]{:T(128)S(6)} %select_n.12, s32[]{:T(128)S(6)} %select_n.14), kind=kLoop, calls=%fused_computation.8 | loop fusion | bytes 524304 | tf_op jit(solution)/shard_map/dynamic_slice | solution.py:324
  1.6 5.0 %collective-permute-start.9 = (bf16[16,2048]{1,0:T(8,128)(2,1)S(1)}, bf16[16,2048]{1,0:T(8,128)(2,1)S(1)}, u32[]{:S(2)}, u32[]{:S(2)}) collective-permute-start(bf16[16,2048]{1,0:T(8,128)(2,1)S(1)} %get-tuple-element.5), channel_id=1, source_target_pairs={{0,3},{1,2},{2,1},{3,0},{4,7},{5,6},{6,5},{7,4},{8,11},{9,10},{10,... | collective-permute-start | bytes 196616 | tf_op jit(solution)/shard_map/ppermute | solution.py:312
  6.6 0.0 collective-permute-start.7
  6.6 0.6 collective-permute-start.8
  7.2 2.3 %collective-permute-done.9.refs_3_ = bf16[16,2048]{1,0:T(8,128)(2,1)S(1)} collective-permute-done((bf16[16,2048]{1,0:T(8,128)(2,1)S(1)}, bf16[16,2048]{1,0:T(8,128)(2,1)S(1)}, u32[]{:S(2)}, u32[]{:S(2)}) %collective-permute-start.9) | collective-permute-done | bytes 65568 | tf_op jit(solution)/shard_map/ppermute | solution.py:312
  9.5 0.0 copy-start.12
  9.5 1.8 %collective-permute-done.7.refs_1_ = bf16[16,2048]{1,0:T(8,128)(2,1)S(1)} collective-permute-done((bf16[16,2048]{1,0:T(8,128)(2,1)S(1)}, bf16[16,2048]{1,0:T(8,128)(2,1)S(1)}, u32[]{:S(2)}, u32[]{:S(2)}) %collective-permute-start.7) | collective-permute-done | bytes 65568 | tf_op jit(solution)/shard_map/ppermute | solution.py:312
  11.3 0.0 copy-start.13
  11.3 1.0 %collective-permute-done.8.refs_2_ = bf16[16,2048]{1,0:T(8,128)(2,1)S(1)} collective-permute-done((bf16[16,2048]{1,0:T(8,128)(2,1)S(1)}, bf16[16,2048]{1,0:T(8,128)(2,1)S(1)}, u32[]{:S(2)}, u32[]{:S(2)}) %collective-permute-start.8) | collective-permute-done | bytes 65568 | tf_op jit(solution)/shard_map/ppermute | solution.py:312
  12.2 0.0 copy-start.14
  12.3 0.0 copy-done.12
  12.3 0.0 copy-done.13
  12.3 0.6 copy-done.14
  12.9 5.9 %spectra.1 = bf16[512,256]{1,0:T(8,128)(2,1)} custom-call(bf16[16,2048]{1,0:T(8,128)(2,1)} %get-tuple-element.7.refs_0_, bf16[16,2048]{1,0:T(8,128)(2,1)} %copy-done.13, bf16[16,2048]{1,0:T(8,128)(2,1)} %copy-done.14, bf16[16,2048]{1,0:T(8,128)(2,1)} %copy-done.12, bf16[4,256,64]{2,1,0:T(8,128)(2,1)} %constant.28.clone.refs_4_, ...), custom_call_target="tpu_custom_call" | custom-call | tf_op jit(solution)/shard_map/spectra/pallas_call | solution.py:340
  18.8 0.0 copy-start.15
  18.8 0.0 copy-start.16
  18.8 0.0 copy-start.4
  18.8 4.4 %all-to-all-start = ((bf16[32,16,256]{2,1,0:T(8,128)(2,1)}), bf16[32,16,256]{2,1,0:T(8,128)(2,1)S(1)}, u32[]{:S(2)}, u32[]{:S(2)}) async-start(bf16[32,16,256]{2,1,0:T(8,128)(2,1)} %bitcast.9), calls=%async_computation | async-start | bytes 524288 | tf_op jit(solution)/shard_map/all_to_all | solution.py:351
  23.2 0.0 copy-done.15
  23.2 0.0 copy-start.2
  23.2 0.0 copy-done.16
  23.3 0.0 copy-done.4
  23.3 0.0 copy-start.1
  23.3 2.5 %collective-permute-start.6 = (bf16[80,512]{1,0:T(8,128)(2,1)S(1)}, bf16[80,512]{1,0:T(8,128)(2,1)S(1)}, u32[]{:S(2)}, u32[]{:S(2)}) collective-permute-start(bf16[80,512]{1,0:T(8,128)(2,1)S(1)} %fusion.4.refs_0_), channel_id=1, source_target_pairs={{0,28},{4,24},{8,20},{12,16},{16,12},{20,8},{24,4},{28,0},{1,29},{... | collective-permute-start | bytes 245768 | tf_op jit(solution)/shard_map/ppermute | solution.py:312
  25.8 0.4 collective-permute-start.5
  26.2 1.4 %collective-permute-start.4 = (bf16[80,512]{1,0:T(8,128)(2,1)S(1)}, bf16[80,512]{1,0:T(8,128)(2,1)S(1)}, u32[]{:S(2)}, u32[]{:S(2)}) collective-permute-start(bf16[80,512]{1,0:T(8,128)(2,1)S(1)} %fusion.4.refs_0_), channel_id=1, source_target_pairs={{0,20},{4,16},{8,28},{12,24},{16,4},{20,0},{24,12},{28,8},{1,21},{... | collective-permute-start | bytes 245768 | tf_op jit(solution)/shard_map/ppermute | solution.py:312
  27.5 0.4 collective-permute-start.3
  27.9 1.4 %collective-permute-start.2 = (bf16[80,512]{1,0:T(8,128)(2,1)S(1)}, bf16[80,512]{1,0:T(8,128)(2,1)S(1)}, u32[]{:S(2)}, u32[]{:S(2)}) collective-permute-start(bf16[80,512]{1,0:T(8,128)(2,1)S(1)} %fusion.4.refs_0_), channel_id=1, source_target_pairs={{0,12},{4,8},{8,4},{12,0},{16,28},{20,24},{24,20},{28,16},{1,13},{... | collective-permute-start | bytes 245768 | tf_op jit(solution)/shard_map/ppermute | solution.py:312
  29.3 0.8 %collective-permute-done.6.refs_7_ = bf16[80,512]{1,0:T(8,128)(2,1)S(1)} collective-permute-done((bf16[80,512]{1,0:T(8,128)(2,1)S(1)}, bf16[80,512]{1,0:T(8,128)(2,1)S(1)}, u32[]{:S(2)}, u32[]{:S(2)}) %collective-permute-start.6) | collective-permute-done | bytes 81952 | tf_op jit(solution)/shard_map/ppermute | solution.py:312
  30.2 0.0 copy-start.5
  30.2 1.3 %collective-permute-start.1 = (bf16[80,512]{1,0:T(8,128)(2,1)S(1)}, bf16[80,512]{1,0:T(8,128)(2,1)S(1)}, u32[]{:S(2)}, u32[]{:S(2)}) collective-permute-start(bf16[80,512]{1,0:T(8,128)(2,1)S(1)} %fusion.4.refs_0_), channel_id=1, source_target_pairs={{0,8},{4,12},{8,0},{12,4},{16,24},{20,28},{24,16},{28,20},{1,9},{5... | collective-permute-start | bytes 245768 | tf_op jit(solution)/shard_map/ppermute | solution.py:312
  31.5 2.1 %collective-permute-done.5.refs_6_ = bf16[80,512]{1,0:T(8,128)(2,1)S(1)} collective-permute-done((bf16[80,512]{1,0:T(8,128)(2,1)S(1)}, bf16[80,512]{1,0:T(8,128)(2,1)S(1)}, u32[]{:S(2)}, u32[]{:S(2)}) %collective-permute-start.5) | collective-permute-done | bytes 81952 | tf_op jit(solution)/shard_map/ppermute | solution.py:312
  33.6 0.0 copy-start.6
  33.6 0.0 collective-permute-start
  33.6 0.0 copy-done.2
  33.6 0.0 copy-start.3
  33.6 0.8 %copy.12 = bf16[8,8,2,1024]{3,1,2,0:T(8,128)(2,1)} copy(bf16[8,8,2,1024]{3,2,1,0:T(2,128)(2,1)S(1)} %bitcast.10) | data formatting | bytes 524288
  34.4 0.0 copy-done.1
  34.4 0.0 copy-done.5
  34.4 0.0 copy-done.6
  34.4 0.3 copy-done.3
  34.7 0.8 %copy.13 = bf16[8,8,2,1024]{3,1,2,0:T(8,128)(2,1)} copy(bf16[8,8,2,1024]{3,2,1,0:T(2,128)(2,1)S(1)} %bitcast.11) | data formatting | bytes 524288
  35.4 0.0 collective-permute-done.4.refs_5_
  35.4 0.0 copy-start.7
  35.4 1.2 %collective-permute-done.3.refs_4_ = bf16[80,512]{1,0:T(8,128)(2,1)S(1)} collective-permute-done((bf16[80,512]{1,0:T(8,128)(2,1)S(1)}, bf16[80,512]{1,0:T(8,128)(2,1)S(1)}, u32[]{:S(2)}, u32[]{:S(2)}) %collective-permute-start.3) | collective-permute-done | bytes 81952 | tf_op jit(solution)/shard_map/ppermute | solution.py:312
  36.6 0.0 collective-permute-done.2.refs_3_
  36.6 0.0 copy-start.9
  36.6 0.0 collective-permute-done.1.refs_2_
  36.6 0.0 copy-start.10
  36.6 0.0 collective-permute-done.refs_1_
  36.7 0.0 copy-start.11
  36.7 0.0 all-to-all-done
  36.7 0.0 copy-start
  36.7 0.0 copy-done.7
  36.7 0.6 copy-done.8
  37.3 0.0 copy-done.9
  37.3 0.0 copy-done.10
  37.3 0.1 copy-done.11
  37.4 0.1 copy-done
  37.4 17.8 %adjoint.1 = f32[128,256]{1,0:T(8,128)} custom-call(bf16[80,512]{1,0:T(8,128)(2,1)} %copy-done.1, bf16[80,512]{1,0:T(8,128)(2,1)} %copy-done.11, bf16[80,512]{1,0:T(8,128)(2,1)} %copy-done.10, bf16[80,512]{1,0:T(8,128)(2,1)} %copy-done.9, bf16[80,512]{1,0:T(8,128)(2,1)} %copy-done.8, bf16[80,512]{1,0:T(8,128)(2,1)} %copy-done.7, bf16[80,512]{1,0:T(8,128)(2,1)} %copy-done.6, ...), custom_call_target="tpu_custom_call" | custom-call | tf_op jit(solution)/shard_map/adjoint/pallas_call | solution.py:355
  55.2 0.9 %reshape.22 = f32[32,4,256]{2,1,0:T(4,128)S(1)} reshape(f32[128,256]{1,0:T(8,128)} %adjoint.1) | data formatting | bytes 262144 | tf_op jit(solution)/shard_map/reshape | solution.py:374
  56.2 12.6 %all_to_all.10 = f32[32,4,256]{2,1,0:T(4,128)S(1)} all-to-all(f32[32,4,256]{2,1,0:T(4,128)S(1)} %reshape.22), channel_id=1, replica_groups=mesh['blk'=8,'src'=4] {'blk','src'}, dimensions={0} | all-to-all | bytes 262144 | tf_op jit(solution)/shard_map/all_to_all | solution.py:373
  68.7 0.7 reshape.23.parts_ref
  69.4 1.8 %image.1 = f32[4,512]{1,0:T(4,128)} custom-call(f32[8,8,128]{2,1,0:T(8,128)} %constant.32.clone.high_ref, f32[128,256]{1,0:T(8,128)} %reshape.23.parts_ref), custom_call_target="tpu_custom_call" | custom-call | tf_op jit(solution)/shard_map/image/pallas_call | solution.py:376
  (5 shorter events, 0.0 us)
Async XLA Ops:
  1.6 7.9 %collective-permute-start.9 = (bf16[16,2048]{1,0:T(8,128)(2,1)S(1)}, bf16[16,2048]{1,0:T(8,128)(2,1)S(1)}, u32[]{:S(2)}, u32[]{:S(2)}) collective-permute-start(bf16[16,2048]{1,0:T(8,128)(2,1)S(1)} %get-tuple-element.5), channel_id=1, source_target_pairs={{0,3},{1,2},{2,1},{3,0},{4,7},{5,6},{6,5},{7,4},{8,11},{9,10},{10,... | collective-permute-start | bytes 196616 | tf_op jit(solution)/shard_map/ppermute | solution.py:312
  6.6 4.7 %collective-permute-start.7 = (bf16[16,2048]{1,0:T(8,128)(2,1)S(1)}, bf16[16,2048]{1,0:T(8,128)(2,1)S(1)}, u32[]{:S(2)}, u32[]{:S(2)}) collective-permute-start(bf16[16,2048]{1,0:T(8,128)(2,1)S(1)} %get-tuple-element.6), channel_id=1, source_target_pairs={{0,1},{1,0},{2,3},{3,2},{4,5},{5,4},{6,7},{7,6},{8,9},{9,8},{10,11... | collective-permute-start | bytes 196616 | tf_op jit(solution)/shard_map/ppermute | solution.py:312
  6.6 5.6 %collective-permute-start.8 = (bf16[16,2048]{1,0:T(8,128)(2,1)S(1)}, bf16[16,2048]{1,0:T(8,128)(2,1)S(1)}, u32[]{:S(2)}, u32[]{:S(2)}) collective-permute-start(bf16[16,2048]{1,0:T(8,128)(2,1)S(1)} %get-tuple-element.8), channel_id=1, source_target_pairs={{0,2},{1,3},{2,0},{3,1},{4,6},{5,7},{6,4},{7,5},{8,10},{9,11},{10,... | collective-permute-start | bytes 196616 | tf_op jit(solution)/shard_map/ppermute | solution.py:312
  9.5 2.7 %copy-start.12 = (bf16[16,2048]{1,0:T(8,128)(2,1)}, bf16[16,2048]{1,0:T(8,128)(2,1)S(1)}, u32[]{:S(2)}) copy-start(bf16[16,2048]{1,0:T(8,128)(2,1)S(1)} %collective-permute-done.9.refs_3_) | copy-start | bytes 196612
  11.3 1.0 %copy-start.13 = (bf16[16,2048]{1,0:T(8,128)(2,1)}, bf16[16,2048]{1,0:T(8,128)(2,1)S(1)}, u32[]{:S(2)}) copy-start(bf16[16,2048]{1,0:T(8,128)(2,1)S(1)} %collective-permute-done.7.refs_1_) | copy-start | bytes 196612
  12.2 0.6 copy-start.14
  18.8 4.4 %copy-start.15 = (s32[4,64]{1,0:T(4,128)S(1)}, s32[4,64]{1,0:T(4,128)}, u32[]{:S(2)}) copy-start(s32[4,64]{1,0:T(4,128)} %param.15) | copy-start | bytes 3076
  18.8 4.5 %copy-start.16 = (s32[4,64]{1,0:T(4,128)S(1)}, s32[4,64]{1,0:T(4,128)}, u32[]{:S(2)}) copy-start(s32[4,64]{1,0:T(4,128)} %param.16) | copy-start | bytes 3076
  18.8 4.5 %copy-start.4 = (s32[64,512]{1,0:T(8,128)S(1)}, s32[64,512]{1,0:T(8,128)}, u32[]{:S(2)}) copy-start(s32[64,512]{1,0:T(8,128)} %param.13) | copy-start | bytes 393220
  18.8 17.9 %all-to-all-start = ((bf16[32,16,256]{2,1,0:T(8,128)(2,1)}), bf16[32,16,256]{2,1,0:T(8,128)(2,1)S(1)}, u32[]{:S(2)}, u32[]{:S(2)}) async-start(bf16[32,16,256]{2,1,0:T(8,128)(2,1)} %bitcast.9), calls=%async_computation | async-start | bytes 524288 | tf_op jit(solution)/shard_map/all_to_all | solution.py:351
  23.2 10.4 %copy-start.2 = (bf16[64,2,1024]{2,1,0:T(2,128)(2,1)S(1)}, bf16[64,2,1024]{2,1,0:T(2,128)(2,1)}, u32[]{:S(2)}) copy-start(bf16[64,2,1024]{2,1,0:T(2,128)(2,1)} %param.12) | copy-start | bytes 786436
  23.3 11.1 %copy-start.1 = (bf16[80,512]{1,0:T(8,128)(2,1)}, bf16[80,512]{1,0:T(8,128)(2,1)S(1)}, u32[]{:S(2)}) copy-start(bf16[80,512]{1,0:T(8,128)(2,1)S(1)} %fusion.4.refs_0_) | copy-start | bytes 245764
  23.3 6.8 %collective-permute-start.6 = (bf16[80,512]{1,0:T(8,128)(2,1)S(1)}, bf16[80,512]{1,0:T(8,128)(2,1)S(1)}, u32[]{:S(2)}, u32[]{:S(2)}) collective-permute-start(bf16[80,512]{1,0:T(8,128)(2,1)S(1)} %fusion.4.refs_0_), channel_id=1, source_target_pairs={{0,28},{4,24},{8,20},{12,16},{16,12},{20,8},{24,4},{28,0},{1,29},{... | collective-permute-start | bytes 245768 | tf_op jit(solution)/shard_map/ppermute | solution.py:312
  25.8 7.8 %collective-permute-start.5 = (bf16[80,512]{1,0:T(8,128)(2,1)S(1)}, bf16[80,512]{1,0:T(8,128)(2,1)S(1)}, u32[]{:S(2)}, u32[]{:S(2)}) collective-permute-start(bf16[80,512]{1,0:T(8,128)(2,1)S(1)} %fusion.4.refs_0_), channel_id=1, source_target_pairs={{0,24},{4,28},{8,16},{12,20},{16,8},{20,12},{24,0},{28,4},{1,25},{... | collective-permute-start | bytes 245768 | tf_op jit(solution)/shard_map/ppermute | solution.py:312
  26.2 9.3 %collective-permute-start.4 = (bf16[80,512]{1,0:T(8,128)(2,1)S(1)}, bf16[80,512]{1,0:T(8,128)(2,1)S(1)}, u32[]{:S(2)}, u32[]{:S(2)}) collective-permute-start(bf16[80,512]{1,0:T(8,128)(2,1)S(1)} %fusion.4.refs_0_), channel_id=1, source_target_pairs={{0,20},{4,16},{8,28},{12,24},{16,4},{20,0},{24,12},{28,8},{1,21},{... | collective-permute-start | bytes 245768 | tf_op jit(solution)/shard_map/ppermute | solution.py:312
  27.5 9.1 %collective-permute-start.3 = (bf16[80,512]{1,0:T(8,128)(2,1)S(1)}, bf16[80,512]{1,0:T(8,128)(2,1)S(1)}, u32[]{:S(2)}, u32[]{:S(2)}) collective-permute-start(bf16[80,512]{1,0:T(8,128)(2,1)S(1)} %fusion.4.refs_0_), channel_id=1, source_target_pairs={{0,16},{4,20},{8,24},{12,28},{16,0},{20,4},{24,8},{28,12},{1,17},{... | collective-permute-start | bytes 245768 | tf_op jit(solution)/shard_map/ppermute | solution.py:312
  27.9 8.7 %collective-permute-start.2 = (bf16[80,512]{1,0:T(8,128)(2,1)S(1)}, bf16[80,512]{1,0:T(8,128)(2,1)S(1)}, u32[]{:S(2)}, u32[]{:S(2)}) collective-permute-start(bf16[80,512]{1,0:T(8,128)(2,1)S(1)} %fusion.4.refs_0_), channel_id=1, source_target_pairs={{0,12},{4,8},{8,4},{12,0},{16,28},{20,24},{24,20},{28,16},{1,13},{... | collective-permute-start | bytes 245768 | tf_op jit(solution)/shard_map/ppermute | solution.py:312
  30.2 4.2 %copy-start.5 = (bf16[80,512]{1,0:T(8,128)(2,1)}, bf16[80,512]{1,0:T(8,128)(2,1)S(1)}, u32[]{:S(2)}) copy-start(bf16[80,512]{1,0:T(8,128)(2,1)S(1)} %collective-permute-done.6.refs_7_) | copy-start | bytes 245764
  30.2 6.5 %collective-permute-start.1 = (bf16[80,512]{1,0:T(8,128)(2,1)S(1)}, bf16[80,512]{1,0:T(8,128)(2,1)S(1)}, u32[]{:S(2)}, u32[]{:S(2)}) collective-permute-start(bf16[80,512]{1,0:T(8,128)(2,1)S(1)} %fusion.4.refs_0_), channel_id=1, source_target_pairs={{0,8},{4,12},{8,0},{12,4},{16,24},{20,28},{24,16},{28,20},{1,9},{5... | collective-permute-start | bytes 245768 | tf_op jit(solution)/shard_map/ppermute | solution.py:312
  33.6 0.8 %copy-start.6 = (bf16[80,512]{1,0:T(8,128)(2,1)}, bf16[80,512]{1,0:T(8,128)(2,1)S(1)}, u32[]{:S(2)}) copy-start(bf16[80,512]{1,0:T(8,128)(2,1)S(1)} %collective-permute-done.5.refs_6_) | copy-start | bytes 245764
  33.6 3.1 %collective-permute-start = (bf16[80,512]{1,0:T(8,128)(2,1)S(1)}, bf16[80,512]{1,0:T(8,128)(2,1)S(1)}, u32[]{:S(2)}, u32[]{:S(2)}) collective-permute-start(bf16[80,512]{1,0:T(8,128)(2,1)S(1)} %fusion.4.refs_0_), channel_id=1, source_target_pairs={{0,4},{4,0},{8,12},{12,8},{16,20},{20,16},{24,28},{28,24},{1,5},{5... | collective-permute-start | bytes 245768 | tf_op jit(solution)/shard_map/ppermute | solution.py:312
  33.6 1.1 %copy-start.3 = (bf16[64,2,1024]{2,1,0:T(2,128)(2,1)S(1)}, bf16[64,2,1024]{2,1,0:T(2,128)(2,1)}, u32[]{:S(2)}) copy-start(bf16[64,2,1024]{2,1,0:T(2,128)(2,1)} %param.14) | copy-start | bytes 786436
  35.4 1.3 %copy-start.7 = (bf16[80,512]{1,0:T(8,128)(2,1)}, bf16[80,512]{1,0:T(8,128)(2,1)S(1)}, u32[]{:S(2)}) copy-start(bf16[80,512]{1,0:T(8,128)(2,1)S(1)} %collective-permute-done.4.refs_5_) | copy-start | bytes 245764
  36.6 0.6 copy-start.8
  36.6 0.7 copy-start.9
  36.6 0.7 copy-start.10
  36.7 0.7 %copy-start.11 = (bf16[80,512]{1,0:T(8,128)(2,1)}, bf16[80,512]{1,0:T(8,128)(2,1)S(1)}, u32[]{:S(2)}) copy-start(bf16[80,512]{1,0:T(8,128)(2,1)S(1)} %collective-permute-done.refs_1_) | copy-start | bytes 245764
  36.7 0.8 %copy-start = (bf16[32,16,256]{2,1,0:T(8,128)(2,1)}, bf16[32,16,256]{2,1,0:T(8,128)(2,1)S(1)}, u32[]{:S(2)}) copy-start(bf16[32,16,256]{2,1,0:T(8,128)(2,1)S(1)} %all-to-all-done) | copy-start | bytes 786436

commit v2 on v1

--- a/solution.py
+++ b/solution.py
@@ -120,6 +120,7 @@
 NT_DIMS = (((1,), (1,)), ((), ()))
 TN_DIMS = (((0,), (0,)), ((), ()))
 VMEM_BYTES = 56 * 1024 * 1024
+PARTS_TYPE = jnp.bfloat16
 
 
 def split_bf16(values):
@@ -149,7 +150,8 @@
     third = np.concatenate(
         [np.concatenate([cos, sin], axis=1), np.concatenate([-sin, cos], axis=1)], axis=0
     )
-    return first, twiddle, (third / math.sqrt(NT)).astype(np.float32)
+    third = split_bf16((third / math.sqrt(NT)).astype(np.float32))
+    return first, twiddle, np.concatenate(third, axis=0)
 
 
 def mode_tables(n_src, n_blk, scale):
@@ -164,12 +166,18 @@
         low[1, parity, :, parity, 1] = cos
     low = low.reshape(4 * TILE_SIDE, 4 * TILE_SIDE) * scale
     devices = np.arange(n_src * n_blk)
-    block = devices % n_src * n_blk + devices // n_src
-    high_freqs = block[:, None] * 2 + np.arange(2)[None, :]
-    angle = 2 * np.pi / TILE_SIDE * ((side[:, None, None] * high_freqs[None]) % TILE_SIDE)
-    high = np.stack([np.cos(angle), -np.sin(angle)], axis=-1).reshape(
-        n_blk, TILE_SIDE // n_blk, 4 * n_src * n_blk
-    )
+    block = np.stack(
+        [devices % n_src * n_blk + ((devices // n_src) ^ other) for other in range(2)], axis=1
+    )
+    high_freqs = block[..., None] * 2 + np.arange(2)
+    angle = 2 * np.pi / TILE_SIDE * ((side[:, None, None, None] * high_freqs[None]) % TILE_SIDE)
+    part = np.stack([np.cos(angle), -np.sin(angle)], axis=-1).reshape(
+        n_blk, TILE_SIDE // n_blk, n_src * n_blk, 2, 4
+    )
+    high = np.zeros((n_blk, 2, TILE_SIDE // n_blk, n_src * n_blk, 2, 2, 4))
+    for half in range(2):
+        high[:, half, :, :, :, half] = part
+    high = high.reshape(n_blk, 2 * TILE_SIDE // n_blk, 16 * n_src * n_blk)
     return low.astype(np.float32), (high / math.sqrt(F)).astype(np.float32)
 
 
@@ -179,7 +187,7 @@
     stations, local = pieces[0].shape
     per_src = local // LANES
     steps = per_src * n_src
-    count = third_ref.shape[0] // 2
+    count = third_ref.shape[0] // 4
     first = first_ref[lax.axis_index("src")]
     for k in range(n_src):
         for a in range(per_src):
@@ -188,122 +196,172 @@
             ].astype(jnp.float32)
     twiddle_real, twiddle_imag = twiddle_ref[0], twiddle_ref[1]
     third = third_ref[...]
-    for station in range(stations):
-        rows = samples[station * steps : (station + 1) * steps, :].astype(jnp.bfloat16)
+    for station in range(0, stations, 2):
+        rows = jnp.concatenate(
+            [samples[(station + h) * steps : (station + h + 1) * steps, :] for h in range(2)], axis=1
+        ).astype(jnp.bfloat16)
         parts = jnp.dot(first, rows, preferred_element_type=jnp.float32)
-        real = parts[:steps] + parts[2 * steps : 3 * steps]
-        imag = parts[steps : 2 * steps] + parts[3 * steps :]
-        real = jnp.concatenate([real] * (LANES // steps), axis=0)
-        imag = jnp.concatenate([imag] * (LANES // steps), axis=0)
-        turned = jnp.concatenate(
-            [
-                real * twiddle_real - imag * twiddle_imag,
-                real * twiddle_imag + imag * twiddle_real,
-            ],
-            axis=1,
+        reals_here = parts[:steps] + parts[2 * steps : 3 * steps]
+        imags_here = parts[steps : 2 * steps] + parts[3 * steps :]
+        turned = []
+        for h in range(2):
+            at = slice(h * LANES, (h + 1) * LANES)
+            real = jnp.concatenate([reals_here[:, at]] * (LANES // steps), axis=0)
+            imag = jnp.concatenate([imags_here[:, at]] * (LANES // steps), axis=0)
+            turned.append(
+                jnp.concatenate(
+                    [
+                        real * twiddle_real - imag * twiddle_imag,
+                        real * twiddle_imag + imag * twiddle_real,
+                    ],
+                    axis=1,
+                )
+            )
+        turned = jnp.concatenate(turned, axis=0)
+        high = turned.astype(jnp.bfloat16)
+        low = (turned - high.astype(jnp.float32)).astype(jnp.bfloat16)
+        result = lax.dot_general(third, high, NT_DIMS, preferred_element_type=jnp.float32)
+        result = (
+            result[: 2 * count]
+            + result[2 * count :]
+            + lax.dot_general(
+                third[: 2 * count], low, NT_DIMS, preferred_element_type=jnp.float32
+            )
         )
-        result = lax.dot_general(
-            third, turned, NT_DIMS, precision=HIGHEST, preferred_element_type=jnp.float32
-        )
-        reals[pl.ds(station, count, stride=stations), :] = result[:count]
-        imags[pl.ds(station, count, stride=stations), :] = result[count:]
+        for h in range(2):
+            at = slice(h * LANES, (h + 1) * LANES)
+            reals[pl.ds(station + h, count, stride=stations), :] = result[:count, at]
+            imags[pl.ds(station + h, count, stride=stations), :] = result[count:, at]
     out_ref[:, :LANES] = reals[...].astype(jnp.bfloat16)
     out_ref[:, LANES:] = imags[...].astype(jnp.bfloat16)
 
 
-def adjoint_kernel(n_blk, n_src, slots, tiles, chunk, *refs):
-    packs = refs[:n_blk]
-    spectra_ref, observed_ref, green_ref, low_ref, out_ref, classes, picks, mixed, total = refs[
-        n_blk:
-    ]
+def adjoint_kernel(panels, slots, n_src, chunk, *refs):
+    packs = refs[:panels]
+    observed_ref, green_ref, spectra_ref, other_ref, low_ref, out_ref = refs[panels : panels + 6]
+    spectra, classes, numbers, bank, green, mixed, total = refs[panels + 6 :]
     stations = spectra_ref.shape[0]
-    panel = stations // n_blk
-    class_count = observed_ref.shape[0]
-    green_count = green_ref.shape[0]
-    local_freqs = observed_ref.shape[1] // 2
+    panel = classes.shape[0] // panels
+    class_count = bank.shape[0]
+    tiles = total.shape[0]
     blk_index = lax.axis_index("blk")
-    for k in range(n_blk):
-        owner = blk_index ^ k
-        at = pl.ds(pl.multiple_of(owner * panel, panel), panel)
-        classes[at, :] = packs[k][:panel].astype(jnp.int32)
-        picks[owner] = packs[k][panel : panel + 16, :LANES].astype(jnp.int32)
-    here = pl.ds(pl.multiple_of(blk_index * LANES, LANES), LANES)
-    there = pl.ds(pl.multiple_of(local_freqs + blk_index * LANES, LANES), LANES)
-    obs_real = observed_ref[:, here].astype(jnp.float32)[None]
-    obs_imag = observed_ref[:, there].astype(jnp.float32)[None]
-    green = jnp.concatenate([green_ref[:, here], green_ref[:, there]], axis=1)
-    spectra = spectra_ref[...]
-    widened = spectra.astype(jnp.float32)
-    power = jnp.sum(widened * widened, axis=0, keepdims=True)
-    power = power[:, :LANES] + power[:, LANES:]
-    power = jnp.concatenate([power, power], axis=1)
+    for other in range(2):
+        at = pl.ds(pl.multiple_of((blk_index ^ other) * LANES, LANES), LANES)
+        lanes = slice(2 * other * LANES, 2 * (other + 1) * LANES)
+        pair = observed_ref[:, :, at].astype(jnp.float32)
+        bank[:, lanes] = jnp.concatenate([pair[:, 0, :], pair[:, 1, :]], axis=1)
+        pair = green_ref[:, :, at].astype(jnp.float32)
+        pair = jnp.concatenate([pair[:, 0, :], pair[:, 1, :]], axis=1)
+        green[:, lanes] = pair.astype(jnp.bfloat16)
+    for k, pack in enumerate(packs):
+        classes[k * panel : (k + 1) * panel, :] = pack[:panel].astype(jnp.int32)
+        ids = pack[panel : panel + 16, :LANES].astype(jnp.int32)
+        for row in range(2):
+            numbers[k, row : row + 1] = jnp.concatenate(
+                [ids[8 * row + slot : 8 * row + slot + 1, :panel] for slot in range(slots)], axis=1
+            )
+    spectra[:, : 2 * LANES] = spectra_ref[...]
+    spectra[:, 2 * LANES :] = other_ref[...]
+    widened = spectra[...].astype(jnp.float32)
+    squares = jnp.sum(widened * widened, axis=0, keepdims=True)
+    lanes = [slice(part * LANES, (part + 1) * LANES) for part in range(4)]
+    power = []
+    for real, imag in (lanes[:2], lanes[2:]):
+        power += [squares[:, real] + squares[:, imag]] * 2
+    power = jnp.concatenate(power, axis=1)
+    green_ids = lax.broadcasted_iota(jnp.int32, (green.shape[0], slots * panel), 0)
+    tile_ids = lax.broadcasted_iota(jnp.int32, (tiles, slots * panel), 0)
     class_ids = lax.broadcasted_iota(jnp.int32, (1, class_count, stations), 1)
     total[...] = jnp.zeros_like(total)
 
-    def one_panel(owner, carry):
-        start = pl.multiple_of(owner * panel, panel)
+    def mix(place):
+        start = pl.multiple_of(place * panel, panel)
         for part in range(panel // chunk):
-            rows = classes[pl.ds(start + part * chunk, chunk), :]
-            hot = jnp.where(rows[:, None, :] == class_ids, 1.0, 0.0).astype(jnp.bfloat16)
+            at = pl.ds(start + part * chunk, chunk)
+            hot = jnp.where(classes[at, :][:, None, :] == class_ids, 1.0, 0.0)
             grouped = jnp.dot(
-                hot.reshape(chunk * class_count, stations),
-                spectra,
+                hot.astype(jnp.bfloat16).reshape(chunk * class_count, stations),
+                spectra[...],
                 preferred_element_type=jnp.float32,
-            ).reshape(chunk, class_count, 2 * LANES)
-            group_real, group_imag = grouped[..., :LANES], grouped[..., LANES:]
-            at = pl.ds(part * chunk, chunk)
-            mixed[at, :LANES] = jnp.sum(obs_real * group_real - obs_imag * group_imag, axis=1)
-            mixed[at, LANES:] = jnp.sum(obs_real * group_imag + obs_imag * group_real, axis=1)
-        own = spectra_ref[pl.ds(start, panel), :].astype(jnp.float32)
-        adjoint = (own * power - mixed[...]) * (1.0 / stations)
-        adj_real, adj_imag = adjoint[:, :LANES], adjoint[:, LANES:]
-        ids = picks[owner]
-        green_ids = lax.broadcasted_iota(jnp.int32, (green_count, panel), 0)
-        tile_ids = lax.broadcasted_iota(jnp.int32, (tiles, panel), 0)
+            ).reshape(chunk, class_count, 4 * LANES)
+            for real, imag in (lanes[:2], lanes[2:]):
+                obs_real, obs_imag = bank[:, real][None], bank[:, imag][None]
+                group_real, group_imag = grouped[..., real], grouped[..., imag]
+                mixed[at, real] = jnp.sum(obs_real * group_real - obs_imag * group_imag, axis=1)
+                mixed[at, imag] = jnp.sum(obs_real * group_imag + obs_imag * group_real, axis=1)
+
+    def gather(place):
+        at = pl.ds(pl.multiple_of(place * panel, panel), panel)
+        owner = blk_index ^ (2 * place)
+        own = spectra[pl.ds(pl.multiple_of(owner * panel, panel), panel), :].astype(jnp.float32)
+        adjoint = (own * power - mixed[at, :]) * (1.0 / stations)
+        ids = numbers[place]
+        pick = jnp.where(ids[:1] == green_ids, 1.0, 0.0).astype(jnp.bfloat16)
+        tile = jnp.where(ids[1:2] == tile_ids, 1.0, 0.0).astype(jnp.bfloat16)
+        all_picked = lax.dot_general(
+            pick, green[...], TN_DIMS, preferred_element_type=jnp.float32
+        )
+        weighted = []
         for slot in range(slots):
-            pick = jnp.where(ids[slot : slot + 1, :panel] == green_ids, 1.0, 0.0)
-            tile = jnp.where(ids[8 + slot : 9 + slot, :panel] == tile_ids, 1.0, 0.0)
-            picked = lax.dot_general(
-                pick.astype(jnp.bfloat16), green, TN_DIMS, preferred_element_type=jnp.float32
-            )
-            pick_real, pick_imag = picked[:, :LANES], picked[:, LANES:]
-            weighted = jnp.concatenate(
-                [
-                    adj_real * pick_real + adj_imag * pick_imag,
-                    adj_real * pick_imag - adj_imag * pick_real,
-                ],
-                axis=1,
-            ).astype(jnp.bfloat16)
-            total[...] += jnp.dot(
-                tile.astype(jnp.bfloat16), weighted, preferred_element_type=jnp.float32
-            )
+            picked = all_picked[slot * panel : (slot + 1) * panel]
+            row = []
+            for real, imag in (lanes[:2], lanes[2:]):
+                row.append(adjoint[:, real] * picked[:, real] + adjoint[:, imag] * picked[:, imag])
+                row.append(adjoint[:, real] * picked[:, imag] - adjoint[:, imag] * picked[:, real])
+            weighted.append(jnp.concatenate(row, axis=1).astype(jnp.bfloat16))
+        total[...] += jnp.dot(
+            tile,
+            jnp.concatenate(weighted, axis=0),
+            preferred_element_type=jnp.float32,
+        )
+
+    mix(0)
+
+    def one_panel(place, carry):
+        gather(place - 1)
+        mix(place)
         return carry
 
-    lax.fori_loop(0, n_blk, one_panel, 0)
-    low = jnp.dot(
-        total[...], low_ref[...], precision=HIGHEST, preferred_element_type=jnp.float32
-    )
-    share = tiles // n_src
+    lax.fori_loop(1, panels, one_panel, 0)
+    gather(panels - 1)
+    low = [
+        jnp.dot(
+            total[:, at], low_ref[...], precision=HIGHEST, preferred_element_type=jnp.float32
+        )
+        for at in (slice(0, 2 * LANES), slice(2 * LANES, 4 * LANES))
+    ]
     rows = []
     for owner in range(n_src):
-        for part in range(4):
-            piece = low[owner * share : (owner + 1) * share, part * TILE_SIDE : (part + 1) * TILE_SIDE]
-            rows.append(jnp.concatenate([piece[t : t + 1] for t in range(share)], axis=1))
-    rows = jnp.concatenate(rows, axis=0)
-    for copy in range(n_blk):
-        out_ref[copy * 4 * n_src : (copy + 1) * 4 * n_src, :] = rows
+        for other in range(2):
+            for half in range(2):
+                at = owner * (tiles // n_src) + 2 * half
+                for part in range(4):
+                    side = slice(part * TILE_SIDE, (part + 1) * TILE_SIDE)
+                    rows.append(
+                        jnp.concatenate(
+                            [low[other][at : at + 1, side], low[other][at + 1 : at + 2, side]], axis=1
+                        )
+                    )
+    rows = jnp.concatenate(rows, axis=0).astype(out_ref.dtype)
+    for copy in range(out_ref.shape[0] // rows.shape[0]):
+        out_ref[copy * 16 * n_src : (copy + 1) * 16 * n_src, :] = rows
 
 
 def image_kernel(high_ref, parts_ref, out_ref):
     high = high_ref[lax.axis_index("blk")]
     image = jnp.dot(
-        high, parts_ref[...], precision=HIGHEST, preferred_element_type=jnp.float32
-    )
-    rows = high.shape[0]
+        high,
+        parts_ref[...].astype(jnp.float32),
+        precision=HIGHEST,
+        preferred_element_type=jnp.float32,
+    )
+    rows = high.shape[0] // 2
     for tile in range(out_ref.shape[0]):
+        half, side = tile // 2, tile % 2
         for row in range(rows):
+            at = half * rows + row
             out_ref[tile : tile + 1, row * TILE_SIDE : (row + 1) * TILE_SIDE] = image[
-                row : row + 1, tile * TILE_SIDE : (tile + 1) * TILE_SIDE
+                at : at + 1, side * TILE_SIDE : (side + 1) * TILE_SIDE
             ]
 
 
@@ -331,7 +389,7 @@
     pack = jnp.concatenate([pair_class, widen(green_index), widen(tile_index)], axis=0).astype(
         jnp.bfloat16
     )
-    packs = [pack] + [swap(pack, "blk", k) for k in range(1, n_blk)]
+    packs = [pack] + [swap(pack, "blk", k) for k in range(2, n_blk, 2)]
 
     first, twiddle, third = forward_tables(n_src, n_blk)
     low, high = mode_tables(n_src, n_blk, math.sqrt(tiles / (stations * slots)))
@@ -352,27 +410,26 @@
         blocks.reshape(devices, share, 2 * LANES), BOTH, 0, 0, tiled=True
     ).reshape(stations, 2 * LANES)
     class_count = observed.shape[0]
+    panels = n_blk // 2
+    spectra, packs = lax.optimization_barrier((spectra, packs))
     parts = pl.pallas_call(
-        functools.partial(adjoint_kernel, n_blk, n_src, slots, tiles, 8),
-        out_shape=jax.ShapeDtypeStruct((4 * devices, TILE_DEV * TILE_SIDE), jnp.float32),
+        functools.partial(adjoint_kernel, panels, slots, n_src, 8),
+        out_shape=jax.ShapeDtypeStruct((16 * devices, 2 * TILE_SIDE), PARTS_TYPE),
         scratch_shapes=[
-            pltpu.VMEM((stations, stations), jnp.int32),
-            pltpu.VMEM((n_blk, 16, LANES), jnp.int32),
-            pltpu.VMEM((panel, 2 * LANES), jnp.float32),
-            pltpu.VMEM((tiles, 2 * LANES), jnp.float32),
+            pltpu.VMEM((stations, 4 * LANES), jnp.bfloat16),
+            pltpu.VMEM((panels * panel, stations), jnp.int32),
+            pltpu.VMEM((panels, 8, slots * panel), jnp.int32),
+            pltpu.VMEM((class_count, 4 * LANES), jnp.float32),
+            pltpu.VMEM((green.shape[0], 4 * LANES), jnp.bfloat16),
+            pltpu.VMEM((panels * panel, 4 * LANES), jnp.float32),
+            pltpu.VMEM((tiles, 4 * LANES), jnp.float32),
         ],
         compiler_params=params,
         name="adjoint",
-    )(
-        *packs,
-        spectra,
-        observed.reshape(class_count, -1),
-        green.reshape(green.shape[0], -1),
-        low,
-    )
+    )(*packs, observed, green, spectra, swap(spectra, "blk", 1), low)
     parts = lax.all_to_all(
-        parts.reshape(devices, 4, TILE_DEV * TILE_SIDE), BOTH, 0, 0, tiled=True
-    ).reshape(4 * devices, TILE_DEV * TILE_SIDE)
+        parts.reshape(devices, 16, 2 * TILE_SIDE), BOTH, 0, 0, tiled=True
+    ).reshape(16 * devices, 2 * TILE_SIDE)
     return pl.pallas_call(
         image_kernel,
         out_shape=jax.ShapeDtypeStruct((TILE_DEV, TP // n_blk), jnp.float32),

time: 71.6 us -> 65.4 us (0.913)
  starting transfers between devices: 17.4 us -> 14 us
  waiting for transfers between devices: 9.2 us -> 12.1 us
  local copies, waits for them, and re-layouts: 6.4 us -> 3.55 us
  Pallas kernels: 25.5 us -> 22.8 us
    ppermute x10 -> x7, starting transfers between devices: 13 us -> 9.57 us  [swap(): return lax.ppermute(values, axis, [(i, i ^ distance) for i in range(size)])]
    ppermute x10 -> x7, waiting for transfers between devices: 9.2 us -> 11.8 us  [swap(): return lax.ppermute(values, axis, [(i, i ^ distance) for i in range(size)])]
    pallas_call x1, Pallas kernels: 5.9 us -> 3.86 us  [split_body(): pl.pallas_call(functools.partial(spectra_kernel, n_src), out_shape=jax.Sh...]
    reshape x2 -> x0, local copies, waits for them, and re-layouts: 1.64 us -> none  [the longest x1 0.94 us: split_body(): parts.reshape(devices, 4, TILE_DEV * TILE_SIDE)]
    unnamed x36 -> x24, local copies, waits for them, and re-layouts: 3.21 us -> 1.99 us
    pallas_call x1, Pallas kernels: 17.8 us -> 17 us  [split_body(): pl.pallas_call(functools.partial(adjoint_kernel, panels, slots, n_src, 8)...]
  transfers between devices with their start and end apart: 11 -> 8, of which waited for: 6 -> 7; matrix products, arithmetic and copies ran while one was open for 2% -> 0% of each run, Pallas kernels for 0% -> 0%
where the time goes in v2:
time: 65.4 us; the launch traced here: 65 us
  Pallas kernels  22.8 us (35%)
  starting transfers between devices  14 us (21%)
  blocking collectives  12.5 us (19%)
  waiting for transfers between devices  12.1 us (19%)
  local copies, waits for them, and re-layouts  3.55 us (5%)
    pallas_call x1, Pallas kernels, split_body(): pl.pallas_call(functools.partial(adjoint_kernel, panels, slots, n_src, 8)...  17 us
    all_to_all x1, blocking collectives, split_body(): lax.all_to_all(parts.reshape(devices, 16, 2 * TILE_SIDE), BOTH, 0, 0, til...  12.5 us
    ppermute x7, waiting for transfers between devices, swap(): return lax.ppermute(values, axis, [(i, i ^ distance) for i in range(size)])  11.8 us
    ppermute x7, starting transfers between devices, swap(): return lax.ppermute(values, axis, [(i, i ^ distance) for i in range(size)])  9.57 us
    all_to_all x1, starting transfers between devices, split_body(): lax.all_to_all(blocks.reshape(devices, share, 2 * LANES), BOTH, 0, 0, til...  4.41 us
    pallas_call x1, Pallas kernels, split_body(): pl.pallas_call(functools.partial(spectra_kernel, n_src), out_shape=jax.Sh...  3.86 us
    unnamed x24, local copies, waits for them, and re-layouts  1.99 us
    pallas_call x1, Pallas kernels, split_body(): pl.pallas_call(image_kernel, out_shape=jax.ShapeDtypeStruct((TILE_DEV, TP...  1.89 us
  transfers between devices with their start and end apart: 8, of which 7 were waited for; matrix products, arithmetic and copies ran while one was open for 0% of the time, Pallas kernels for 0%

profile of v2, /device:TPU:0, one launch (start us, length us, event | category | flops | bytes accessed | tf_op | source)
XLA Modules:
  0.0 65.0 jit_solution(11973567458107962557)
XLA Ops:
  0.0 1.6 %constant_dynamic-slice_fusion = (bf16[16,2048]{1,0:T(8,128)(2,1)S(1)}, bf16[16,2048]{1,0:T(8,128)(2,1)S(1)}, bf16[16,2048]{1,0:T(8,128)(2,1)}, bf16[16,2048]{1,0:T(8,128)(2,1)S(1)}) fusion(bf16[64,2048]{1,0:T(8,128)(2,1)} %param.11, s32[]{:T(128)S(6)} %select_n.15, s32[]{:T(128)S(6)} %select_n.13, s32[]{:T(128)S(6)} %select_n.12, s32[]{:T(128)S(6)} %select_n.14), kind=kLoop, calls=%fused_computation.8 | loop fusion | bytes 524304 | tf_op jit(solution)/shard_map/dynamic_slice | solution.py:382
  1.6 5.0 %collective-permute-start.2 = (bf16[16,2048]{1,0:T(8,128)(2,1)S(1)}, bf16[16,2048]{1,0:T(8,128)(2,1)S(1)}, u32[]{:S(2)}, u32[]{:S(2)}) collective-permute-start(bf16[16,2048]{1,0:T(8,128)(2,1)S(1)} %get-tuple-element.15), channel_id=1, source_target_pairs={{0,3},{1,2},{2,1},{3,0},{4,7},{5,6},{6,5},{7,4},{8,11},{9,10},{10,... | collective-permute-start | bytes 196616 | tf_op jit(solution)/shard_map/ppermute | solution.py:370
  6.6 0.0 collective-permute-start
  6.6 0.6 collective-permute-start.1
  7.2 2.3 %collective-permute-done.2.refs_3_ = bf16[16,2048]{1,0:T(8,128)(2,1)S(1)} collective-permute-done((bf16[16,2048]{1,0:T(8,128)(2,1)S(1)}, bf16[16,2048]{1,0:T(8,128)(2,1)S(1)}, u32[]{:S(2)}, u32[]{:S(2)}) %collective-permute-start.2) | collective-permute-done | bytes 65568 | tf_op jit(solution)/shard_map/ppermute | solution.py:370
  9.5 0.0 copy-start.7
  9.5 1.8 %collective-permute-done.refs_1_ = bf16[16,2048]{1,0:T(8,128)(2,1)S(1)} collective-permute-done((bf16[16,2048]{1,0:T(8,128)(2,1)S(1)}, bf16[16,2048]{1,0:T(8,128)(2,1)S(1)}, u32[]{:S(2)}, u32[]{:S(2)}) %collective-permute-start) | collective-permute-done | bytes 65568 | tf_op jit(solution)/shard_map/ppermute | solution.py:370
  11.3 0.0 copy-start.8
  11.3 1.0 %collective-permute-done.1.refs_2_ = bf16[16,2048]{1,0:T(8,128)(2,1)S(1)} collective-permute-done((bf16[16,2048]{1,0:T(8,128)(2,1)S(1)}, bf16[16,2048]{1,0:T(8,128)(2,1)S(1)}, u32[]{:S(2)}, u32[]{:S(2)}) %collective-permute-start.1) | collective-permute-done | bytes 65568 | tf_op jit(solution)/shard_map/ppermute | solution.py:370
  12.3 0.0 copy-start.9
  12.3 0.0 copy-done.7
  12.3 0.0 copy-done.8
  12.3 0.6 copy-done.9
  12.9 3.9 %spectra.1 = bf16[512,256]{1,0:T(8,128)(2,1)} custom-call(bf16[16,2048]{1,0:T(8,128)(2,1)} %get-tuple-element.17.refs_0_, bf16[16,2048]{1,0:T(8,128)(2,1)} %copy-done.8, bf16[16,2048]{1,0:T(8,128)(2,1)} %copy-done.9, bf16[16,2048]{1,0:T(8,128)(2,1)} %copy-done.7, bf16[4,256,64]{2,1,0:T(8,128)(2,1)} %constant.28.clone.refs_4_, ...), custom_call_target="tpu_custom_call" | custom-call | tf_op jit(solution)/shard_map/spectra/pallas_call | solution.py:398
  16.7 0.0 copy-start.10
  16.7 0.0 copy-start.3
  16.7 4.4 %all-to-all-start = ((bf16[32,16,256]{2,1,0:T(8,128)(2,1)}), bf16[32,16,256]{2,1,0:T(8,128)(2,1)S(1)}, u32[]{:S(2)}, u32[]{:S(2)}) async-start(bf16[32,16,256]{2,1,0:T(8,128)(2,1)} %bitcast.6), calls=%async_computation | async-start | bytes 524288 | tf_op jit(solution)/shard_map/all_to_all | solution.py:409
  21.1 0.0 copy-done.10
  21.2 0.0 copy-start.11
  21.2 0.7 %copy-done.11 = s32[4,64]{1,0:T(4,128)S(1)} copy-done((s32[4,64]{1,0:T(4,128)S(1)}, s32[4,64]{1,0:T(4,128)}, u32[]{:S(2)}) %copy-start.11) | copy-done | bytes 1048
  21.8 0.0 copy-done.3
  21.9 0.0 copy-start.1
  21.9 2.7 %collective-permute-start.5 = (bf16[80,512]{1,0:T(8,128)(2,1)S(1)}, bf16[80,512]{1,0:T(8,128)(2,1)S(1)}, u32[]{:S(2)}, u32[]{:S(2)}) collective-permute-start(bf16[80,512]{1,0:T(8,128)(2,1)S(1)} %fusion.4.refs_0_), channel_id=1, source_target_pairs={{0,24},{4,28},{8,16},{12,20},{16,8},{20,12},{24,0},{28,4},{1,25},{... | collective-permute-start | bytes 245768 | tf_op jit(solution)/shard_map/ppermute | solution.py:370
  24.6 0.6 collective-permute-start.4
  25.2 0.3 collective-permute-start.3
  25.4 3.7 %collective-permute-done.5.refs_3_ = bf16[80,512]{1,0:T(8,128)(2,1)S(1)} collective-permute-done((bf16[80,512]{1,0:T(8,128)(2,1)S(1)}, bf16[80,512]{1,0:T(8,128)(2,1)S(1)}, u32[]{:S(2)}, u32[]{:S(2)}) %collective-permute-start.5) | collective-permute-done | bytes 81952 | tf_op jit(solution)/shard_map/ppermute | solution.py:370
  29.1 0.0 copy-start.4
  29.1 1.9 %collective-permute-done.4.refs_2_ = bf16[80,512]{1,0:T(8,128)(2,1)S(1)} collective-permute-done((bf16[80,512]{1,0:T(8,128)(2,1)S(1)}, bf16[80,512]{1,0:T(8,128)(2,1)S(1)}, u32[]{:S(2)}, u32[]{:S(2)}) %collective-permute-start.4) | collective-permute-done | bytes 81952 | tf_op jit(solution)/shard_map/ppermute | solution.py:370
  31.0 0.0 copy-start.5
  31.0 0.0 collective-permute-done.3.refs_1_
  31.0 0.0 copy-start.6
  31.0 0.4 all-to-all-done
  31.3 0.0 copy-start
  31.3 0.4 collective-permute-start.6
  31.7 1.2 %collective-permute-done.6.refs_7_ = bf16[512,256]{1,0:T(8,128)(2,1)S(1)} collective-permute-done((bf16[512,256]{1,0:T(8,128)(2,1)S(1)}, bf16[512,256]{1,0:T(8,128)(2,1)S(1)}, u32[]{:S(2)}, u32[]{:S(2)}) %collective-permute-start.6) | collective-permute-done | bytes 262176 | tf_op jit(solution)/shard_map/ppermute | solution.py:370
  32.9 0.0 copy-done.1
  32.9 0.0 copy-done.4
  32.9 0.0 copy-done.5
  32.9 0.0 copy-done.6
  32.9 0.0 copy-done
  32.9 0.0 copy-start.2
  32.9 0.7 %copy-done.2 = bf16[512,256]{1,0:T(8,128)(2,1)} copy-done((bf16[512,256]{1,0:T(8,128)(2,1)}, bf16[512,256]{1,0:T(8,128)(2,1)S(1)}, u32[]{:S(2)}) %copy-start.2) | copy-done | bytes 262168
  33.6 17.0 %adjoint.1 = bf16[512,128]{1,0:T(8,128)(2,1)} custom-call(bf16[80,512]{1,0:T(8,128)(2,1)} %copy-done.1, bf16[80,512]{1,0:T(8,128)(2,1)} %copy-done.6, bf16[80,512]{1,0:T(8,128)(2,1)} %copy-done.5, bf16[80,512]{1,0:T(8,128)(2,1)} %copy-done.4, bf16[64,2,1024]{2,1,0:T(2,128)(2,1)} %refs_4_.2, bf16[64,2,1024]{2,1,0:T(2,128)(2,1)} %refs_5_.2, ...), custom_call_target="tpu_custom_call" | custom-call | tf_op jit(solution)/shard_map/adjoint/pallas_call | solution.py:415
  50.6 12.5 %all_to_all.10 = bf16[32,16,128]{2,1,0:T(8,128)(2,1)} all-to-all(bf16[32,16,128]{2,1,0:T(8,128)(2,1)} %bitcast.7), channel_id=1, replica_groups=mesh['blk'=8,'src'=4] {'blk','src'}, dimensions={0} | all-to-all | bytes 262144 | tf_op jit(solution)/shard_map/all_to_all | solution.py:430
  63.1 1.9 %image.1 = f32[4,512]{1,0:T(4,128)} custom-call(f32[8,16,512]{2,1,0:T(8,128)} %constant.32.clone.high_ref, bf16[512,128]{1,0:T(8,128)(2,1)} %bitcast.8), custom_call_target="tpu_custom_call" | custom-call | tf_op jit(solution)/shard_map/image/pallas_call | solution.py:433
  (4 shorter events, 0.0 us)
Async XLA Ops:
  1.6 7.9 %collective-permute-start.2 = (bf16[16,2048]{1,0:T(8,128)(2,1)S(1)}, bf16[16,2048]{1,0:T(8,128)(2,1)S(1)}, u32[]{:S(2)}, u32[]{:S(2)}) collective-permute-start(bf16[16,2048]{1,0:T(8,128)(2,1)S(1)} %get-tuple-element.15), channel_id=1, source_target_pairs={{0,3},{1,2},{2,1},{3,0},{4,7},{5,6},{6,5},{7,4},{8,11},{9,10},{10,... | collective-permute-start | bytes 196616 | tf_op jit(solution)/shard_map/ppermute | solution.py:370
  6.6 4.7 %collective-permute-start = (bf16[16,2048]{1,0:T(8,128)(2,1)S(1)}, bf16[16,2048]{1,0:T(8,128)(2,1)S(1)}, u32[]{:S(2)}, u32[]{:S(2)}) collective-permute-start(bf16[16,2048]{1,0:T(8,128)(2,1)S(1)} %get-tuple-element.16), channel_id=1, source_target_pairs={{0,1},{1,0},{2,3},{3,2},{4,5},{5,4},{6,7},{7,6},{8,9},{9,8},{10,11... | collective-permute-start | bytes 196616 | tf_op jit(solution)/shard_map/ppermute | solution.py:370
  6.6 5.6 %collective-permute-start.1 = (bf16[16,2048]{1,0:T(8,128)(2,1)S(1)}, bf16[16,2048]{1,0:T(8,128)(2,1)S(1)}, u32[]{:S(2)}, u32[]{:S(2)}) collective-permute-start(bf16[16,2048]{1,0:T(8,128)(2,1)S(1)} %get-tuple-element.18), channel_id=1, source_target_pairs={{0,2},{1,3},{2,0},{3,1},{4,6},{5,7},{6,4},{7,5},{8,10},{9,11},{10,... | collective-permute-start | bytes 196616 | tf_op jit(solution)/shard_map/ppermute | solution.py:370
  9.5 2.7 %copy-start.7 = (bf16[16,2048]{1,0:T(8,128)(2,1)}, bf16[16,2048]{1,0:T(8,128)(2,1)S(1)}, u32[]{:S(2)}) copy-start(bf16[16,2048]{1,0:T(8,128)(2,1)S(1)} %collective-permute-done.2.refs_3_) | copy-start | bytes 196612
  11.3 1.0 %copy-start.8 = (bf16[16,2048]{1,0:T(8,128)(2,1)}, bf16[16,2048]{1,0:T(8,128)(2,1)S(1)}, u32[]{:S(2)}) copy-start(bf16[16,2048]{1,0:T(8,128)(2,1)S(1)} %collective-permute-done.refs_1_) | copy-start | bytes 196612
  12.3 0.6 copy-start.9
  16.7 4.4 %copy-start.10 = (s32[4,64]{1,0:T(4,128)S(1)}, s32[4,64]{1,0:T(4,128)}, u32[]{:S(2)}) copy-start(s32[4,64]{1,0:T(4,128)} %param.15) | copy-start | bytes 3076
  16.7 5.1 %copy-start.3 = (s32[64,512]{1,0:T(8,128)S(1)}, s32[64,512]{1,0:T(8,128)}, u32[]{:S(2)}) copy-start(s32[64,512]{1,0:T(8,128)} %param.13) | copy-start | bytes 393220
  16.7 14.6 %all-to-all-start = ((bf16[32,16,256]{2,1,0:T(8,128)(2,1)}), bf16[32,16,256]{2,1,0:T(8,128)(2,1)S(1)}, u32[]{:S(2)}, u32[]{:S(2)}) async-start(bf16[32,16,256]{2,1,0:T(8,128)(2,1)} %bitcast.6), calls=%async_computation | async-start | bytes 524288 | tf_op jit(solution)/shard_map/all_to_all | solution.py:409
  21.2 0.7 %copy-start.11 = (s32[4,64]{1,0:T(4,128)S(1)}, s32[4,64]{1,0:T(4,128)}, u32[]{:S(2)}) copy-start(s32[4,64]{1,0:T(4,128)} %param.16) | copy-start | bytes 3076
  21.9 11.0 %copy-start.1 = (bf16[80,512]{1,0:T(8,128)(2,1)}, bf16[80,512]{1,0:T(8,128)(2,1)S(1)}, u32[]{:S(2)}) copy-start(bf16[80,512]{1,0:T(8,128)(2,1)S(1)} %fusion.4.refs_0_) | copy-start | bytes 245764
  21.9 7.2 %collective-permute-start.5 = (bf16[80,512]{1,0:T(8,128)(2,1)S(1)}, bf16[80,512]{1,0:T(8,128)(2,1)S(1)}, u32[]{:S(2)}, u32[]{:S(2)}) collective-permute-start(bf16[80,512]{1,0:T(8,128)(2,1)S(1)} %fusion.4.refs_0_), channel_id=1, source_target_pairs={{0,24},{4,28},{8,16},{12,20},{16,8},{20,12},{24,0},{28,4},{1,25},{... | collective-permute-start | bytes 245768 | tf_op jit(solution)/shard_map/ppermute | solution.py:370
  24.6 6.4 %collective-permute-start.4 = (bf16[80,512]{1,0:T(8,128)(2,1)S(1)}, bf16[80,512]{1,0:T(8,128)(2,1)S(1)}, u32[]{:S(2)}, u32[]{:S(2)}) collective-permute-start(bf16[80,512]{1,0:T(8,128)(2,1)S(1)} %fusion.4.refs_0_), channel_id=1, source_target_pairs={{0,16},{4,20},{8,24},{12,28},{16,0},{20,4},{24,8},{28,12},{1,17},{... | collective-permute-start | bytes 245768 | tf_op jit(solution)/shard_map/ppermute | solution.py:370
  25.2 5.8 %collective-permute-start.3 = (bf16[80,512]{1,0:T(8,128)(2,1)S(1)}, bf16[80,512]{1,0:T(8,128)(2,1)S(1)}, u32[]{:S(2)}, u32[]{:S(2)}) collective-permute-start(bf16[80,512]{1,0:T(8,128)(2,1)S(1)} %fusion.4.refs_0_), channel_id=1, source_target_pairs={{0,8},{4,12},{8,0},{12,4},{16,24},{20,28},{24,16},{28,20},{1,9},{5... | collective-permute-start | bytes 245768 | tf_op jit(solution)/shard_map/ppermute | solution.py:370
  29.1 3.8 %copy-start.4 = (bf16[80,512]{1,0:T(8,128)(2,1)}, bf16[80,512]{1,0:T(8,128)(2,1)S(1)}, u32[]{:S(2)}) copy-start(bf16[80,512]{1,0:T(8,128)(2,1)S(1)} %collective-permute-done.5.refs_3_) | copy-start | bytes 245764
  31.0 1.9 %copy-start.5 = (bf16[80,512]{1,0:T(8,128)(2,1)}, bf16[80,512]{1,0:T(8,128)(2,1)S(1)}, u32[]{:S(2)}) copy-start(bf16[80,512]{1,0:T(8,128)(2,1)S(1)} %collective-permute-done.4.refs_2_) | copy-start | bytes 245764
  31.0 1.9 %copy-start.6 = (bf16[80,512]{1,0:T(8,128)(2,1)}, bf16[80,512]{1,0:T(8,128)(2,1)S(1)}, u32[]{:S(2)}) copy-start(bf16[80,512]{1,0:T(8,128)(2,1)S(1)} %collective-permute-done.3.refs_1_) | copy-start | bytes 245764
  31.3 1.6 %copy-start = (bf16[32,16,256]{2,1,0:T(8,128)(2,1)}, bf16[32,16,256]{2,1,0:T(8,128)(2,1)S(1)}, u32[]{:S(2)}) copy-start(bf16[32,16,256]{2,1,0:T(8,128)(2,1)S(1)} %all-to-all-done) | copy-start | bytes 786436
  31.3 1.6 %collective-permute-start.6 = (bf16[512,256]{1,0:T(8,128)(2,1)S(1)}, bf16[512,256]{1,0:T(8,128)(2,1)S(1)}, u32[]{:S(2)}, u32[]{:S(2)}) collective-permute-start(bf16[512,256]{1,0:T(8,128)(2,1)S(1)} %bitcast.4), channel_id=1, source_target_pairs={{0,4},{4,0},{8,12},{12,8},{16,20},{20,16},{24,28},{28,24},{1,5},{5... | collective-permute-start | bytes 786440 | tf_op jit(solution)/shard_map/ppermute | solution.py:370
  32.9 0.7 %copy-start.2 = (bf16[512,256]{1,0:T(8,128)(2,1)}, bf16[512,256]{1,0:T(8,128)(2,1)S(1)}, u32[]{:S(2)}) copy-start(bf16[512,256]{1,0:T(8,128)(2,1)S(1)} %collective-permute-done.6.refs_7_) | copy-start | bytes 786436

commit v3 on v2

--- a/solution.py
+++ b/solution.py
@@ -119,7 +119,7 @@
 HIGHEST = lax.Precision.HIGHEST
 NT_DIMS = (((1,), (1,)), ((), ()))
 TN_DIMS = (((0,), (0,)), ((), ()))
-VMEM_BYTES = 56 * 1024 * 1024
+VMEM_BYTES = 20 * 1024 * 1024
 PARTS_TYPE = jnp.bfloat16
 
 
@@ -178,17 +178,21 @@
     for half in range(2):
         high[:, half, :, :, :, half] = part
     high = high.reshape(n_blk, 2 * TILE_SIDE // n_blk, 16 * n_src * n_blk)
-    return low.astype(np.float32), (high / math.sqrt(F)).astype(np.float32)
+    high = split_bf16((high / math.sqrt(F)).astype(np.float32))
+    return low.astype(np.float32), np.concatenate(high, axis=1)
 
 
 def spectra_kernel(n_src, *refs):
     pieces = refs[:n_src]
     first_ref, twiddle_ref, third_ref, out_ref, samples, reals, imags = refs[n_src:]
-    stations, local = pieces[0].shape
+    stations, local = pieces[1].shape
+    src_index = lax.axis_index("src")
+    own = pieces[0].at[pl.ds(pl.multiple_of(src_index * stations, stations), stations), :]
+    pieces = (own,) + pieces[1:]
     per_src = local // LANES
     steps = per_src * n_src
     count = third_ref.shape[0] // 4
-    first = first_ref[lax.axis_index("src")]
+    first = first_ref[src_index]
     for k in range(n_src):
         for a in range(per_src):
             samples[pl.ds(k * per_src + a, stations, stride=steps), :] = pieces[k][
@@ -254,7 +258,7 @@
         pair = jnp.concatenate([pair[:, 0, :], pair[:, 1, :]], axis=1)
         green[:, lanes] = pair.astype(jnp.bfloat16)
     for k, pack in enumerate(packs):
-        classes[k * panel : (k + 1) * panel, :] = pack[:panel].astype(jnp.int32)
+        classes[k * panel : (k + 1) * panel, :] = pack[:panel].astype(jnp.float32)
         ids = pack[panel : panel + 16, :LANES].astype(jnp.int32)
         for row in range(2):
             numbers[k, row : row + 1] = jnp.concatenate(
@@ -271,24 +275,37 @@
     power = jnp.concatenate(power, axis=1)
     green_ids = lax.broadcasted_iota(jnp.int32, (green.shape[0], slots * panel), 0)
     tile_ids = lax.broadcasted_iota(jnp.int32, (tiles, slots * panel), 0)
-    class_ids = lax.broadcasted_iota(jnp.int32, (1, class_count, stations), 1)
+    class_ids = lax.broadcasted_iota(jnp.int32, (class_count, stations), 0).astype(jnp.float32)
+    class_ids = class_ids.astype(jnp.bfloat16).reshape(1, class_count // 16, 16, stations)
     total[...] = jnp.zeros_like(total)
 
     def mix(place):
         start = pl.multiple_of(place * panel, panel)
-        for part in range(panel // chunk):
-            at = pl.ds(start + part * chunk, chunk)
-            hot = jnp.where(classes[at, :][:, None, :] == class_ids, 1.0, 0.0)
-            grouped = jnp.dot(
-                hot.astype(jnp.bfloat16).reshape(chunk * class_count, stations),
-                spectra[...],
-                preferred_element_type=jnp.float32,
-            ).reshape(chunk, class_count, 4 * LANES)
+        places = [pl.ds(start + part * chunk, chunk) for part in range(panel // chunk)]
+
+        def one_hot(at):
+            wide = jnp.broadcast_to(classes[at, :][:, None, :], (chunk, 16, stations))
+            wide = wide.astype(jnp.bfloat16)[:, None]
+            hot = jnp.where(wide == class_ids, jnp.bfloat16(1.0), jnp.bfloat16(0.0))
+            return hot.reshape(chunk * class_count, stations)
+
+        def reduce(at, grouped):
+            grouped = grouped.reshape(chunk, class_count, 4 * LANES)
             for real, imag in (lanes[:2], lanes[2:]):
                 obs_real, obs_imag = bank[:, real][None], bank[:, imag][None]
                 group_real, group_imag = grouped[..., real], grouped[..., imag]
                 mixed[at, real] = jnp.sum(obs_real * group_real - obs_imag * group_imag, axis=1)
                 mixed[at, imag] = jnp.sum(obs_real * group_imag + obs_imag * group_real, axis=1)
+
+        hot, before = one_hot(places[0]), None
+        for part, at in enumerate(places):
+            grouped = jnp.dot(hot, spectra[...], preferred_element_type=jnp.float32)
+            if part + 1 < len(places):
+                hot = one_hot(places[part + 1])
+            if before is not None:
+                reduce(*before)
+            before = (at, grouped)
+        reduce(*before)
 
     def gather(place):
         at = pl.ds(pl.multiple_of(place * panel, panel), panel)
@@ -315,15 +332,13 @@
             preferred_element_type=jnp.float32,
         )
 
-    mix(0)
-
-    def one_panel(place, carry):
-        gather(place - 1)
+    def mix_panel(place, carry):
         mix(place)
         return carry
 
-    lax.fori_loop(1, panels, one_panel, 0)
-    gather(panels - 1)
+    lax.fori_loop(0, panels, mix_panel, 0)
+    for place in range(panels):
+        gather(place)
     low = [
         jnp.dot(
             total[:, at], low_ref[...], precision=HIGHEST, preferred_element_type=jnp.float32
@@ -349,13 +364,10 @@
 
 def image_kernel(high_ref, parts_ref, out_ref):
     high = high_ref[lax.axis_index("blk")]
-    image = jnp.dot(
-        high,
-        parts_ref[...].astype(jnp.float32),
-        precision=HIGHEST,
-        preferred_element_type=jnp.float32,
-    )
-    rows = high.shape[0] // 2
+    image = jnp.dot(high, parts_ref[...], preferred_element_type=jnp.float32)
+    count = image.shape[0] // 2
+    image = image[:count] + image[count:]
+    rows = count // 2
     for tile in range(out_ref.shape[0]):
         half, side = tile // 2, tile % 2
         for row in range(rows):
@@ -379,9 +391,10 @@
     tiles = TILE_DEV * n_src
     share = panel // n_src
     pieces = [
-        lax.dynamic_slice_in_dim(windows, (src_index ^ k) * share, share, 0) for k in range(n_src)
+        lax.dynamic_slice_in_dim(windows, (src_index ^ k) * share, share, 0)
+        for k in range(1, n_src)
     ]
-    pieces = [pieces[0]] + [swap(pieces[k], "src", k) for k in range(1, n_src)]
+    pieces = [windows] + [swap(piece, "src", k + 1) for k, piece in enumerate(pieces)]
 
     def widen(ids):
         return jnp.pad(ids, ((0, 8 - slots), (0, stations - panel)))
@@ -413,11 +426,11 @@
     panels = n_blk // 2
     spectra, packs = lax.optimization_barrier((spectra, packs))
     parts = pl.pallas_call(
-        functools.partial(adjoint_kernel, panels, slots, n_src, 8),
+        functools.partial(adjoint_kernel, panels, slots, n_src, 16),
         out_shape=jax.ShapeDtypeStruct((16 * devices, 2 * TILE_SIDE), PARTS_TYPE),
         scratch_shapes=[
             pltpu.VMEM((stations, 4 * LANES), jnp.bfloat16),
-            pltpu.VMEM((panels * panel, stations), jnp.int32),
+            pltpu.VMEM((panels * panel, stations), jnp.float32),
             pltpu.VMEM((panels, 8, slots * panel), jnp.int32),
             pltpu.VMEM((class_count, 4 * LANES), jnp.float32),
             pltpu.VMEM((green.shape[0], 4 * LANES), jnp.bfloat16),

time: 65.4 us -> 59.7 us (0.913)
  Pallas kernels: 22.8 us -> 17.3 us
  local copies, waits for them, and re-layouts: 3.55 us -> 2.79 us
  starting transfers between devices: 14 us -> 14.7 us
    pallas_call x1, Pallas kernels: 17 us -> 13.7 us  [split_body(): pl.pallas_call(functools.partial(adjoint_kernel, panels, slots, n_src, 16...]
    pallas_call x1, Pallas kernels: 3.86 us -> 2.73 us  [split_body(): pl.pallas_call(functools.partial(spectra_kernel, n_src), out_shape=jax.Sh...]
    pallas_call x1, Pallas kernels: 1.89 us -> 0.82 us  [split_body(): pl.pallas_call(image_kernel, out_shape=jax.ShapeDtypeStruct((TILE_DEV, TP...]
    unnamed x24 -> x22, local copies, waits for them, and re-layouts: 1.99 us -> 1.82 us
  transfers between devices with their start and end apart: 8 -> 8, of which waited for: 7 -> 6; matrix products, arithmetic and copies ran while one was open for 0% -> 0% of each run, Pallas kernels for 0% -> 0%
where the time goes in v3:
time: 59.7 us; the launch traced here: 59.5 us
  Pallas kernels  17.3 us (29%)
  starting transfers between devices  14.7 us (25%)
  waiting for transfers between devices  12.7 us (21%)
  blocking collectives  11.9 us (20%)
  local copies, waits for them, and re-layouts  2.79 us (5%)
    pallas_call x1, Pallas kernels, split_body(): pl.pallas_call(functools.partial(adjoint_kernel, panels, slots, n_src, 16...  13.7 us
    ppermute x7, waiting for transfers between devices, swap(): return lax.ppermute(values, axis, [(i, i ^ distance) for i in range(size)])  12 us
    all_to_all x1, blocking collectives, split_body(): lax.all_to_all(parts.reshape(devices, 16, 2 * TILE_SIDE), BOTH, 0, 0, til...  11.9 us
    ppermute x7, starting transfers between devices, swap(): return lax.ppermute(values, axis, [(i, i ^ distance) for i in range(size)])  9.71 us
    all_to_all x1, starting transfers between devices, split_body(): lax.all_to_all(blocks.reshape(devices, share, 2 * LANES), BOTH, 0, 0, til...  4.97 us
    pallas_call x1, Pallas kernels, split_body(): pl.pallas_call(functools.partial(spectra_kernel, n_src), out_shape=jax.Sh...  2.73 us
    unnamed x22, local copies, waits for them, and re-layouts  1.82 us
  transfers between devices with their start and end apart: 8, of which 6 were waited for; matrix products, arithmetic and copies ran while one was open for 0% of the time, Pallas kernels for 0%

profile of v3, /device:TPU:0, one launch (start us, length us, event | category | flops | bytes accessed | tf_op | source)
XLA Modules:
  0.0 59.5 jit_solution(4579613355130576792)
XLA Ops:
  0.0 0.0 copy-start
  0.0 0.0 copy-start.6
  0.0 1.0 %constant_dynamic-slice_fusion = (bf16[16,2048]{1,0:T(8,128)(2,1)S(1)}, bf16[16,2048]{1,0:T(8,128)(2,1)S(1)}, bf16[16,2048]{1,0:T(8,128)(2,1)S(1)}) fusion(bf16[64,2048]{1,0:T(8,128)(2,1)} %refs_0_.1, s32[]{:T(128)S(6)} %select_n.11, s32[]{:T(128)S(6)} %select_n.10, s32[]{:T(128)S(6)} %select_n.9), kind=kLoop, calls=%fused_computation.8 | loop fusion | bytes 393228 | tf_op jit(solution)/shard_map/dynamic_slice | solution.py:394
  1.0 5.1 %collective-permute-start.2 = (bf16[16,2048]{1,0:T(8,128)(2,1)S(1)}, bf16[16,2048]{1,0:T(8,128)(2,1)S(1)}, u32[]{:S(2)}, u32[]{:S(2)}) collective-permute-start(bf16[16,2048]{1,0:T(8,128)(2,1)S(1)} %get-tuple-element.15), channel_id=1, source_target_pairs={{0,3},{1,2},{2,1},{3,0},{4,7},{5,6},{6,5},{7,4},{8,11},{9,10},{10,... | collective-permute-start | bytes 196616 | tf_op jit(solution)/shard_map/ppermute | solution.py:382
  6.1 0.0 collective-permute-start.1
  6.1 0.6 %collective-permute-start = (bf16[16,2048]{1,0:T(8,128)(2,1)S(1)}, bf16[16,2048]{1,0:T(8,128)(2,1)S(1)}, u32[]{:S(2)}, u32[]{:S(2)}) collective-permute-start(bf16[16,2048]{1,0:T(8,128)(2,1)S(1)} %get-tuple-element.17), channel_id=1, source_target_pairs={{0,1},{1,0},{2,3},{3,2},{4,5},{5,4},{6,7},{7,6},{8,9},{9,8},{10,11... | collective-permute-start | bytes 196616 | tf_op jit(solution)/shard_map/ppermute | solution.py:382
  6.7 1.9 %collective-permute-done.2.refs_3_ = bf16[16,2048]{1,0:T(8,128)(2,1)S(1)} collective-permute-done((bf16[16,2048]{1,0:T(8,128)(2,1)S(1)}, bf16[16,2048]{1,0:T(8,128)(2,1)S(1)}, u32[]{:S(2)}, u32[]{:S(2)}) %collective-permute-start.2) | collective-permute-done | bytes 65568 | tf_op jit(solution)/shard_map/ppermute | solution.py:382
  8.7 3.0 %collective-permute-done.1.refs_2_ = bf16[16,2048]{1,0:T(8,128)(2,1)S(1)} collective-permute-done((bf16[16,2048]{1,0:T(8,128)(2,1)S(1)}, bf16[16,2048]{1,0:T(8,128)(2,1)S(1)}, u32[]{:S(2)}, u32[]{:S(2)}) %collective-permute-start.1) | collective-permute-done | bytes 65568 | tf_op jit(solution)/shard_map/ppermute | solution.py:382
  11.7 0.0 collective-permute-done.refs_1_
  11.7 0.0 copy-done
  11.7 0.0 copy-done.6
  11.7 0.0 copy-start.5
  11.7 0.9 %copy-done.5 = bf16[4,256,64]{2,1,0:T(8,128)(2,1)S(1)} copy-done((bf16[4,256,64]{2,1,0:T(8,128)(2,1)S(1)}, bf16[4,256,64]{2,1,0:T(8,128)(2,1)}, u32[]{:S(2)}) %copy-start.5) | copy-done | bytes 131096
  12.7 0.0 copy-start.7
  12.7 0.8 %copy-done.7 = bf16[128,256]{1,0:T(8,128)(2,1)S(1)} copy-done((bf16[128,256]{1,0:T(8,128)(2,1)S(1)}, bf16[128,256]{1,0:T(8,128)(2,1)}, u32[]{:S(2)}) %copy-start.7) | copy-done | bytes 65560
  13.5 0.0 copy-start.9
  13.5 0.0 copy-start.8
  13.5 2.7 %spectra.1 = bf16[512,256]{1,0:T(8,128)(2,1)} custom-call(bf16[64,2048]{1,0:T(8,128)(2,1)S(1)} %copy-done, bf16[16,2048]{1,0:T(8,128)(2,1)S(1)} %collective-permute-done.refs_1_, bf16[16,2048]{1,0:T(8,128)(2,1)S(1)} %collective-permute-done.1.refs_2_, bf16[16,2048]{1,0:T(8,128)(2,1)S(1)} %collective-permute-done.2.refs_3_, ...), custom_call_target="tpu_custom_call" | custom-call | tf_op jit(solution)/shard_map/spectra/pallas_call | solution.py:411
  16.2 0.0 copy-start.10
  16.2 0.0 copy-start.2
  16.2 0.0 copy-start.3
  16.2 5.0 %all-to-all-start = ((bf16[32,16,256]{2,1,0:T(8,128)(2,1)}), bf16[32,16,256]{2,1,0:T(8,128)(2,1)S(1)}, u32[]{:S(2)}, u32[]{:S(2)}) async-start(bf16[32,16,256]{2,1,0:T(8,128)(2,1)} %bitcast), calls=%async_computation | async-start | bytes 524288 | tf_op jit(solution)/shard_map/all_to_all | solution.py:422
  21.2 0.0 copy-done.9
  21.2 0.0 copy-start.1
  21.2 0.0 copy-done.10
  21.3 0.0 copy-done.8
  21.3 2.7 %collective-permute-start.5 = (bf16[80,512]{1,0:T(8,128)(2,1)S(1)}, bf16[80,512]{1,0:T(8,128)(2,1)S(1)}, u32[]{:S(2)}, u32[]{:S(2)}) collective-permute-start(bf16[80,512]{1,0:T(8,128)(2,1)S(1)} %fusion.4.refs_0_), channel_id=1, source_target_pairs={{0,24},{4,28},{8,16},{12,20},{16,8},{20,12},{24,0},{28,4},{1,25},{... | collective-permute-start | bytes 245768 | tf_op jit(solution)/shard_map/ppermute | solution.py:382
  24.0 0.6 collective-permute-start.4
  24.6 0.3 collective-permute-start.3
  24.9 4.3 %collective-permute-done.5.refs_3_ = bf16[80,512]{1,0:T(8,128)(2,1)S(1)} collective-permute-done((bf16[80,512]{1,0:T(8,128)(2,1)S(1)}, bf16[80,512]{1,0:T(8,128)(2,1)S(1)}, u32[]{:S(2)}, u32[]{:S(2)}) %collective-permute-start.5) | collective-permute-done | bytes 81952 | tf_op jit(solution)/shard_map/ppermute | solution.py:382
  29.2 1.6 %collective-permute-done.4.refs_2_ = bf16[80,512]{1,0:T(8,128)(2,1)S(1)} collective-permute-done((bf16[80,512]{1,0:T(8,128)(2,1)S(1)}, bf16[80,512]{1,0:T(8,128)(2,1)S(1)}, u32[]{:S(2)}, u32[]{:S(2)}) %collective-permute-start.4) | collective-permute-done | bytes 81952 | tf_op jit(solution)/shard_map/ppermute | solution.py:382
  30.7 0.0 collective-permute-done.3.refs_1_
  30.7 0.7 %all-to-all-done = bf16[32,16,256]{2,1,0:T(8,128)(2,1)S(1)} async-done(((bf16[32,16,256]{2,1,0:T(8,128)(2,1)}), bf16[32,16,256]{2,1,0:T(8,128)(2,1)S(1)}, u32[]{:S(2)}, u32[]{:S(2)}) %all-to-all-start) | async-done | bytes 262176 | tf_op jit(solution)/shard_map/all_to_all | solution.py:422
  31.4 0.4 collective-permute-start.6
  31.8 1.2 %collective-permute-done.6.refs_7_ = bf16[512,256]{1,0:T(8,128)(2,1)S(1)} collective-permute-done((bf16[512,256]{1,0:T(8,128)(2,1)S(1)}, bf16[512,256]{1,0:T(8,128)(2,1)S(1)}, u32[]{:S(2)}, u32[]{:S(2)}) %collective-permute-start.6) | collective-permute-done | bytes 262176 | tf_op jit(solution)/shard_map/ppermute | solution.py:382
  33.0 0.0 copy-done.2
  33.0 0.0 copy-done.3
  33.0 0.0 copy-done.1
  33.0 13.7 %adjoint.1 = bf16[512,128]{1,0:T(8,128)(2,1)S(1)} custom-call(bf16[80,512]{1,0:T(8,128)(2,1)S(1)} %fusion.4.refs_0_, bf16[80,512]{1,0:T(8,128)(2,1)S(1)} %collective-permute-done.3.refs_1_, bf16[80,512]{1,0:T(8,128)(2,1)S(1)} %collective-permute-done.4.refs_2_, bf16[80,512]{1,0:T(8,128)(2,1)S(1)} %collective-permute-done.5.refs_3_, ...), custom_call_target="tpu_custom_call" | custom-call | tf_op jit(solution)/shard_map/adjoint/pallas_call | solution.py:428
  46.7 0.0 copy-start.4
  46.7 11.9 %all_to_all.10 = bf16[32,16,128]{2,1,0:T(8,128)(2,1)S(1)} all-to-all(bf16[32,16,128]{2,1,0:T(8,128)(2,1)S(1)} %bitcast.6), channel_id=1, replica_groups=mesh['blk'=8,'src'=4] {'blk','src'}, dimensions={0} | all-to-all | bytes 262144 | tf_op jit(solution)/shard_map/all_to_all | solution.py:443
  58.6 0.0 copy-done.4
  58.6 0.8 %image.1 = f32[4,512]{1,0:T(4,128)} custom-call(bf16[8,32,512]{2,1,0:T(8,128)(2,1)S(1)} %copy-done.4, bf16[512,128]{1,0:T(8,128)(2,1)S(1)} %bitcast.7), custom_call_target="tpu_custom_call" | custom-call | tf_op jit(solution)/shard_map/image/pallas_call | solution.py:446
  (4 shorter events, 0.0 us)
Async XLA Ops:
  0.0 11.7 %copy-start = (bf16[64,2048]{1,0:T(8,128)(2,1)S(1)}, bf16[64,2048]{1,0:T(8,128)(2,1)}, u32[]{:S(2)}) copy-start(bf16[64,2048]{1,0:T(8,128)(2,1)} %refs_0_.1) | copy-start | bytes 786436
  0.0 11.7 %copy-start.6 = (f32[2,128,128]{2,1,0:T(8,128)S(1)}, f32[2,128,128]{2,1,0:T(8,128)}, u32[]{:S(2)}) copy-start(f32[2,128,128]{2,1,0:T(8,128)} %constant.29.clone.refs_5_) | copy-start | bytes 393220
  1.0 7.7 %collective-permute-start.2 = (bf16[16,2048]{1,0:T(8,128)(2,1)S(1)}, bf16[16,2048]{1,0:T(8,128)(2,1)S(1)}, u32[]{:S(2)}, u32[]{:S(2)}) collective-permute-start(bf16[16,2048]{1,0:T(8,128)(2,1)S(1)} %get-tuple-element.15), channel_id=1, source_target_pairs={{0,3},{1,2},{2,1},{3,0},{4,7},{5,6},{6,5},{7,4},{8,11},{9,10},{10,... | collective-permute-start | bytes 196616 | tf_op jit(solution)/shard_map/ppermute | solution.py:382
  6.1 5.6 %collective-permute-start.1 = (bf16[16,2048]{1,0:T(8,128)(2,1)S(1)}, bf16[16,2048]{1,0:T(8,128)(2,1)S(1)}, u32[]{:S(2)}, u32[]{:S(2)}) collective-permute-start(bf16[16,2048]{1,0:T(8,128)(2,1)S(1)} %get-tuple-element.16), channel_id=1, source_target_pairs={{0,2},{1,3},{2,0},{3,1},{4,6},{5,7},{6,4},{7,5},{8,10},{9,11},{10,... | collective-permute-start | bytes 196616 | tf_op jit(solution)/shard_map/ppermute | solution.py:382
  6.1 5.6 %collective-permute-start = (bf16[16,2048]{1,0:T(8,128)(2,1)S(1)}, bf16[16,2048]{1,0:T(8,128)(2,1)S(1)}, u32[]{:S(2)}, u32[]{:S(2)}) collective-permute-start(bf16[16,2048]{1,0:T(8,128)(2,1)S(1)} %get-tuple-element.17), channel_id=1, source_target_pairs={{0,1},{1,0},{2,3},{3,2},{4,5},{5,4},{6,7},{7,6},{8,9},{9,8},{10,11... | collective-permute-start | bytes 196616 | tf_op jit(solution)/shard_map/ppermute | solution.py:382
  11.7 1.0 %copy-start.5 = (bf16[4,256,64]{2,1,0:T(8,128)(2,1)S(1)}, bf16[4,256,64]{2,1,0:T(8,128)(2,1)}, u32[]{:S(2)}) copy-start(bf16[4,256,64]{2,1,0:T(8,128)(2,1)} %constant.28.clone.refs_4_) | copy-start | bytes 393220
  12.7 0.8 %copy-start.7 = (bf16[128,256]{1,0:T(8,128)(2,1)S(1)}, bf16[128,256]{1,0:T(8,128)(2,1)}, u32[]{:S(2)}) copy-start(bf16[128,256]{1,0:T(8,128)(2,1)} %constant.30.clone.refs_6_) | copy-start | bytes 196612
  13.5 7.7 %copy-start.9 = (s32[4,64]{1,0:T(4,128)S(1)}, s32[4,64]{1,0:T(4,128)}, u32[]{:S(2)}) copy-start(s32[4,64]{1,0:T(4,128)} %param.15) | copy-start | bytes 3076
  13.5 7.8 %copy-start.8 = (s32[64,512]{1,0:T(8,128)S(1)}, s32[64,512]{1,0:T(8,128)}, u32[]{:S(2)}) copy-start(s32[64,512]{1,0:T(8,128)} %param.13) | copy-start | bytes 393220
  16.2 5.0 %copy-start.10 = (s32[4,64]{1,0:T(4,128)S(1)}, s32[4,64]{1,0:T(4,128)}, u32[]{:S(2)}) copy-start(s32[4,64]{1,0:T(4,128)} %param.16) | copy-start | bytes 3076
  16.2 16.7 %copy-start.2 = (bf16[64,2,1024]{2,1,0:T(2,128)(2,1)S(1)}, bf16[64,2,1024]{2,1,0:T(2,128)(2,1)}, u32[]{:S(2)}) copy-start(bf16[64,2,1024]{2,1,0:T(2,128)(2,1)} %refs_5_.2) | copy-start | bytes 786436
  16.2 16.7 %copy-start.3 = (f32[256,256]{1,0:T(8,128)S(1)}, f32[256,256]{1,0:T(8,128)}, u32[]{:S(2)}) copy-start(f32[256,256]{1,0:T(8,128)} %constant.31.clone.refs_8_) | copy-start | bytes 786436
  16.2 15.2 %all-to-all-start = ((bf16[32,16,256]{2,1,0:T(8,128)(2,1)}), bf16[32,16,256]{2,1,0:T(8,128)(2,1)S(1)}, u32[]{:S(2)}, u32[]{:S(2)}) async-start(bf16[32,16,256]{2,1,0:T(8,128)(2,1)} %bitcast), calls=%async_computation | async-start | bytes 524288 | tf_op jit(solution)/shard_map/all_to_all | solution.py:422
  21.2 11.8 %copy-start.1 = (bf16[64,2,1024]{2,1,0:T(2,128)(2,1)S(1)}, bf16[64,2,1024]{2,1,0:T(2,128)(2,1)}, u32[]{:S(2)}) copy-start(bf16[64,2,1024]{2,1,0:T(2,128)(2,1)} %refs_4_.2) | copy-start | bytes 786436
  21.3 7.8 %collective-permute-start.5 = (bf16[80,512]{1,0:T(8,128)(2,1)S(1)}, bf16[80,512]{1,0:T(8,128)(2,1)S(1)}, u32[]{:S(2)}, u32[]{:S(2)}) collective-permute-start(bf16[80,512]{1,0:T(8,128)(2,1)S(1)} %fusion.4.refs_0_), channel_id=1, source_target_pairs={{0,24},{4,28},{8,16},{12,20},{16,8},{20,12},{24,0},{28,4},{1,25},{... | collective-permute-start | bytes 245768 | tf_op jit(solution)/shard_map/ppermute | solution.py:382
  24.0 6.7 %collective-permute-start.4 = (bf16[80,512]{1,0:T(8,128)(2,1)S(1)}, bf16[80,512]{1,0:T(8,128)(2,1)S(1)}, u32[]{:S(2)}, u32[]{:S(2)}) collective-permute-start(bf16[80,512]{1,0:T(8,128)(2,1)S(1)} %fusion.4.refs_0_), channel_id=1, source_target_pairs={{0,16},{4,20},{8,24},{12,28},{16,0},{20,4},{24,8},{28,12},{1,17},{... | collective-permute-start | bytes 245768 | tf_op jit(solution)/shard_map/ppermute | solution.py:382
  24.6 6.1 %collective-permute-start.3 = (bf16[80,512]{1,0:T(8,128)(2,1)S(1)}, bf16[80,512]{1,0:T(8,128)(2,1)S(1)}, u32[]{:S(2)}, u32[]{:S(2)}) collective-permute-start(bf16[80,512]{1,0:T(8,128)(2,1)S(1)} %fusion.4.refs_0_), channel_id=1, source_target_pairs={{0,8},{4,12},{8,0},{12,4},{16,24},{20,28},{24,16},{28,20},{1,9},{5... | collective-permute-start | bytes 245768 | tf_op jit(solution)/shard_map/ppermute | solution.py:382
  31.4 1.6 %collective-permute-start.6 = (bf16[512,256]{1,0:T(8,128)(2,1)S(1)}, bf16[512,256]{1,0:T(8,128)(2,1)S(1)}, u32[]{:S(2)}, u32[]{:S(2)}) collective-permute-start(bf16[512,256]{1,0:T(8,128)(2,1)S(1)} %bitcast.4), channel_id=1, source_target_pairs={{0,4},{4,0},{8,12},{12,8},{16,20},{20,16},{24,28},{28,24},{1,5},{5... | collective-permute-start | bytes 786440 | tf_op jit(solution)/shard_map/ppermute | solution.py:382
  46.7 11.9 %copy-start.4 = (bf16[8,32,512]{2,1,0:T(8,128)(2,1)S(1)}, bf16[8,32,512]{2,1,0:T(8,128)(2,1)}, u32[]{:S(2)}) copy-start(bf16[8,32,512]{2,1,0:T(8,128)(2,1)} %constant.32.clone.high_ref) | copy-start | bytes 786436

commit v4 on v3

--- a/solution.py
+++ b/solution.py
@@ -131,15 +131,10 @@
 
 def forward_tables(n_src, n_blk):
     steps = NT // LANES
-    per_src = steps // n_src
-    own = np.arange(n_src)
-    order = np.stack(
-        [np.concatenate([(s ^ k) * per_src + np.arange(per_src) for k in range(n_src)]) for s in own]
-    )
     rows = np.arange(steps)
-    angle = 2 * np.pi / steps * ((rows[None, :, None] * order[:, None, :]) % steps)
-    first = np.concatenate([np.cos(angle), -np.sin(angle)], axis=1).astype(np.float32)
-    first = np.concatenate(split_bf16(first), axis=1)
+    angle = 2 * np.pi / steps * ((rows[:, None] * rows[None, :]) % steps)
+    first = np.concatenate([np.cos(angle), -np.sin(angle)], axis=0).astype(np.float32)
+    first = np.concatenate(split_bf16(first), axis=0)
     lanes = np.arange(LANES)
     angle = 2 * np.pi / NT * ((lanes[:, None] * lanes[None, :]) % NT)
     twiddle = np.stack([np.cos(angle), -np.sin(angle)]).astype(np.float32)
@@ -187,15 +182,14 @@
     first_ref, twiddle_ref, third_ref, out_ref, samples, reals, imags = refs[n_src:]
     stations, local = pieces[1].shape
     src_index = lax.axis_index("src")
-    own = pieces[0].at[pl.ds(pl.multiple_of(src_index * stations, stations), stations), :]
-    pieces = (own,) + pieces[1:]
     per_src = local // LANES
     steps = per_src * n_src
     count = third_ref.shape[0] // 4
-    first = first_ref[src_index]
+    first = first_ref[...]
     for k in range(n_src):
+        start = (src_index ^ k) * per_src
         for a in range(per_src):
-            samples[pl.ds(k * per_src + a, stations, stride=steps), :] = pieces[k][
+            samples[pl.ds(start + a, stations, stride=steps), :] = pieces[k][
                 :, a * LANES : (a + 1) * LANES
             ].astype(jnp.float32)
     twiddle_real, twiddle_imag = twiddle_ref[0], twiddle_ref[1]
@@ -332,13 +326,11 @@
             preferred_element_type=jnp.float32,
         )
 
-    def mix_panel(place, carry):
+    mix(0)
+    for place in range(1, panels):
         mix(place)
-        return carry
-
-    lax.fori_loop(0, panels, mix_panel, 0)
-    for place in range(panels):
-        gather(place)
+        gather(place - 1)
+    gather(panels - 1)
     low = [
         jnp.dot(
             total[:, at], low_ref[...], precision=HIGHEST, preferred_element_type=jnp.float32
@@ -392,9 +384,9 @@
     share = panel // n_src
     pieces = [
         lax.dynamic_slice_in_dim(windows, (src_index ^ k) * share, share, 0)
-        for k in range(1, n_src)
+        for k in range(n_src)
     ]
-    pieces = [windows] + [swap(piece, "src", k + 1) for k, piece in enumerate(pieces)]
+    pieces = pieces[:1] + [swap(pieces[k], "src", k) for k in range(1, n_src)]
 
     def widen(ids):
         return jnp.pad(ids, ((0, 8 - slots), (0, stations - panel)))

time: 59.7 us -> 56.4 us (0.945)
  local copies, waits for them, and re-layouts: 2.79 us -> 1.04 us
  Pallas kernels: 17.3 us -> 16.2 us
  starting transfers between devices: 14.7 us -> 14.1 us
    unnamed x22 -> x20, local copies, waits for them, and re-layouts: 1.82 us -> 0.05 us
    pallas_call x1, Pallas kernels: 13.7 us -> 12.5 us  [split_body(): pl.pallas_call(functools.partial(adjoint_kernel, panels, slots, n_src, 16...]
  transfers between devices with their start and end apart: 8 -> 8, of which waited for: 6 -> 7; matrix products, arithmetic and copies ran while one was open for 0% -> 0% of each run, Pallas kernels for 0% -> 0%
where the time goes in v4:
time: 56.4 us; the launch traced here: 56.1 us
  Pallas kernels  16.2 us (29%)
  starting transfers between devices  14.1 us (25%)
  waiting for transfers between devices  12.7 us (23%)
  blocking collectives  11.9 us (21%)
  local copies, waits for them, and re-layouts  1.04 us (2%)
    pallas_call x1, Pallas kernels, split_body(): pl.pallas_call(functools.partial(adjoint_kernel, panels, slots, n_src, 16...  12.5 us
    ppermute x7, waiting for transfers between devices, swap(): return lax.ppermute(values, axis, [(i, i ^ distance) for i in range(size)])  12 us
    all_to_all x1, blocking collectives, split_body(): lax.all_to_all(parts.reshape(devices, 16, 2 * TILE_SIDE), BOTH, 0, 0, til...  11.9 us
    ppermute x7, starting transfers between devices, swap(): return lax.ppermute(values, axis, [(i, i ^ distance) for i in range(size)])  9.72 us
    all_to_all x1, starting transfers between devices, split_body(): lax.all_to_all(blocks.reshape(devices, share, 2 * LANES), BOTH, 0, 0, til...  4.42 us
    pallas_call x1, Pallas kernels, split_body(): pl.pallas_call(functools.partial(spectra_kernel, n_src), out_shape=jax.Sh...  2.83 us
  transfers between devices with their start and end apart: 8, of which 7 were waited for; matrix products, arithmetic and copies ran while one was open for 0% of the time, Pallas kernels for 0%

profile of v4, /device:TPU:0, one launch (start us, length us, event | category | flops | bytes accessed | tf_op | source)
XLA Modules:
  0.0 56.1 jit_solution(14679346646671208113)
XLA Ops:
  0.0 0.0 copy-start.4
  0.0 0.0 copy-start.5
  0.0 0.0 copy-start.6
  0.0 1.0 %constant_dynamic-slice_fusion = (bf16[16,2048]{1,0:T(8,128)(2,1)S(1)}, bf16[16,2048]{1,0:T(8,128)(2,1)S(1)}, bf16[16,2048]{1,0:T(8,128)(2,1)S(1)}, bf16[16,2048]{1,0:T(8,128)(2,1)S(1)}) fusion(bf16[64,2048]{1,0:T(8,128)(2,1)} %param.11, s32[]{:T(128)S(6)} %select_n.15, s32[]{:T(128)S(6)} %select_n.13, s32[]{:T(128)S(6)} %select_n.12, s32[]{:T(128)S(6)} %select_n.14), kind=kLoop, calls=%fused_computation.8 | loop fusion | bytes 524304 | tf_op jit(solution)/shard_map/dynamic_slice | solution.py:386
  1.0 5.1 %collective-permute-start.2 = (bf16[16,2048]{1,0:T(8,128)(2,1)S(1)}, bf16[16,2048]{1,0:T(8,128)(2,1)S(1)}, u32[]{:S(2)}, u32[]{:S(2)}) collective-permute-start(bf16[16,2048]{1,0:T(8,128)(2,1)S(1)} %get-tuple-element.15), channel_id=1, source_target_pairs={{0,3},{1,2},{2,1},{3,0},{4,7},{5,6},{6,5},{7,4},{8,11},{9,10},{10,... | collective-permute-start | bytes 196616 | tf_op jit(solution)/shard_map/ppermute | solution.py:374
  6.1 0.0 collective-permute-start
  6.1 0.6 %collective-permute-start.1 = (bf16[16,2048]{1,0:T(8,128)(2,1)S(1)}, bf16[16,2048]{1,0:T(8,128)(2,1)S(1)}, u32[]{:S(2)}, u32[]{:S(2)}) collective-permute-start(bf16[16,2048]{1,0:T(8,128)(2,1)S(1)} %get-tuple-element.18), channel_id=1, source_target_pairs={{0,2},{1,3},{2,0},{3,1},{4,6},{5,7},{6,4},{7,5},{8,10},{9,11},{10,... | collective-permute-start | bytes 196616 | tf_op jit(solution)/shard_map/ppermute | solution.py:374
  6.8 2.3 %collective-permute-done.2.refs_3_ = bf16[16,2048]{1,0:T(8,128)(2,1)S(1)} collective-permute-done((bf16[16,2048]{1,0:T(8,128)(2,1)S(1)}, bf16[16,2048]{1,0:T(8,128)(2,1)S(1)}, u32[]{:S(2)}, u32[]{:S(2)}) %collective-permute-start.2) | collective-permute-done | bytes 65568 | tf_op jit(solution)/shard_map/ppermute | solution.py:374
  9.0 1.8 %collective-permute-done.refs_1_ = bf16[16,2048]{1,0:T(8,128)(2,1)S(1)} collective-permute-done((bf16[16,2048]{1,0:T(8,128)(2,1)S(1)}, bf16[16,2048]{1,0:T(8,128)(2,1)S(1)}, u32[]{:S(2)}, u32[]{:S(2)}) %collective-permute-start) | collective-permute-done | bytes 65568 | tf_op jit(solution)/shard_map/ppermute | solution.py:374
  10.8 1.0 %collective-permute-done.1.refs_2_ = bf16[16,2048]{1,0:T(8,128)(2,1)S(1)} collective-permute-done((bf16[16,2048]{1,0:T(8,128)(2,1)S(1)}, bf16[16,2048]{1,0:T(8,128)(2,1)S(1)}, u32[]{:S(2)}, u32[]{:S(2)}) %collective-permute-start.1) | collective-permute-done | bytes 65568 | tf_op jit(solution)/shard_map/ppermute | solution.py:374
  11.8 0.0 copy-done.4
  11.8 0.0 copy-done.5
  11.8 0.0 copy-done.6
  11.8 0.0 copy-start.8
  11.8 0.0 copy-start.7
  11.8 2.8 %spectra.1 = bf16[512,256]{1,0:T(8,128)(2,1)} custom-call(bf16[16,2048]{1,0:T(8,128)(2,1)S(1)} %get-tuple-element.17.refs_0_, bf16[16,2048]{1,0:T(8,128)(2,1)S(1)} %collective-permute-done.refs_1_, bf16[16,2048]{1,0:T(8,128)(2,1)S(1)} %collective-permute-done.1.refs_2_, bf16[16,2048]{1,0:T(8,128)(2,1)S(1)} %collective-permute-done.2.refs_3_, ...), custom_call_target="tpu_custom_call" | custom-call | tf_op jit(solution)/shard_map/spectra/pallas_call | solution.py:403
  14.6 0.0 copy-start.9
  14.6 0.0 copy-start.1
  14.6 0.0 copy-start.2
  14.6 4.4 %all-to-all-start = ((bf16[32,16,256]{2,1,0:T(8,128)(2,1)}), bf16[32,16,256]{2,1,0:T(8,128)(2,1)S(1)}, u32[]{:S(2)}, u32[]{:S(2)}) async-start(bf16[32,16,256]{2,1,0:T(8,128)(2,1)} %bitcast), calls=%async_computation | async-start | bytes 524288 | tf_op jit(solution)/shard_map/all_to_all | solution.py:414
  19.1 0.0 copy-done.8
  19.1 0.0 copy-start
  19.1 0.0 copy-done.9
  19.1 0.0 copy-done.7
  19.2 2.7 %collective-permute-start.5 = (bf16[80,512]{1,0:T(8,128)(2,1)S(1)}, bf16[80,512]{1,0:T(8,128)(2,1)S(1)}, u32[]{:S(2)}, u32[]{:S(2)}) collective-permute-start(bf16[80,512]{1,0:T(8,128)(2,1)S(1)} %fusion.4.refs_0_), channel_id=1, source_target_pairs={{0,24},{4,28},{8,16},{12,20},{16,8},{20,12},{24,0},{28,4},{1,25},{... | collective-permute-start | bytes 245768 | tf_op jit(solution)/shard_map/ppermute | solution.py:374
  21.9 0.6 collective-permute-start.4
  22.5 0.3 collective-permute-start.3
  22.7 4.3 %collective-permute-done.5.refs_3_ = bf16[80,512]{1,0:T(8,128)(2,1)S(1)} collective-permute-done((bf16[80,512]{1,0:T(8,128)(2,1)S(1)}, bf16[80,512]{1,0:T(8,128)(2,1)S(1)}, u32[]{:S(2)}, u32[]{:S(2)}) %collective-permute-start.5) | collective-permute-done | bytes 81952 | tf_op jit(solution)/shard_map/ppermute | solution.py:374
  27.0 1.6 %collective-permute-done.4.refs_2_ = bf16[80,512]{1,0:T(8,128)(2,1)S(1)} collective-permute-done((bf16[80,512]{1,0:T(8,128)(2,1)S(1)}, bf16[80,512]{1,0:T(8,128)(2,1)S(1)}, u32[]{:S(2)}, u32[]{:S(2)}) %collective-permute-start.4) | collective-permute-done | bytes 81952 | tf_op jit(solution)/shard_map/ppermute | solution.py:374
  28.6 0.0 collective-permute-done.3.refs_1_
  28.6 0.7 %all-to-all-done = bf16[32,16,256]{2,1,0:T(8,128)(2,1)S(1)} async-done(((bf16[32,16,256]{2,1,0:T(8,128)(2,1)}), bf16[32,16,256]{2,1,0:T(8,128)(2,1)S(1)}, u32[]{:S(2)}, u32[]{:S(2)}) %all-to-all-start) | async-done | bytes 262176 | tf_op jit(solution)/shard_map/all_to_all | solution.py:414
  29.3 0.4 collective-permute-start.6
  29.7 1.2 %collective-permute-done.6.refs_7_ = bf16[512,256]{1,0:T(8,128)(2,1)S(1)} collective-permute-done((bf16[512,256]{1,0:T(8,128)(2,1)S(1)}, bf16[512,256]{1,0:T(8,128)(2,1)S(1)}, u32[]{:S(2)}, u32[]{:S(2)}) %collective-permute-start.6) | collective-permute-done | bytes 262176 | tf_op jit(solution)/shard_map/ppermute | solution.py:374
  30.8 0.0 copy-done.1
  30.8 0.0 copy-done.2
  30.8 0.0 copy-done
  30.8 12.5 %adjoint.1 = bf16[512,128]{1,0:T(8,128)(2,1)S(1)} custom-call(bf16[80,512]{1,0:T(8,128)(2,1)S(1)} %fusion.4.refs_0_, bf16[80,512]{1,0:T(8,128)(2,1)S(1)} %collective-permute-done.3.refs_1_, bf16[80,512]{1,0:T(8,128)(2,1)S(1)} %collective-permute-done.4.refs_2_, bf16[80,512]{1,0:T(8,128)(2,1)S(1)} %collective-permute-done.5.refs_3_, ...), custom_call_target="tpu_custom_call" | custom-call | tf_op jit(solution)/shard_map/adjoint/pallas_call | solution.py:420
  43.4 0.0 copy-start.3
  43.4 11.9 %all_to_all.10 = bf16[32,16,128]{2,1,0:T(8,128)(2,1)S(1)} all-to-all(bf16[32,16,128]{2,1,0:T(8,128)(2,1)S(1)} %bitcast.6), channel_id=1, replica_groups=mesh['blk'=8,'src'=4] {'blk','src'}, dimensions={0} | all-to-all | bytes 262144 | tf_op jit(solution)/shard_map/all_to_all | solution.py:435
  55.3 0.0 copy-done.3
  55.3 0.8 %image.1 = f32[4,512]{1,0:T(4,128)} custom-call(bf16[8,32,512]{2,1,0:T(8,128)(2,1)S(1)} %copy-done.3, bf16[512,128]{1,0:T(8,128)(2,1)S(1)} %bitcast.7), custom_call_target="tpu_custom_call" | custom-call | tf_op jit(solution)/shard_map/image/pallas_call | solution.py:438
  (4 shorter events, 0.0 us)
Async XLA Ops:
  0.0 11.8 %copy-start.4 = (f32[2,128,128]{2,1,0:T(8,128)S(1)}, f32[2,128,128]{2,1,0:T(8,128)}, u32[]{:S(2)}) copy-start(f32[2,128,128]{2,1,0:T(8,128)} %constant.29.clone.refs_5_) | copy-start | bytes 393220
  0.0 11.8 %copy-start.5 = (bf16[128,256]{1,0:T(8,128)(2,1)S(1)}, bf16[128,256]{1,0:T(8,128)(2,1)}, u32[]{:S(2)}) copy-start(bf16[128,256]{1,0:T(8,128)(2,1)} %constant.30.clone.refs_6_) | copy-start | bytes 196612
  0.0 11.8 %copy-start.6 = (bf16[256,64]{1,0:T(8,128)(2,1)S(1)}, bf16[256,64]{1,0:T(8,128)(2,1)}, u32[]{:S(2)}) copy-start(bf16[256,64]{1,0:T(8,128)(2,1)} %constant.28.clone.refs_4_) | copy-start | bytes 98308
  1.0 8.0 %collective-permute-start.2 = (bf16[16,2048]{1,0:T(8,128)(2,1)S(1)}, bf16[16,2048]{1,0:T(8,128)(2,1)S(1)}, u32[]{:S(2)}, u32[]{:S(2)}) collective-permute-start(bf16[16,2048]{1,0:T(8,128)(2,1)S(1)} %get-tuple-element.15), channel_id=1, source_target_pairs={{0,3},{1,2},{2,1},{3,0},{4,7},{5,6},{6,5},{7,4},{8,11},{9,10},{10,... | collective-permute-start | bytes 196616 | tf_op jit(solution)/shard_map/ppermute | solution.py:374
  6.1 4.7 %collective-permute-start = (bf16[16,2048]{1,0:T(8,128)(2,1)S(1)}, bf16[16,2048]{1,0:T(8,128)(2,1)S(1)}, u32[]{:S(2)}, u32[]{:S(2)}) collective-permute-start(bf16[16,2048]{1,0:T(8,128)(2,1)S(1)} %get-tuple-element.16), channel_id=1, source_target_pairs={{0,1},{1,0},{2,3},{3,2},{4,5},{5,4},{6,7},{7,6},{8,9},{9,8},{10,11... | collective-permute-start | bytes 196616 | tf_op jit(solution)/shard_map/ppermute | solution.py:374
  6.1 5.6 %collective-permute-start.1 = (bf16[16,2048]{1,0:T(8,128)(2,1)S(1)}, bf16[16,2048]{1,0:T(8,128)(2,1)S(1)}, u32[]{:S(2)}, u32[]{:S(2)}) collective-permute-start(bf16[16,2048]{1,0:T(8,128)(2,1)S(1)} %get-tuple-element.18), channel_id=1, source_target_pairs={{0,2},{1,3},{2,0},{3,1},{4,6},{5,7},{6,4},{7,5},{8,10},{9,11},{10,... | collective-permute-start | bytes 196616 | tf_op jit(solution)/shard_map/ppermute | solution.py:374
  11.8 7.3 %copy-start.8 = (s32[4,64]{1,0:T(4,128)S(1)}, s32[4,64]{1,0:T(4,128)}, u32[]{:S(2)}) copy-start(s32[4,64]{1,0:T(4,128)} %param.15) | copy-start | bytes 3076
  11.8 7.3 %copy-start.7 = (s32[64,512]{1,0:T(8,128)S(1)}, s32[64,512]{1,0:T(8,128)}, u32[]{:S(2)}) copy-start(s32[64,512]{1,0:T(8,128)} %param.13) | copy-start | bytes 393220
  14.6 4.5 %copy-start.9 = (s32[4,64]{1,0:T(4,128)S(1)}, s32[4,64]{1,0:T(4,128)}, u32[]{:S(2)}) copy-start(s32[4,64]{1,0:T(4,128)} %param.16) | copy-start | bytes 3076
  14.6 16.2 %copy-start.1 = (bf16[64,2,1024]{2,1,0:T(2,128)(2,1)S(1)}, bf16[64,2,1024]{2,1,0:T(2,128)(2,1)}, u32[]{:S(2)}) copy-start(bf16[64,2,1024]{2,1,0:T(2,128)(2,1)} %refs_5_.2) | copy-start | bytes 786436
  14.6 16.2 %copy-start.2 = (f32[256,256]{1,0:T(8,128)S(1)}, f32[256,256]{1,0:T(8,128)}, u32[]{:S(2)}) copy-start(f32[256,256]{1,0:T(8,128)} %constant.31.clone.refs_8_) | copy-start | bytes 786436
  14.6 14.6 %all-to-all-start = ((bf16[32,16,256]{2,1,0:T(8,128)(2,1)}), bf16[32,16,256]{2,1,0:T(8,128)(2,1)S(1)}, u32[]{:S(2)}, u32[]{:S(2)}) async-start(bf16[32,16,256]{2,1,0:T(8,128)(2,1)} %bitcast), calls=%async_computation | async-start | bytes 524288 | tf_op jit(solution)/shard_map/all_to_all | solution.py:414
  19.1 11.8 %copy-start = (bf16[64,2,1024]{2,1,0:T(2,128)(2,1)S(1)}, bf16[64,2,1024]{2,1,0:T(2,128)(2,1)}, u32[]{:S(2)}) copy-start(bf16[64,2,1024]{2,1,0:T(2,128)(2,1)} %refs_4_.2) | copy-start | bytes 786436
  19.2 7.8 %collective-permute-start.5 = (bf16[80,512]{1,0:T(8,128)(2,1)S(1)}, bf16[80,512]{1,0:T(8,128)(2,1)S(1)}, u32[]{:S(2)}, u32[]{:S(2)}) collective-permute-start(bf16[80,512]{1,0:T(8,128)(2,1)S(1)} %fusion.4.refs_0_), channel_id=1, source_target_pairs={{0,24},{4,28},{8,16},{12,20},{16,8},{20,12},{24,0},{28,4},{1,25},{... | collective-permute-start | bytes 245768 | tf_op jit(solution)/shard_map/ppermute | solution.py:374
  21.9 6.7 %collective-permute-start.4 = (bf16[80,512]{1,0:T(8,128)(2,1)S(1)}, bf16[80,512]{1,0:T(8,128)(2,1)S(1)}, u32[]{:S(2)}, u32[]{:S(2)}) collective-permute-start(bf16[80,512]{1,0:T(8,128)(2,1)S(1)} %fusion.4.refs_0_), channel_id=1, source_target_pairs={{0,16},{4,20},{8,24},{12,28},{16,0},{20,4},{24,8},{28,12},{1,17},{... | collective-permute-start | bytes 245768 | tf_op jit(solution)/shard_map/ppermute | solution.py:374
  22.5 6.1 %collective-permute-start.3 = (bf16[80,512]{1,0:T(8,128)(2,1)S(1)}, bf16[80,512]{1,0:T(8,128)(2,1)S(1)}, u32[]{:S(2)}, u32[]{:S(2)}) collective-permute-start(bf16[80,512]{1,0:T(8,128)(2,1)S(1)} %fusion.4.refs_0_), channel_id=1, source_target_pairs={{0,8},{4,12},{8,0},{12,4},{16,24},{20,28},{24,16},{28,20},{1,9},{5... | collective-permute-start | bytes 245768 | tf_op jit(solution)/shard_map/ppermute | solution.py:374
  29.3 1.6 %collective-permute-start.6 = (bf16[512,256]{1,0:T(8,128)(2,1)S(1)}, bf16[512,256]{1,0:T(8,128)(2,1)S(1)}, u32[]{:S(2)}, u32[]{:S(2)}) collective-permute-start(bf16[512,256]{1,0:T(8,128)(2,1)S(1)} %bitcast.4), channel_id=1, source_target_pairs={{0,4},{4,0},{8,12},{12,8},{16,20},{20,16},{24,28},{28,24},{1,5},{5... | collective-permute-start | bytes 786440 | tf_op jit(solution)/shard_map/ppermute | solution.py:374
  43.4 11.9 %copy-start.3 = (bf16[8,32,512]{2,1,0:T(8,128)(2,1)S(1)}, bf16[8,32,512]{2,1,0:T(8,128)(2,1)}, u32[]{:S(2)}) copy-start(bf16[8,32,512]{2,1,0:T(8,128)(2,1)} %constant.32.clone.high_ref) | copy-start | bytes 786436

commit v5 on v4

--- a/solution.py
+++ b/solution.py
@@ -237,9 +237,9 @@
 def adjoint_kernel(panels, slots, n_src, chunk, *refs):
     packs = refs[:panels]
     observed_ref, green_ref, spectra_ref, other_ref, low_ref, out_ref = refs[panels : panels + 6]
-    spectra, classes, numbers, bank, green, mixed, total = refs[panels + 6 :]
+    spectra, numbers, bank, green, mixed, total = refs[panels + 6 :]
     stations = spectra_ref.shape[0]
-    panel = classes.shape[0] // panels
+    panel = mixed.shape[0] // panels
     class_count = bank.shape[0]
     tiles = total.shape[0]
     blk_index = lax.axis_index("blk")
@@ -247,12 +247,12 @@
         at = pl.ds(pl.multiple_of((blk_index ^ other) * LANES, LANES), LANES)
         lanes = slice(2 * other * LANES, 2 * (other + 1) * LANES)
         pair = observed_ref[:, :, at].astype(jnp.float32)
-        bank[:, lanes] = jnp.concatenate([pair[:, 0, :], pair[:, 1, :]], axis=1)
+        pair = jnp.concatenate([pair[:, 0, :], pair[:, 1, :]], axis=1)
+        bank[:, :, lanes] = jnp.broadcast_to(pair[:, None, :], (class_count, 8, 2 * LANES))
         pair = green_ref[:, :, at].astype(jnp.float32)
         pair = jnp.concatenate([pair[:, 0, :], pair[:, 1, :]], axis=1)
         green[:, lanes] = pair.astype(jnp.bfloat16)
     for k, pack in enumerate(packs):
-        classes[k * panel : (k + 1) * panel, :] = pack[:panel].astype(jnp.float32)
         ids = pack[panel : panel + 16, :LANES].astype(jnp.int32)
         for row in range(2):
             numbers[k, row : row + 1] = jnp.concatenate(
@@ -269,37 +269,29 @@
     power = jnp.concatenate(power, axis=1)
     green_ids = lax.broadcasted_iota(jnp.int32, (green.shape[0], slots * panel), 0)
     tile_ids = lax.broadcasted_iota(jnp.int32, (tiles, slots * panel), 0)
-    class_ids = lax.broadcasted_iota(jnp.int32, (class_count, stations), 0).astype(jnp.float32)
-    class_ids = class_ids.astype(jnp.bfloat16).reshape(1, class_count // 16, 16, stations)
+    class_ids = lax.broadcasted_iota(jnp.int32, (class_count, chunk, stations), 0)
+    class_ids = class_ids.astype(jnp.float32).astype(jnp.bfloat16)
     total[...] = jnp.zeros_like(total)
 
     def mix(place):
-        start = pl.multiple_of(place * panel, panel)
-        places = [pl.ds(start + part * chunk, chunk) for part in range(panel // chunk)]
-
-        def one_hot(at):
-            wide = jnp.broadcast_to(classes[at, :][:, None, :], (chunk, 16, stations))
-            wide = wide.astype(jnp.bfloat16)[:, None]
-            hot = jnp.where(wide == class_ids, jnp.bfloat16(1.0), jnp.bfloat16(0.0))
-            return hot.reshape(chunk * class_count, stations)
-
-        def reduce(at, grouped):
-            grouped = grouped.reshape(chunk, class_count, 4 * LANES)
+        for start in range(0, panel, chunk):
+            rows = packs[place][start : start + chunk]
+            hot = jnp.where(rows[None] == class_ids, jnp.bfloat16(1.0), jnp.bfloat16(0.0))
+            grouped = jnp.dot(
+                hot.reshape(class_count * chunk, stations),
+                spectra[...],
+                preferred_element_type=jnp.float32,
+            ).reshape(class_count, chunk // 8, 8, 4 * LANES)
+            at = slice(place * panel + start, place * panel + start + chunk)
             for real, imag in (lanes[:2], lanes[2:]):
-                obs_real, obs_imag = bank[:, real][None], bank[:, imag][None]
+                obs_real, obs_imag = bank[:, :, real][:, None], bank[:, :, imag][:, None]
                 group_real, group_imag = grouped[..., real], grouped[..., imag]
-                mixed[at, real] = jnp.sum(obs_real * group_real - obs_imag * group_imag, axis=1)
-                mixed[at, imag] = jnp.sum(obs_real * group_imag + obs_imag * group_real, axis=1)
-
-        hot, before = one_hot(places[0]), None
-        for part, at in enumerate(places):
-            grouped = jnp.dot(hot, spectra[...], preferred_element_type=jnp.float32)
-            if part + 1 < len(places):
-                hot = one_hot(places[part + 1])
-            if before is not None:
-                reduce(*before)
-            before = (at, grouped)
-        reduce(*before)
+                mixed[at, real] = jnp.sum(
+                    obs_real * group_real - obs_imag * group_imag, axis=0
+                ).reshape(chunk, LANES)
+                mixed[at, imag] = jnp.sum(
+                    obs_real * group_imag + obs_imag * group_real, axis=0
+                ).reshape(chunk, LANES)
 
     def gather(place):
         at = pl.ds(pl.multiple_of(place * panel, panel), panel)
@@ -422,9 +414,8 @@
         out_shape=jax.ShapeDtypeStruct((16 * devices, 2 * TILE_SIDE), PARTS_TYPE),
         scratch_shapes=[
             pltpu.VMEM((stations, 4 * LANES), jnp.bfloat16),
-            pltpu.VMEM((panels * panel, stations), jnp.float32),
             pltpu.VMEM((panels, 8, slots * panel), jnp.int32),
-            pltpu.VMEM((class_count, 4 * LANES), jnp.float32),
+            pltpu.VMEM((class_count, 8, 4 * LANES), jnp.float32),
             pltpu.VMEM((green.shape[0], 4 * LANES), jnp.bfloat16),
             pltpu.VMEM((panels * panel, 4 * LANES), jnp.float32),
             pltpu.VMEM((tiles, 4 * LANES), jnp.float32),

time: 56.4 us -> 54.9 us (0.973)
  Pallas kernels: 16.2 us -> 14.7 us
    pallas_call x1, Pallas kernels: 12.5 us -> 11.1 us  [split_body(): pl.pallas_call(functools.partial(adjoint_kernel, panels, slots, n_src, 16...]
where the time goes in v5:
time: 54.9 us; the launch traced here: 54.6 us
  Pallas kernels  14.7 us (27%)
  starting transfers between devices  14.1 us (26%)
  waiting for transfers between devices  12.7 us (23%)
  blocking collectives  11.9 us (22%)
  local copies, waits for them, and re-layouts  1.04 us (2%)
    ppermute x7, waiting for transfers between devices, swap(): return lax.ppermute(values, axis, [(i, i ^ distance) for i in range(size)])  12 us
    all_to_all x1, blocking collectives, split_body(): lax.all_to_all(parts.reshape(devices, 16, 2 * TILE_SIDE), BOTH, 0, 0, til...  11.9 us
    pallas_call x1, Pallas kernels, split_body(): pl.pallas_call(functools.partial(adjoint_kernel, panels, slots, n_src, 16...  11.1 us
    ppermute x7, starting transfers between devices, swap(): return lax.ppermute(values, axis, [(i, i ^ distance) for i in range(size)])  9.72 us
    all_to_all x1, starting transfers between devices, split_body(): lax.all_to_all(blocks.reshape(devices, share, 2 * LANES), BOTH, 0, 0, til...  4.42 us
    pallas_call x1, Pallas kernels, split_body(): pl.pallas_call(functools.partial(spectra_kernel, n_src), out_shape=jax.Sh...  2.83 us
  transfers between devices with their start and end apart: 8, of which 7 were waited for; matrix products, arithmetic and copies ran while one was open for 0% of the time, Pallas kernels for 0%

profile of v5, /device:TPU:0, one launch (start us, length us, event | category | flops | bytes accessed | tf_op | source)
XLA Modules:
  0.0 54.6 jit_solution(11696562117062821250)
XLA Ops:
  0.0 0.0 copy-start.4
  0.0 0.0 copy-start.5
  0.0 0.0 copy-start.6
  0.0 1.0 %constant_dynamic-slice_fusion = (bf16[16,2048]{1,0:T(8,128)(2,1)S(1)}, bf16[16,2048]{1,0:T(8,128)(2,1)S(1)}, bf16[16,2048]{1,0:T(8,128)(2,1)S(1)}, bf16[16,2048]{1,0:T(8,128)(2,1)S(1)}) fusion(bf16[64,2048]{1,0:T(8,128)(2,1)} %param.11, s32[]{:T(128)S(6)} %select_n.15, s32[]{:T(128)S(6)} %select_n.13, s32[]{:T(128)S(6)} %select_n.12, s32[]{:T(128)S(6)} %select_n.14), kind=kLoop, calls=%fused_computation.8 | loop fusion | bytes 524304 | tf_op jit(solution)/shard_map/dynamic_slice | solution.py:378
  1.0 5.1 %collective-permute-start.2 = (bf16[16,2048]{1,0:T(8,128)(2,1)S(1)}, bf16[16,2048]{1,0:T(8,128)(2,1)S(1)}, u32[]{:S(2)}, u32[]{:S(2)}) collective-permute-start(bf16[16,2048]{1,0:T(8,128)(2,1)S(1)} %get-tuple-element.15), channel_id=1, source_target_pairs={{0,3},{1,2},{2,1},{3,0},{4,7},{5,6},{6,5},{7,4},{8,11},{9,10},{10,... | collective-permute-start | bytes 196616 | tf_op jit(solution)/shard_map/ppermute | solution.py:366
  6.1 0.0 collective-permute-start
  6.1 0.6 %collective-permute-start.1 = (bf16[16,2048]{1,0:T(8,128)(2,1)S(1)}, bf16[16,2048]{1,0:T(8,128)(2,1)S(1)}, u32[]{:S(2)}, u32[]{:S(2)}) collective-permute-start(bf16[16,2048]{1,0:T(8,128)(2,1)S(1)} %get-tuple-element.18), channel_id=1, source_target_pairs={{0,2},{1,3},{2,0},{3,1},{4,6},{5,7},{6,4},{7,5},{8,10},{9,11},{10,... | collective-permute-start | bytes 196616 | tf_op jit(solution)/shard_map/ppermute | solution.py:366
  6.8 2.3 %collective-permute-done.2.refs_3_ = bf16[16,2048]{1,0:T(8,128)(2,1)S(1)} collective-permute-done((bf16[16,2048]{1,0:T(8,128)(2,1)S(1)}, bf16[16,2048]{1,0:T(8,128)(2,1)S(1)}, u32[]{:S(2)}, u32[]{:S(2)}) %collective-permute-start.2) | collective-permute-done | bytes 65568 | tf_op jit(solution)/shard_map/ppermute | solution.py:366
  9.0 1.8 %collective-permute-done.refs_1_ = bf16[16,2048]{1,0:T(8,128)(2,1)S(1)} collective-permute-done((bf16[16,2048]{1,0:T(8,128)(2,1)S(1)}, bf16[16,2048]{1,0:T(8,128)(2,1)S(1)}, u32[]{:S(2)}, u32[]{:S(2)}) %collective-permute-start) | collective-permute-done | bytes 65568 | tf_op jit(solution)/shard_map/ppermute | solution.py:366
  10.8 1.0 %collective-permute-done.1.refs_2_ = bf16[16,2048]{1,0:T(8,128)(2,1)S(1)} collective-permute-done((bf16[16,2048]{1,0:T(8,128)(2,1)S(1)}, bf16[16,2048]{1,0:T(8,128)(2,1)S(1)}, u32[]{:S(2)}, u32[]{:S(2)}) %collective-permute-start.1) | collective-permute-done | bytes 65568 | tf_op jit(solution)/shard_map/ppermute | solution.py:366
  11.8 0.0 copy-done.4
  11.8 0.0 copy-done.5
  11.8 0.0 copy-done.6
  11.8 0.0 copy-start.8
  11.8 0.0 copy-start.7
  11.8 2.8 %spectra.1 = bf16[512,256]{1,0:T(8,128)(2,1)} custom-call(bf16[16,2048]{1,0:T(8,128)(2,1)S(1)} %get-tuple-element.17.refs_0_, bf16[16,2048]{1,0:T(8,128)(2,1)S(1)} %collective-permute-done.refs_1_, bf16[16,2048]{1,0:T(8,128)(2,1)S(1)} %collective-permute-done.1.refs_2_, bf16[16,2048]{1,0:T(8,128)(2,1)S(1)} %collective-permute-done.2.refs_3_, ...), custom_call_target="tpu_custom_call" | custom-call | tf_op jit(solution)/shard_map/spectra/pallas_call | solution.py:395
  14.6 0.0 copy-start.9
  14.6 0.0 copy-start.1
  14.6 0.0 copy-start.2
  14.6 4.4 %all-to-all-start = ((bf16[32,16,256]{2,1,0:T(8,128)(2,1)}), bf16[32,16,256]{2,1,0:T(8,128)(2,1)S(1)}, u32[]{:S(2)}, u32[]{:S(2)}) async-start(bf16[32,16,256]{2,1,0:T(8,128)(2,1)} %bitcast), calls=%async_computation | async-start | bytes 524288 | tf_op jit(solution)/shard_map/all_to_all | solution.py:406
  19.1 0.0 copy-done.8
  19.1 0.0 copy-start
  19.1 0.0 copy-done.9
  19.1 0.0 copy-done.7
  19.2 2.7 %collective-permute-start.5 = (bf16[80,512]{1,0:T(8,128)(2,1)S(1)}, bf16[80,512]{1,0:T(8,128)(2,1)S(1)}, u32[]{:S(2)}, u32[]{:S(2)}) collective-permute-start(bf16[80,512]{1,0:T(8,128)(2,1)S(1)} %fusion.4.refs_0_), channel_id=1, source_target_pairs={{0,24},{4,28},{8,16},{12,20},{16,8},{20,12},{24,0},{28,4},{1,25},{... | collective-permute-start | bytes 245768 | tf_op jit(solution)/shard_map/ppermute | solution.py:366
  21.9 0.6 %collective-permute-start.4 = (bf16[80,512]{1,0:T(8,128)(2,1)S(1)}, bf16[80,512]{1,0:T(8,128)(2,1)S(1)}, u32[]{:S(2)}, u32[]{:S(2)}) collective-permute-start(bf16[80,512]{1,0:T(8,128)(2,1)S(1)} %fusion.4.refs_0_), channel_id=1, source_target_pairs={{0,16},{4,20},{8,24},{12,28},{16,0},{20,4},{24,8},{28,12},{1,17},{... | collective-permute-start | bytes 245768 | tf_op jit(solution)/shard_map/ppermute | solution.py:366
  22.5 0.3 collective-permute-start.3
  22.7 4.3 %collective-permute-done.5.refs_3_ = bf16[80,512]{1,0:T(8,128)(2,1)S(1)} collective-permute-done((bf16[80,512]{1,0:T(8,128)(2,1)S(1)}, bf16[80,512]{1,0:T(8,128)(2,1)S(1)}, u32[]{:S(2)}, u32[]{:S(2)}) %collective-permute-start.5) | collective-permute-done | bytes 81952 | tf_op jit(solution)/shard_map/ppermute | solution.py:366
  27.0 1.6 %collective-permute-done.4.refs_2_ = bf16[80,512]{1,0:T(8,128)(2,1)S(1)} collective-permute-done((bf16[80,512]{1,0:T(8,128)(2,1)S(1)}, bf16[80,512]{1,0:T(8,128)(2,1)S(1)}, u32[]{:S(2)}, u32[]{:S(2)}) %collective-permute-start.4) | collective-permute-done | bytes 81952 | tf_op jit(solution)/shard_map/ppermute | solution.py:366
  28.6 0.0 collective-permute-done.3.refs_1_
  28.6 0.7 %all-to-all-done = bf16[32,16,256]{2,1,0:T(8,128)(2,1)S(1)} async-done(((bf16[32,16,256]{2,1,0:T(8,128)(2,1)}), bf16[32,16,256]{2,1,0:T(8,128)(2,1)S(1)}, u32[]{:S(2)}, u32[]{:S(2)}) %all-to-all-start) | async-done | bytes 262176 | tf_op jit(solution)/shard_map/all_to_all | solution.py:406
  29.3 0.4 collective-permute-start.6
  29.7 1.2 %collective-permute-done.6.refs_7_ = bf16[512,256]{1,0:T(8,128)(2,1)S(1)} collective-permute-done((bf16[512,256]{1,0:T(8,128)(2,1)S(1)}, bf16[512,256]{1,0:T(8,128)(2,1)S(1)}, u32[]{:S(2)}, u32[]{:S(2)}) %collective-permute-start.6) | collective-permute-done | bytes 262176 | tf_op jit(solution)/shard_map/ppermute | solution.py:366
  30.8 0.0 copy-done.1
  30.8 0.0 copy-done.2
  30.8 0.0 copy-done
  30.8 11.1 %adjoint.1 = bf16[512,128]{1,0:T(8,128)(2,1)S(1)} custom-call(bf16[80,512]{1,0:T(8,128)(2,1)S(1)} %fusion.4.refs_0_, bf16[80,512]{1,0:T(8,128)(2,1)S(1)} %collective-permute-done.3.refs_1_, bf16[80,512]{1,0:T(8,128)(2,1)S(1)} %collective-permute-done.4.refs_2_, bf16[80,512]{1,0:T(8,128)(2,1)S(1)} %collective-permute-done.5.refs_3_, ...), custom_call_target="tpu_custom_call" | custom-call | tf_op jit(solution)/shard_map/adjoint/pallas_call | solution.py:412
  41.9 0.0 copy-start.3
  41.9 11.9 %all_to_all.10 = bf16[32,16,128]{2,1,0:T(8,128)(2,1)S(1)} all-to-all(bf16[32,16,128]{2,1,0:T(8,128)(2,1)S(1)} %bitcast.6), channel_id=1, replica_groups=mesh['blk'=8,'src'=4] {'blk','src'}, dimensions={0} | all-to-all | bytes 262144 | tf_op jit(solution)/shard_map/all_to_all | solution.py:426
  53.8 0.0 copy-done.3
  53.8 0.8 %image.1 = f32[4,512]{1,0:T(4,128)} custom-call(bf16[8,32,512]{2,1,0:T(8,128)(2,1)S(1)} %copy-done.3, bf16[512,128]{1,0:T(8,128)(2,1)S(1)} %bitcast.7), custom_call_target="tpu_custom_call" | custom-call | tf_op jit(solution)/shard_map/image/pallas_call | solution.py:429
  (4 shorter events, 0.0 us)
Async XLA Ops:
  0.0 11.8 %copy-start.4 = (f32[2,128,128]{2,1,0:T(8,128)S(1)}, f32[2,128,128]{2,1,0:T(8,128)}, u32[]{:S(2)}) copy-start(f32[2,128,128]{2,1,0:T(8,128)} %constant.29.clone.refs_5_) | copy-start | bytes 393220
  0.0 11.8 %copy-start.5 = (bf16[128,256]{1,0:T(8,128)(2,1)S(1)}, bf16[128,256]{1,0:T(8,128)(2,1)}, u32[]{:S(2)}) copy-start(bf16[128,256]{1,0:T(8,128)(2,1)} %constant.30.clone.refs_6_) | copy-start | bytes 196612
  0.0 11.8 %copy-start.6 = (bf16[256,64]{1,0:T(8,128)(2,1)S(1)}, bf16[256,64]{1,0:T(8,128)(2,1)}, u32[]{:S(2)}) copy-start(bf16[256,64]{1,0:T(8,128)(2,1)} %constant.28.clone.refs_4_) | copy-start | bytes 98308
  1.0 8.0 %collective-permute-start.2 = (bf16[16,2048]{1,0:T(8,128)(2,1)S(1)}, bf16[16,2048]{1,0:T(8,128)(2,1)S(1)}, u32[]{:S(2)}, u32[]{:S(2)}) collective-permute-start(bf16[16,2048]{1,0:T(8,128)(2,1)S(1)} %get-tuple-element.15), channel_id=1, source_target_pairs={{0,3},{1,2},{2,1},{3,0},{4,7},{5,6},{6,5},{7,4},{8,11},{9,10},{10,... | collective-permute-start | bytes 196616 | tf_op jit(solution)/shard_map/ppermute | solution.py:366
  6.1 4.7 %collective-permute-start = (bf16[16,2048]{1,0:T(8,128)(2,1)S(1)}, bf16[16,2048]{1,0:T(8,128)(2,1)S(1)}, u32[]{:S(2)}, u32[]{:S(2)}) collective-permute-start(bf16[16,2048]{1,0:T(8,128)(2,1)S(1)} %get-tuple-element.16), channel_id=1, source_target_pairs={{0,1},{1,0},{2,3},{3,2},{4,5},{5,4},{6,7},{7,6},{8,9},{9,8},{10,11... | collective-permute-start | bytes 196616 | tf_op jit(solution)/shard_map/ppermute | solution.py:366
  6.1 5.6 %collective-permute-start.1 = (bf16[16,2048]{1,0:T(8,128)(2,1)S(1)}, bf16[16,2048]{1,0:T(8,128)(2,1)S(1)}, u32[]{:S(2)}, u32[]{:S(2)}) collective-permute-start(bf16[16,2048]{1,0:T(8,128)(2,1)S(1)} %get-tuple-element.18), channel_id=1, source_target_pairs={{0,2},{1,3},{2,0},{3,1},{4,6},{5,7},{6,4},{7,5},{8,10},{9,11},{10,... | collective-permute-start | bytes 196616 | tf_op jit(solution)/shard_map/ppermute | solution.py:366
  11.8 7.3 %copy-start.8 = (s32[4,64]{1,0:T(4,128)S(1)}, s32[4,64]{1,0:T(4,128)}, u32[]{:S(2)}) copy-start(s32[4,64]{1,0:T(4,128)} %param.15) | copy-start | bytes 3076
  11.8 7.3 %copy-start.7 = (s32[64,512]{1,0:T(8,128)S(1)}, s32[64,512]{1,0:T(8,128)}, u32[]{:S(2)}) copy-start(s32[64,512]{1,0:T(8,128)} %param.13) | copy-start | bytes 393220
  14.6 4.5 %copy-start.9 = (s32[4,64]{1,0:T(4,128)S(1)}, s32[4,64]{1,0:T(4,128)}, u32[]{:S(2)}) copy-start(s32[4,64]{1,0:T(4,128)} %param.16) | copy-start | bytes 3076
  14.6 16.2 %copy-start.1 = (bf16[64,2,1024]{2,1,0:T(2,128)(2,1)S(1)}, bf16[64,2,1024]{2,1,0:T(2,128)(2,1)}, u32[]{:S(2)}) copy-start(bf16[64,2,1024]{2,1,0:T(2,128)(2,1)} %refs_5_.2) | copy-start | bytes 786436
  14.6 16.2 %copy-start.2 = (f32[256,256]{1,0:T(8,128)S(1)}, f32[256,256]{1,0:T(8,128)}, u32[]{:S(2)}) copy-start(f32[256,256]{1,0:T(8,128)} %constant.31.clone.refs_8_) | copy-start | bytes 786436
  14.6 14.6 %all-to-all-start = ((bf16[32,16,256]{2,1,0:T(8,128)(2,1)}), bf16[32,16,256]{2,1,0:T(8,128)(2,1)S(1)}, u32[]{:S(2)}, u32[]{:S(2)}) async-start(bf16[32,16,256]{2,1,0:T(8,128)(2,1)} %bitcast), calls=%async_computation | async-start | bytes 524288 | tf_op jit(solution)/shard_map/all_to_all | solution.py:406
  19.1 11.8 %copy-start = (bf16[64,2,1024]{2,1,0:T(2,128)(2,1)S(1)}, bf16[64,2,1024]{2,1,0:T(2,128)(2,1)}, u32[]{:S(2)}) copy-start(bf16[64,2,1024]{2,1,0:T(2,128)(2,1)} %refs_4_.2) | copy-start | bytes 786436
  19.2 7.8 %collective-permute-start.5 = (bf16[80,512]{1,0:T(8,128)(2,1)S(1)}, bf16[80,512]{1,0:T(8,128)(2,1)S(1)}, u32[]{:S(2)}, u32[]{:S(2)}) collective-permute-start(bf16[80,512]{1,0:T(8,128)(2,1)S(1)} %fusion.4.refs_0_), channel_id=1, source_target_pairs={{0,24},{4,28},{8,16},{12,20},{16,8},{20,12},{24,0},{28,4},{1,25},{... | collective-permute-start | bytes 245768 | tf_op jit(solution)/shard_map/ppermute | solution.py:366
  21.9 6.7 %collective-permute-start.4 = (bf16[80,512]{1,0:T(8,128)(2,1)S(1)}, bf16[80,512]{1,0:T(8,128)(2,1)S(1)}, u32[]{:S(2)}, u32[]{:S(2)}) collective-permute-start(bf16[80,512]{1,0:T(8,128)(2,1)S(1)} %fusion.4.refs_0_), channel_id=1, source_target_pairs={{0,16},{4,20},{8,24},{12,28},{16,0},{20,4},{24,8},{28,12},{1,17},{... | collective-permute-start | bytes 245768 | tf_op jit(solution)/shard_map/ppermute | solution.py:366
  22.5 6.1 %collective-permute-start.3 = (bf16[80,512]{1,0:T(8,128)(2,1)S(1)}, bf16[80,512]{1,0:T(8,128)(2,1)S(1)}, u32[]{:S(2)}, u32[]{:S(2)}) collective-permute-start(bf16[80,512]{1,0:T(8,128)(2,1)S(1)} %fusion.4.refs_0_), channel_id=1, source_target_pairs={{0,8},{4,12},{8,0},{12,4},{16,24},{20,28},{24,16},{28,20},{1,9},{5... | collective-permute-start | bytes 245768 | tf_op jit(solution)/shard_map/ppermute | solution.py:366
  29.3 1.6 %collective-permute-start.6 = (bf16[512,256]{1,0:T(8,128)(2,1)S(1)}, bf16[512,256]{1,0:T(8,128)(2,1)S(1)}, u32[]{:S(2)}, u32[]{:S(2)}) collective-permute-start(bf16[512,256]{1,0:T(8,128)(2,1)S(1)} %bitcast.4), channel_id=1, source_target_pairs={{0,4},{4,0},{8,12},{12,8},{16,20},{20,16},{24,28},{28,24},{1,5},{5... | collective-permute-start | bytes 786440 | tf_op jit(solution)/shard_map/ppermute | solution.py:366
  41.9 11.9 %copy-start.3 = (bf16[8,32,512]{2,1,0:T(8,128)(2,1)S(1)}, bf16[8,32,512]{2,1,0:T(8,128)(2,1)}, u32[]{:S(2)}) copy-start(bf16[8,32,512]{2,1,0:T(8,128)(2,1)} %constant.32.clone.high_ref) | copy-start | bytes 786436

commit v6 on v5

--- a/solution.py
+++ b/solution.py
@@ -234,30 +234,49 @@
     out_ref[:, LANES:] = imags[...].astype(jnp.bfloat16)
 
 
+def bank_kernel(observed_ref, green_ref, bank_ref, bank_green_ref):
+    for other in range(2):
+        at = pl.ds(pl.multiple_of((lax.axis_index("blk") ^ other) * LANES, LANES), LANES)
+        lanes = slice(2 * other * LANES, 2 * (other + 1) * LANES)
+        pair = observed_ref[:, :, at].astype(jnp.float32)
+        pair = jnp.concatenate([pair[:, 0, :], pair[:, 1, :]], axis=1)
+        bank_ref[:, :, lanes] = jnp.broadcast_to(
+            pair[:, None, :], (pair.shape[0], 8, 2 * LANES)
+        )
+        pair = green_ref[:, :, at].astype(jnp.float32)
+        pair = jnp.concatenate([pair[:, 0, :], pair[:, 1, :]], axis=1)
+        bank_green_ref[:, lanes] = pair.astype(jnp.bfloat16)
+
+
+def pick_kernel(slots, *refs):
+    *packs, green_ref, picked_ref, tile_ref = refs
+    panel = picked_ref.shape[1] // slots
+    green_ids = lax.broadcasted_iota(jnp.int32, (green_ref.shape[0], slots * panel), 0)
+    tile_ids = lax.broadcasted_iota(jnp.int32, (tile_ref.shape[1], slots * panel), 0)
+    for k, pack in enumerate(packs):
+        ids = pack[panel : panel + 16, :LANES].astype(jnp.int32)
+        picks, seats = (
+            jnp.concatenate([ids[row + slot : row + slot + 1, :panel] for slot in range(slots)], axis=1)
+            for row in (0, 8)
+        )
+        picked_ref[k] = lax.dot_general(
+            jnp.where(picks == green_ids, 1.0, 0.0).astype(jnp.bfloat16),
+            green_ref[...],
+            TN_DIMS,
+            preferred_element_type=jnp.float32,
+        ).astype(jnp.bfloat16)
+        tile_ref[k] = jnp.where(seats == tile_ids, 1.0, 0.0).astype(jnp.bfloat16)
+
+
 def adjoint_kernel(panels, slots, n_src, chunk, *refs):
     packs = refs[:panels]
-    observed_ref, green_ref, spectra_ref, other_ref, low_ref, out_ref = refs[panels : panels + 6]
-    spectra, numbers, bank, green, mixed, total = refs[panels + 6 :]
+    picked_ref, tile_ref, bank, spectra_ref, other_ref, low_ref, out_ref = refs[panels : panels + 7]
+    spectra, mixed, total = refs[panels + 7 :]
     stations = spectra_ref.shape[0]
     panel = mixed.shape[0] // panels
     class_count = bank.shape[0]
     tiles = total.shape[0]
     blk_index = lax.axis_index("blk")
-    for other in range(2):
-        at = pl.ds(pl.multiple_of((blk_index ^ other) * LANES, LANES), LANES)
-        lanes = slice(2 * other * LANES, 2 * (other + 1) * LANES)
-        pair = observed_ref[:, :, at].astype(jnp.float32)
-        pair = jnp.concatenate([pair[:, 0, :], pair[:, 1, :]], axis=1)
-        bank[:, :, lanes] = jnp.broadcast_to(pair[:, None, :], (class_count, 8, 2 * LANES))
-        pair = green_ref[:, :, at].astype(jnp.float32)
-        pair = jnp.concatenate([pair[:, 0, :], pair[:, 1, :]], axis=1)
-        green[:, lanes] = pair.astype(jnp.bfloat16)
-    for k, pack in enumerate(packs):
-        ids = pack[panel : panel + 16, :LANES].astype(jnp.int32)
-        for row in range(2):
-            numbers[k, row : row + 1] = jnp.concatenate(
-                [ids[8 * row + slot : 8 * row + slot + 1, :panel] for slot in range(slots)], axis=1
-            )
     spectra[:, : 2 * LANES] = spectra_ref[...]
     spectra[:, 2 * LANES :] = other_ref[...]
     widened = spectra[...].astype(jnp.float32)
@@ -267,8 +286,6 @@
     for real, imag in (lanes[:2], lanes[2:]):
         power += [squares[:, real] + squares[:, imag]] * 2
     power = jnp.concatenate(power, axis=1)
-    green_ids = lax.broadcasted_iota(jnp.int32, (green.shape[0], slots * panel), 0)
-    tile_ids = lax.broadcasted_iota(jnp.int32, (tiles, slots * panel), 0)
     class_ids = lax.broadcasted_iota(jnp.int32, (class_count, chunk, stations), 0)
     class_ids = class_ids.astype(jnp.float32).astype(jnp.bfloat16)
     total[...] = jnp.zeros_like(total)
@@ -298,22 +315,16 @@
         owner = blk_index ^ (2 * place)
         own = spectra[pl.ds(pl.multiple_of(owner * panel, panel), panel), :].astype(jnp.float32)
         adjoint = (own * power - mixed[at, :]) * (1.0 / stations)
-        ids = numbers[place]
-        pick = jnp.where(ids[:1] == green_ids, 1.0, 0.0).astype(jnp.bfloat16)
-        tile = jnp.where(ids[1:2] == tile_ids, 1.0, 0.0).astype(jnp.bfloat16)
-        all_picked = lax.dot_general(
-            pick, green[...], TN_DIMS, preferred_element_type=jnp.float32
-        )
         weighted = []
         for slot in range(slots):
-            picked = all_picked[slot * panel : (slot + 1) * panel]
+            picked = picked_ref[place, slot * panel : (slot + 1) * panel].astype(jnp.float32)
             row = []
             for real, imag in (lanes[:2], lanes[2:]):
                 row.append(adjoint[:, real] * picked[:, real] + adjoint[:, imag] * picked[:, imag])
                 row.append(adjoint[:, real] * picked[:, imag] - adjoint[:, imag] * picked[:, real])
             weighted.append(jnp.concatenate(row, axis=1).astype(jnp.bfloat16))
         total[...] += jnp.dot(
-            tile,
+            tile_ref[place],
             jnp.concatenate(weighted, axis=0),
             preferred_element_type=jnp.float32,
         )
@@ -392,6 +403,16 @@
     low, high = mode_tables(n_src, n_blk, math.sqrt(tiles / (stations * slots)))
     devices = n_blk * n_src
     params = pltpu.CompilerParams(vmem_limit_bytes=VMEM_BYTES)
+    banks = pl.pallas_call(
+        bank_kernel,
+        out_shape=(
+            jax.ShapeDtypeStruct((observed.shape[0], 8, 4 * LANES), jnp.float32),
+            jax.ShapeDtypeStruct((green.shape[0], 4 * LANES), jnp.bfloat16),
+        ),
+        compiler_params=params,
+        name="bank",
+    )(observed, green)
+    pieces, banks = lax.optimization_barrier((pieces, banks))
     blocks = pl.pallas_call(
         functools.partial(spectra_kernel, n_src),
         out_shape=jax.ShapeDtypeStruct((devices * share, 2 * LANES), jnp.bfloat16),
@@ -409,20 +430,26 @@
     class_count = observed.shape[0]
     panels = n_blk // 2
     spectra, packs = lax.optimization_barrier((spectra, packs))
+    picked, tile = pl.pallas_call(
+        functools.partial(pick_kernel, slots),
+        out_shape=(
+            jax.ShapeDtypeStruct((panels, slots * panel, 4 * LANES), jnp.bfloat16),
+            jax.ShapeDtypeStruct((panels, tiles, slots * panel), jnp.bfloat16),
+        ),
+        compiler_params=params,
+        name="pick",
+    )(*packs, banks[1])
     parts = pl.pallas_call(
         functools.partial(adjoint_kernel, panels, slots, n_src, 16),
         out_shape=jax.ShapeDtypeStruct((16 * devices, 2 * TILE_SIDE), PARTS_TYPE),
         scratch_shapes=[
             pltpu.VMEM((stations, 4 * LANES), jnp.bfloat16),
-            pltpu.VMEM((panels, 8, slots * panel), jnp.int32),
-            pltpu.VMEM((class_count, 8, 4 * LANES), jnp.float32),
-            pltpu.VMEM((green.shape[0], 4 * LANES), jnp.bfloat16),
             pltpu.VMEM((panels * panel, 4 * LANES), jnp.float32),
             pltpu.VMEM((tiles, 4 * LANES), jnp.float32),
         ],
         compiler_params=params,
         name="adjoint",
-    )(*packs, observed, green, spectra, swap(spectra, "blk", 1), low)
+    )(*packs, picked, tile, banks[0], spectra, swap(spectra, "blk", 1), low)
     parts = lax.all_to_all(
         parts.reshape(devices, 16, 2 * TILE_SIDE), BOTH, 0, 0, tiled=True
     ).reshape(16 * devices, 2 * TILE_SIDE)

time: 54.9 us -> 54.1 us (0.985)
  waiting for transfers between devices: 12.7 us -> 11.2 us
  local copies, waits for them, and re-layouts: 1.04 us -> 1.71 us
    ppermute x7, waiting for transfers between devices: 12 us -> 10.8 us  [swap(): return lax.ppermute(values, axis, [(i, i ^ distance) for i in range(size)])]
    pallas_call x1, Pallas kernels: 11.1 us -> 10.2 us  [split_body(): pl.pallas_call(functools.partial(adjoint_kernel, panels, slots, n_src, 16...]
    pallas_call x0 -> x2, Pallas kernels: none -> 0.85 us  [the longest x1 0.53 us: split_body(): pl.pallas_call(functools.partial(pick_kernel, slots), out_shape=(jax.Shap...]
    unnamed x20, local copies, waits for them, and re-layouts: 0.05 us -> 0.7 us
  transfers between devices with their start and end apart: 8 -> 8, of which waited for: 7 -> 7; matrix products, arithmetic and copies ran while one was open for 0% -> 0% of each run, Pallas kernels for 0% -> 2%
where the time goes in v6:
time: 54.1 us; the launch traced here: 53.9 us
  Pallas kernels  14.7 us (27%)
  starting transfers between devices  14.1 us (26%)
  blocking collectives  12 us (22%)
  waiting for transfers between devices  11.2 us (21%)
  local copies, waits for them, and re-layouts  1.71 us (3%)
    all_to_all x1, blocking collectives, split_body(): lax.all_to_all(parts.reshape(devices, 16, 2 * TILE_SIDE), BOTH, 0, 0, til...  12 us
    ppermute x7, waiting for transfers between devices, swap(): return lax.ppermute(values, axis, [(i, i ^ distance) for i in range(size)])  10.8 us
    pallas_call x1, Pallas kernels, split_body(): pl.pallas_call(functools.partial(adjoint_kernel, panels, slots, n_src, 16...  10.2 us
    ppermute x7, starting transfers between devices, swap(): return lax.ppermute(values, axis, [(i, i ^ distance) for i in range(size)])  9.7 us
    all_to_all x1, starting transfers between devices, split_body(): lax.all_to_all(blocks.reshape(devices, share, 2 * LANES), BOTH, 0, 0, til...  4.42 us
    pallas_call x1, Pallas kernels, split_body(): pl.pallas_call(functools.partial(spectra_kernel, n_src), out_shape=jax.Sh...  2.83 us
  transfers between devices with their start and end apart: 8, of which 7 were waited for; matrix products, arithmetic and copies ran while one was open for 0% of the time, Pallas kernels for 2%

profile of v6, /device:TPU:0, one launch (start us, length us, event | category | flops | bytes accessed | tf_op | source)
XLA Modules:
  0.0 53.9 jit_solution(1386026558231672493)
XLA Ops:
  0.0 0.0 copy-start.1
  0.0 0.0 copy-start.2
  0.0 1.0 %constant_dynamic-slice_fusion = (bf16[16,2048]{1,0:T(8,128)(2,1)S(1)}, bf16[16,2048]{1,0:T(8,128)(2,1)S(1)}, bf16[16,2048]{1,0:T(8,128)(2,1)S(1)}, bf16[16,2048]{1,0:T(8,128)(2,1)S(1)}) fusion(bf16[64,2048]{1,0:T(8,128)(2,1)} %param.11, s32[]{:T(128)S(6)} %select_n.15, s32[]{:T(128)S(6)} %select_n.13, s32[]{:T(128)S(6)} %select_n.12, s32[]{:T(128)S(6)} %select_n.14), kind=kLoop, calls=%fused_computation.8 | loop fusion | bytes 524304 | tf_op jit(solution)/shard_map/dynamic_slice | solution.py:389
  1.0 5.1 %collective-permute-start.2 = (bf16[16,2048]{1,0:T(8,128)(2,1)S(1)}, bf16[16,2048]{1,0:T(8,128)(2,1)S(1)}, u32[]{:S(2)}, u32[]{:S(2)}) collective-permute-start(bf16[16,2048]{1,0:T(8,128)(2,1)S(1)} %get-tuple-element.35), channel_id=1, source_target_pairs={{0,3},{1,2},{2,1},{3,0},{4,7},{5,6},{6,5},{7,4},{8,11},{9,10},{10,... | collective-permute-start | bytes 196616 | tf_op jit(solution)/shard_map/ppermute | solution.py:377
  6.1 0.0 collective-permute-start
  6.1 0.0 copy-start.4
  6.1 0.0 copy-start.5
  6.1 0.0 copy-start.6
  6.1 0.6 %collective-permute-start.1 = (bf16[16,2048]{1,0:T(8,128)(2,1)S(1)}, bf16[16,2048]{1,0:T(8,128)(2,1)S(1)}, u32[]{:S(2)}, u32[]{:S(2)}) collective-permute-start(bf16[16,2048]{1,0:T(8,128)(2,1)S(1)} %get-tuple-element.38), channel_id=1, source_target_pairs={{0,2},{1,3},{2,0},{3,1},{4,6},{5,7},{6,4},{7,5},{8,10},{9,11},{10,... | collective-permute-start | bytes 196616 | tf_op jit(solution)/shard_map/ppermute | solution.py:377
  6.8 0.0 copy-done.1
  6.8 0.0 copy-done.2
  6.8 0.3 bank.1
  7.1 1.9 %collective-permute-done.2.refs_3_ = bf16[16,2048]{1,0:T(8,128)(2,1)S(1)} collective-permute-done((bf16[16,2048]{1,0:T(8,128)(2,1)S(1)}, bf16[16,2048]{1,0:T(8,128)(2,1)S(1)}, u32[]{:S(2)}, u32[]{:S(2)}) %collective-permute-start.2) | collective-permute-done | bytes 65568 | tf_op jit(solution)/shard_map/ppermute | solution.py:377
  9.0 1.7 %collective-permute-done.refs_1_ = bf16[16,2048]{1,0:T(8,128)(2,1)S(1)} collective-permute-done((bf16[16,2048]{1,0:T(8,128)(2,1)S(1)}, bf16[16,2048]{1,0:T(8,128)(2,1)S(1)}, u32[]{:S(2)}, u32[]{:S(2)}) %collective-permute-start) | collective-permute-done | bytes 65568 | tf_op jit(solution)/shard_map/ppermute | solution.py:377
  10.8 1.0 %collective-permute-done.1.refs_2_ = bf16[16,2048]{1,0:T(8,128)(2,1)S(1)} collective-permute-done((bf16[16,2048]{1,0:T(8,128)(2,1)S(1)}, bf16[16,2048]{1,0:T(8,128)(2,1)S(1)}, u32[]{:S(2)}, u32[]{:S(2)}) %collective-permute-start.1) | collective-permute-done | bytes 65568 | tf_op jit(solution)/shard_map/ppermute | solution.py:377
  11.8 0.0 copy-done.4
  11.8 0.0 copy-done.5
  11.8 0.0 copy-done.6
  11.8 2.8 %spectra.1 = bf16[512,256]{1,0:T(8,128)(2,1)} custom-call(bf16[16,2048]{1,0:T(8,128)(2,1)S(1)} %get-tuple-element.22.refs_0_, bf16[16,2048]{1,0:T(8,128)(2,1)S(1)} %collective-permute-done.refs_1_, bf16[16,2048]{1,0:T(8,128)(2,1)S(1)} %collective-permute-done.1.refs_2_, bf16[16,2048]{1,0:T(8,128)(2,1)S(1)} %collective-permute-done.2.refs_3_, ...), custom_call_target="tpu_custom_call" | custom-call | tf_op jit(solution)/shard_map/spectra/pallas_call | solution.py:416
  14.6 0.0 copy-start.8
  14.6 0.0 copy-start.7
  14.6 4.4 %all-to-all-start = ((bf16[32,16,256]{2,1,0:T(8,128)(2,1)}), bf16[32,16,256]{2,1,0:T(8,128)(2,1)S(1)}, u32[]{:S(2)}, u32[]{:S(2)}) async-start(bf16[32,16,256]{2,1,0:T(8,128)(2,1)} %bitcast), calls=%async_computation | async-start | bytes 524288 | tf_op jit(solution)/shard_map/all_to_all | solution.py:427
  19.0 0.0 copy-done.8
  19.1 0.0 copy-start.9
  19.1 0.7 %copy-done.9 = s32[4,64]{1,0:T(4,128)S(1)} copy-done((s32[4,64]{1,0:T(4,128)S(1)}, s32[4,64]{1,0:T(4,128)}, u32[]{:S(2)}) %copy-start.9) | copy-done | bytes 1048
  19.7 0.0 copy-done.7
  19.8 0.0 copy-start
  19.8 2.7 %collective-permute-start.5 = (bf16[80,512]{1,0:T(8,128)(2,1)S(1)}, bf16[80,512]{1,0:T(8,128)(2,1)S(1)}, u32[]{:S(2)}, u32[]{:S(2)}) collective-permute-start(bf16[80,512]{1,0:T(8,128)(2,1)S(1)} %fusion.4.refs_0_), channel_id=1, source_target_pairs={{0,24},{4,28},{8,16},{12,20},{16,8},{20,12},{24,0},{28,4},{1,25},{... | collective-permute-start | bytes 245768 | tf_op jit(solution)/shard_map/ppermute | solution.py:377
  22.5 0.6 %collective-permute-start.4 = (bf16[80,512]{1,0:T(8,128)(2,1)S(1)}, bf16[80,512]{1,0:T(8,128)(2,1)S(1)}, u32[]{:S(2)}, u32[]{:S(2)}) collective-permute-start(bf16[80,512]{1,0:T(8,128)(2,1)S(1)} %fusion.4.refs_0_), channel_id=1, source_target_pairs={{0,16},{4,20},{8,24},{12,28},{16,0},{20,4},{24,8},{28,12},{1,17},{... | collective-permute-start | bytes 245768 | tf_op jit(solution)/shard_map/ppermute | solution.py:377
  23.1 0.3 collective-permute-start.3
  23.3 3.6 %collective-permute-done.5.refs_3_ = bf16[80,512]{1,0:T(8,128)(2,1)S(1)} collective-permute-done((bf16[80,512]{1,0:T(8,128)(2,1)S(1)}, bf16[80,512]{1,0:T(8,128)(2,1)S(1)}, u32[]{:S(2)}, u32[]{:S(2)}) %collective-permute-start.5) | collective-permute-done | bytes 81952 | tf_op jit(solution)/shard_map/ppermute | solution.py:377
  27.0 1.9 %collective-permute-done.4.refs_2_ = bf16[80,512]{1,0:T(8,128)(2,1)S(1)} collective-permute-done((bf16[80,512]{1,0:T(8,128)(2,1)S(1)}, bf16[80,512]{1,0:T(8,128)(2,1)S(1)}, u32[]{:S(2)}, u32[]{:S(2)}) %collective-permute-start.4) | collective-permute-done | bytes 81952 | tf_op jit(solution)/shard_map/ppermute | solution.py:377
  28.9 0.0 collective-permute-done.3.refs_1_
  28.9 0.4 all-to-all-done
  29.2 0.4 collective-permute-start.6
  29.6 0.5 pick.1
  30.2 0.6 %collective-permute-done.6.refs_8_ = bf16[512,256]{1,0:T(8,128)(2,1)S(1)} collective-permute-done((bf16[512,256]{1,0:T(8,128)(2,1)S(1)}, bf16[512,256]{1,0:T(8,128)(2,1)S(1)}, u32[]{:S(2)}, u32[]{:S(2)}) %collective-permute-start.6) | collective-permute-done | bytes 262176 | tf_op jit(solution)/shard_map/ppermute | solution.py:377
  30.8 0.0 copy-done
  30.8 10.2 %adjoint.1 = bf16[512,128]{1,0:T(8,128)(2,1)S(1)} custom-call(bf16[80,512]{1,0:T(8,128)(2,1)S(1)} %fusion.4.refs_0_, bf16[80,512]{1,0:T(8,128)(2,1)S(1)} %collective-permute-done.3.refs_1_, bf16[80,512]{1,0:T(8,128)(2,1)S(1)} %collective-permute-done.4.refs_2_, bf16[80,512]{1,0:T(8,128)(2,1)S(1)} %collective-permute-done.5.refs_3_, ...), custom_call_target="tpu_custom_call" | custom-call | tf_op jit(solution)/shard_map/adjoint/pallas_call | solution.py:442
  41.0 0.0 copy-start.3
  41.0 12.0 %all_to_all.10 = bf16[32,16,128]{2,1,0:T(8,128)(2,1)S(1)} all-to-all(bf16[32,16,128]{2,1,0:T(8,128)(2,1)S(1)} %bitcast.6), channel_id=1, replica_groups=mesh['blk'=8,'src'=4] {'blk','src'}, dimensions={0} | all-to-all | bytes 262144 | tf_op jit(solution)/shard_map/all_to_all | solution.py:453
  53.1 0.0 copy-done.3
  53.1 0.8 %image.1 = f32[4,512]{1,0:T(4,128)} custom-call(bf16[8,32,512]{2,1,0:T(8,128)(2,1)S(1)} %copy-done.3, bf16[512,128]{1,0:T(8,128)(2,1)S(1)} %bitcast.7), custom_call_target="tpu_custom_call" | custom-call | tf_op jit(solution)/shard_map/image/pallas_call | solution.py:456
  (4 shorter events, 0.0 us)
Async XLA Ops:
  0.0 6.8 %copy-start.1 = (bf16[64,2,1024]{2,1,0:T(2,128)(2,1)S(1)}, bf16[64,2,1024]{2,1,0:T(2,128)(2,1)}, u32[]{:S(2)}) copy-start(bf16[64,2,1024]{2,1,0:T(2,128)(2,1)} %observed_ref.1) | copy-start | bytes 786436
  0.0 6.8 %copy-start.2 = (bf16[64,2,1024]{2,1,0:T(2,128)(2,1)S(1)}, bf16[64,2,1024]{2,1,0:T(2,128)(2,1)}, u32[]{:S(2)}) copy-start(bf16[64,2,1024]{2,1,0:T(2,128)(2,1)} %green_ref.1) | copy-start | bytes 786436
  1.0 8.0 %collective-permute-start.2 = (bf16[16,2048]{1,0:T(8,128)(2,1)S(1)}, bf16[16,2048]{1,0:T(8,128)(2,1)S(1)}, u32[]{:S(2)}, u32[]{:S(2)}) collective-permute-start(bf16[16,2048]{1,0:T(8,128)(2,1)S(1)} %get-tuple-element.35), channel_id=1, source_target_pairs={{0,3},{1,2},{2,1},{3,0},{4,7},{5,6},{6,5},{7,4},{8,11},{9,10},{10,... | collective-permute-start | bytes 196616 | tf_op jit(solution)/shard_map/ppermute | solution.py:377
  6.1 4.6 %collective-permute-start = (bf16[16,2048]{1,0:T(8,128)(2,1)S(1)}, bf16[16,2048]{1,0:T(8,128)(2,1)S(1)}, u32[]{:S(2)}, u32[]{:S(2)}) collective-permute-start(bf16[16,2048]{1,0:T(8,128)(2,1)S(1)} %get-tuple-element.36), channel_id=1, source_target_pairs={{0,1},{1,0},{2,3},{3,2},{4,5},{5,4},{6,7},{7,6},{8,9},{9,8},{10,11... | collective-permute-start | bytes 196616 | tf_op jit(solution)/shard_map/ppermute | solution.py:377
  6.1 5.6 %copy-start.4 = (f32[2,128,128]{2,1,0:T(8,128)S(1)}, f32[2,128,128]{2,1,0:T(8,128)}, u32[]{:S(2)}) copy-start(f32[2,128,128]{2,1,0:T(8,128)} %constant.29.clone.refs_5_) | copy-start | bytes 393220
  6.1 5.6 %copy-start.5 = (bf16[128,256]{1,0:T(8,128)(2,1)S(1)}, bf16[128,256]{1,0:T(8,128)(2,1)}, u32[]{:S(2)}) copy-start(bf16[128,256]{1,0:T(8,128)(2,1)} %constant.30.clone.refs_6_) | copy-start | bytes 196612
  6.1 5.6 %copy-start.6 = (bf16[256,64]{1,0:T(8,128)(2,1)S(1)}, bf16[256,64]{1,0:T(8,128)(2,1)}, u32[]{:S(2)}) copy-start(bf16[256,64]{1,0:T(8,128)(2,1)} %constant.28.clone.refs_4_) | copy-start | bytes 98308
  6.1 5.6 %collective-permute-start.1 = (bf16[16,2048]{1,0:T(8,128)(2,1)S(1)}, bf16[16,2048]{1,0:T(8,128)(2,1)S(1)}, u32[]{:S(2)}, u32[]{:S(2)}) collective-permute-start(bf16[16,2048]{1,0:T(8,128)(2,1)S(1)} %get-tuple-element.38), channel_id=1, source_target_pairs={{0,2},{1,3},{2,0},{3,1},{4,6},{5,7},{6,4},{7,5},{8,10},{9,11},{10,... | collective-permute-start | bytes 196616 | tf_op jit(solution)/shard_map/ppermute | solution.py:377
  14.6 4.4 %copy-start.8 = (s32[4,64]{1,0:T(4,128)S(1)}, s32[4,64]{1,0:T(4,128)}, u32[]{:S(2)}) copy-start(s32[4,64]{1,0:T(4,128)} %param.15) | copy-start | bytes 3076
  14.6 5.1 %copy-start.7 = (s32[64,512]{1,0:T(8,128)S(1)}, s32[64,512]{1,0:T(8,128)}, u32[]{:S(2)}) copy-start(s32[64,512]{1,0:T(8,128)} %param.13) | copy-start | bytes 393220
  14.6 14.6 %all-to-all-start = ((bf16[32,16,256]{2,1,0:T(8,128)(2,1)}), bf16[32,16,256]{2,1,0:T(8,128)(2,1)S(1)}, u32[]{:S(2)}, u32[]{:S(2)}) async-start(bf16[32,16,256]{2,1,0:T(8,128)(2,1)} %bitcast), calls=%async_computation | async-start | bytes 524288 | tf_op jit(solution)/shard_map/all_to_all | solution.py:427
  19.1 0.7 %copy-start.9 = (s32[4,64]{1,0:T(4,128)S(1)}, s32[4,64]{1,0:T(4,128)}, u32[]{:S(2)}) copy-start(s32[4,64]{1,0:T(4,128)} %param.16) | copy-start | bytes 3076
  19.8 11.0 %copy-start = (f32[256,256]{1,0:T(8,128)S(1)}, f32[256,256]{1,0:T(8,128)}, u32[]{:S(2)}) copy-start(f32[256,256]{1,0:T(8,128)} %constant.31.clone.refs_9_) | copy-start | bytes 786436
  19.8 7.2 %collective-permute-start.5 = (bf16[80,512]{1,0:T(8,128)(2,1)S(1)}, bf16[80,512]{1,0:T(8,128)(2,1)S(1)}, u32[]{:S(2)}, u32[]{:S(2)}) collective-permute-start(bf16[80,512]{1,0:T(8,128)(2,1)S(1)} %fusion.4.refs_0_), channel_id=1, source_target_pairs={{0,24},{4,28},{8,16},{12,20},{16,8},{20,12},{24,0},{28,4},{1,25},{... | collective-permute-start | bytes 245768 | tf_op jit(solution)/shard_map/ppermute | solution.py:377
  22.5 6.4 %collective-permute-start.4 = (bf16[80,512]{1,0:T(8,128)(2,1)S(1)}, bf16[80,512]{1,0:T(8,128)(2,1)S(1)}, u32[]{:S(2)}, u32[]{:S(2)}) collective-permute-start(bf16[80,512]{1,0:T(8,128)(2,1)S(1)} %fusion.4.refs_0_), channel_id=1, source_target_pairs={{0,16},{4,20},{8,24},{12,28},{16,0},{20,4},{24,8},{28,12},{1,17},{... | collective-permute-start | bytes 245768 | tf_op jit(solution)/shard_map/ppermute | solution.py:377
  23.1 5.8 %collective-permute-start.3 = (bf16[80,512]{1,0:T(8,128)(2,1)S(1)}, bf16[80,512]{1,0:T(8,128)(2,1)S(1)}, u32[]{:S(2)}, u32[]{:S(2)}) collective-permute-start(bf16[80,512]{1,0:T(8,128)(2,1)S(1)} %fusion.4.refs_0_), channel_id=1, source_target_pairs={{0,8},{4,12},{8,0},{12,4},{16,24},{20,28},{24,16},{28,20},{1,9},{5... | collective-permute-start | bytes 245768 | tf_op jit(solution)/shard_map/ppermute | solution.py:377
  29.2 1.6 %collective-permute-start.6 = (bf16[512,256]{1,0:T(8,128)(2,1)S(1)}, bf16[512,256]{1,0:T(8,128)(2,1)S(1)}, u32[]{:S(2)}, u32[]{:S(2)}) collective-permute-start(bf16[512,256]{1,0:T(8,128)(2,1)S(1)} %bitcast.4), channel_id=1, source_target_pairs={{0,4},{4,0},{8,12},{12,8},{16,20},{20,16},{24,28},{28,24},{1,5},{5... | collective-permute-start | bytes 786440 | tf_op jit(solution)/shard_map/ppermute | solution.py:377
  41.0 12.1 %copy-start.3 = (bf16[8,32,512]{2,1,0:T(8,128)(2,1)S(1)}, bf16[8,32,512]{2,1,0:T(8,128)(2,1)}, u32[]{:S(2)}) copy-start(bf16[8,32,512]{2,1,0:T(8,128)(2,1)} %constant.32.clone.high_ref) | copy-start | bytes 786436

commit v7 on v6

--- a/solution.py
+++ b/solution.py
@@ -174,7 +174,8 @@
         high[:, half, :, :, :, half] = part
     high = high.reshape(n_blk, 2 * TILE_SIDE // n_blk, 16 * n_src * n_blk)
     high = split_bf16((high / math.sqrt(F)).astype(np.float32))
-    return low.astype(np.float32), np.concatenate(high, axis=1)
+    low = np.concatenate(split_bf16(low.astype(np.float32)), axis=1)
+    return low, np.concatenate(high, axis=1)
 
 
 def spectra_kernel(n_src, *refs):
@@ -268,6 +269,15 @@
         tile_ref[k] = jnp.where(seats == tile_ids, 1.0, 0.0).astype(jnp.bfloat16)
 
 
+def three_pass(values, table_ref):
+    width = table_ref.shape[1] // 2
+    high = values.astype(jnp.bfloat16)
+    low = (values - high.astype(jnp.float32)).astype(jnp.bfloat16)
+    both = jnp.dot(high, table_ref[...], preferred_element_type=jnp.float32)
+    rest = jnp.dot(low, table_ref[:, :width], preferred_element_type=jnp.float32)
+    return both[:, :width] + both[:, width:] + rest
+
+
 def adjoint_kernel(panels, slots, n_src, chunk, *refs):
     packs = refs[:panels]
     picked_ref, tile_ref, bank, spectra_ref, other_ref, low_ref, out_ref = refs[panels : panels + 7]
@@ -329,15 +339,12 @@
             preferred_element_type=jnp.float32,
         )
 
-    mix(0)
-    for place in range(1, panels):
+    for place in range(panels):
         mix(place)
-        gather(place - 1)
-    gather(panels - 1)
+    for place in range(panels):
+        gather(place)
     low = [
-        jnp.dot(
-            total[:, at], low_ref[...], precision=HIGHEST, preferred_element_type=jnp.float32
-        )
+        three_pass(total[:, at], low_ref)
         for at in (slice(0, 2 * LANES), slice(2 * LANES, 4 * LANES))
     ]
     rows = []

time: 54.1 us -> 53.9 us (level)
  no operation moved by 1% of the time
where the time goes in v7:
time: 53.9 us; the launch traced here: 53.7 us
  Pallas kernels  14.5 us (27%)
  starting transfers between devices  14.1 us (26%)
  blocking collectives  12 us (22%)
  waiting for transfers between devices  11.2 us (21%)
  local copies, waits for them, and re-layouts  1.71 us (3%)
    all_to_all x1, blocking collectives, split_body(): lax.all_to_all(parts.reshape(devices, 16, 2 * TILE_SIDE), BOTH, 0, 0, til...  12 us
    ppermute x7, waiting for transfers between devices, swap(): return lax.ppermute(values, axis, [(i, i ^ distance) for i in range(size)])  10.8 us
    pallas_call x1, Pallas kernels, split_body(): pl.pallas_call(functools.partial(adjoint_kernel, panels, slots, n_src, 16...  9.99 us
    ppermute x7, starting transfers between devices, swap(): return lax.ppermute(values, axis, [(i, i ^ distance) for i in range(size)])  9.7 us
    all_to_all x1, starting transfers between devices, split_body(): lax.all_to_all(blocks.reshape(devices, share, 2 * LANES), BOTH, 0, 0, til...  4.42 us
    pallas_call x1, Pallas kernels, split_body(): pl.pallas_call(functools.partial(spectra_kernel, n_src), out_shape=jax.Sh...  2.83 us
  transfers between devices with their start and end apart: 8, of which 7 were waited for; matrix products, arithmetic and copies ran while one was open for 0% of the time, Pallas kernels for 2%

profile of v7, /device:TPU:0, one launch (start us, length us, event | category | flops | bytes accessed | tf_op | source)
XLA Modules:
  0.0 53.7 jit_solution(6657309497451576727)
XLA Ops:
  0.0 0.0 copy-start.1
  0.0 0.0 copy-start.2
  0.0 1.0 %constant_dynamic-slice_fusion = (bf16[16,2048]{1,0:T(8,128)(2,1)S(1)}, bf16[16,2048]{1,0:T(8,128)(2,1)S(1)}, bf16[16,2048]{1,0:T(8,128)(2,1)S(1)}, bf16[16,2048]{1,0:T(8,128)(2,1)S(1)}) fusion(bf16[64,2048]{1,0:T(8,128)(2,1)} %param.11, s32[]{:T(128)S(6)} %select_n.15, s32[]{:T(128)S(6)} %select_n.13, s32[]{:T(128)S(6)} %select_n.12, s32[]{:T(128)S(6)} %select_n.14), kind=kLoop, calls=%fused_computation.8 | loop fusion | bytes 524304 | tf_op jit(solution)/shard_map/dynamic_slice | solution.py:396
  1.0 5.1 %collective-permute-start.2 = (bf16[16,2048]{1,0:T(8,128)(2,1)S(1)}, bf16[16,2048]{1,0:T(8,128)(2,1)S(1)}, u32[]{:S(2)}, u32[]{:S(2)}) collective-permute-start(bf16[16,2048]{1,0:T(8,128)(2,1)S(1)} %get-tuple-element.35), channel_id=1, source_target_pairs={{0,3},{1,2},{2,1},{3,0},{4,7},{5,6},{6,5},{7,4},{8,11},{9,10},{10,... | collective-permute-start | bytes 196616 | tf_op jit(solution)/shard_map/ppermute | solution.py:384
  6.1 0.0 collective-permute-start
  6.1 0.0 copy-start.4
  6.1 0.0 copy-start.5
  6.1 0.0 copy-start.6
  6.1 0.6 %collective-permute-start.1 = (bf16[16,2048]{1,0:T(8,128)(2,1)S(1)}, bf16[16,2048]{1,0:T(8,128)(2,1)S(1)}, u32[]{:S(2)}, u32[]{:S(2)}) collective-permute-start(bf16[16,2048]{1,0:T(8,128)(2,1)S(1)} %get-tuple-element.38), channel_id=1, source_target_pairs={{0,2},{1,3},{2,0},{3,1},{4,6},{5,7},{6,4},{7,5},{8,10},{9,11},{10,... | collective-permute-start | bytes 196616 | tf_op jit(solution)/shard_map/ppermute | solution.py:384
  6.8 0.0 copy-done.1
  6.8 0.0 copy-done.2
  6.8 0.3 bank.1
  7.1 1.9 %collective-permute-done.2.refs_3_ = bf16[16,2048]{1,0:T(8,128)(2,1)S(1)} collective-permute-done((bf16[16,2048]{1,0:T(8,128)(2,1)S(1)}, bf16[16,2048]{1,0:T(8,128)(2,1)S(1)}, u32[]{:S(2)}, u32[]{:S(2)}) %collective-permute-start.2) | collective-permute-done | bytes 65568 | tf_op jit(solution)/shard_map/ppermute | solution.py:384
  9.0 1.7 %collective-permute-done.refs_1_ = bf16[16,2048]{1,0:T(8,128)(2,1)S(1)} collective-permute-done((bf16[16,2048]{1,0:T(8,128)(2,1)S(1)}, bf16[16,2048]{1,0:T(8,128)(2,1)S(1)}, u32[]{:S(2)}, u32[]{:S(2)}) %collective-permute-start) | collective-permute-done | bytes 65568 | tf_op jit(solution)/shard_map/ppermute | solution.py:384
  10.8 1.0 %collective-permute-done.1.refs_2_ = bf16[16,2048]{1,0:T(8,128)(2,1)S(1)} collective-permute-done((bf16[16,2048]{1,0:T(8,128)(2,1)S(1)}, bf16[16,2048]{1,0:T(8,128)(2,1)S(1)}, u32[]{:S(2)}, u32[]{:S(2)}) %collective-permute-start.1) | collective-permute-done | bytes 65568 | tf_op jit(solution)/shard_map/ppermute | solution.py:384
  11.8 0.0 copy-done.4
  11.8 0.0 copy-done.5
  11.8 0.0 copy-done.6
  11.8 2.8 %spectra.1 = bf16[512,256]{1,0:T(8,128)(2,1)} custom-call(bf16[16,2048]{1,0:T(8,128)(2,1)S(1)} %get-tuple-element.22.refs_0_, bf16[16,2048]{1,0:T(8,128)(2,1)S(1)} %collective-permute-done.refs_1_, bf16[16,2048]{1,0:T(8,128)(2,1)S(1)} %collective-permute-done.1.refs_2_, bf16[16,2048]{1,0:T(8,128)(2,1)S(1)} %collective-permute-done.2.refs_3_, ...), custom_call_target="tpu_custom_call" | custom-call | tf_op jit(solution)/shard_map/spectra/pallas_call | solution.py:423
  14.6 0.0 copy-start.8
  14.6 0.0 copy-start.7
  14.6 4.4 %all-to-all-start = ((bf16[32,16,256]{2,1,0:T(8,128)(2,1)}), bf16[32,16,256]{2,1,0:T(8,128)(2,1)S(1)}, u32[]{:S(2)}, u32[]{:S(2)}) async-start(bf16[32,16,256]{2,1,0:T(8,128)(2,1)} %bitcast), calls=%async_computation | async-start | bytes 524288 | tf_op jit(solution)/shard_map/all_to_all | solution.py:434
  19.0 0.0 copy-done.8
  19.1 0.0 copy-start.9
  19.1 0.7 %copy-done.9 = s32[4,64]{1,0:T(4,128)S(1)} copy-done((s32[4,64]{1,0:T(4,128)S(1)}, s32[4,64]{1,0:T(4,128)}, u32[]{:S(2)}) %copy-start.9) | copy-done | bytes 1048
  19.7 0.0 copy-done.7
  19.8 0.0 copy-start
  19.8 2.7 %collective-permute-start.5 = (bf16[80,512]{1,0:T(8,128)(2,1)S(1)}, bf16[80,512]{1,0:T(8,128)(2,1)S(1)}, u32[]{:S(2)}, u32[]{:S(2)}) collective-permute-start(bf16[80,512]{1,0:T(8,128)(2,1)S(1)} %fusion.4.refs_0_), channel_id=1, source_target_pairs={{0,24},{4,28},{8,16},{12,20},{16,8},{20,12},{24,0},{28,4},{1,25},{... | collective-permute-start | bytes 245768 | tf_op jit(solution)/shard_map/ppermute | solution.py:384
  22.5 0.6 %collective-permute-start.4 = (bf16[80,512]{1,0:T(8,128)(2,1)S(1)}, bf16[80,512]{1,0:T(8,128)(2,1)S(1)}, u32[]{:S(2)}, u32[]{:S(2)}) collective-permute-start(bf16[80,512]{1,0:T(8,128)(2,1)S(1)} %fusion.4.refs_0_), channel_id=1, source_target_pairs={{0,16},{4,20},{8,24},{12,28},{16,0},{20,4},{24,8},{28,12},{1,17},{... | collective-permute-start | bytes 245768 | tf_op jit(solution)/shard_map/ppermute | solution.py:384
  23.1 0.3 collective-permute-start.3
  23.3 3.6 %collective-permute-done.5.refs_3_ = bf16[80,512]{1,0:T(8,128)(2,1)S(1)} collective-permute-done((bf16[80,512]{1,0:T(8,128)(2,1)S(1)}, bf16[80,512]{1,0:T(8,128)(2,1)S(1)}, u32[]{:S(2)}, u32[]{:S(2)}) %collective-permute-start.5) | collective-permute-done | bytes 81952 | tf_op jit(solution)/shard_map/ppermute | solution.py:384
  27.0 1.9 %collective-permute-done.4.refs_2_ = bf16[80,512]{1,0:T(8,128)(2,1)S(1)} collective-permute-done((bf16[80,512]{1,0:T(8,128)(2,1)S(1)}, bf16[80,512]{1,0:T(8,128)(2,1)S(1)}, u32[]{:S(2)}, u32[]{:S(2)}) %collective-permute-start.4) | collective-permute-done | bytes 81952 | tf_op jit(solution)/shard_map/ppermute | solution.py:384
  28.9 0.0 collective-permute-done.3.refs_1_
  28.9 0.4 all-to-all-done
  29.2 0.4 collective-permute-start.6
  29.6 0.5 pick.1
  30.2 0.6 %collective-permute-done.6.refs_8_ = bf16[512,256]{1,0:T(8,128)(2,1)S(1)} collective-permute-done((bf16[512,256]{1,0:T(8,128)(2,1)S(1)}, bf16[512,256]{1,0:T(8,128)(2,1)S(1)}, u32[]{:S(2)}, u32[]{:S(2)}) %collective-permute-start.6) | collective-permute-done | bytes 262176 | tf_op jit(solution)/shard_map/ppermute | solution.py:384
  30.8 0.0 copy-done
  30.8 10.0 %adjoint.1 = bf16[512,128]{1,0:T(8,128)(2,1)S(1)} custom-call(bf16[80,512]{1,0:T(8,128)(2,1)S(1)} %fusion.4.refs_0_, bf16[80,512]{1,0:T(8,128)(2,1)S(1)} %collective-permute-done.3.refs_1_, bf16[80,512]{1,0:T(8,128)(2,1)S(1)} %collective-permute-done.4.refs_2_, bf16[80,512]{1,0:T(8,128)(2,1)S(1)} %collective-permute-done.5.refs_3_, ...), custom_call_target="tpu_custom_call" | custom-call | tf_op jit(solution)/shard_map/adjoint/pallas_call | solution.py:449
  40.8 0.0 copy-start.3
  40.8 12.0 %all_to_all.10 = bf16[32,16,128]{2,1,0:T(8,128)(2,1)S(1)} all-to-all(bf16[32,16,128]{2,1,0:T(8,128)(2,1)S(1)} %bitcast.6), channel_id=1, replica_groups=mesh['blk'=8,'src'=4] {'blk','src'}, dimensions={0} | all-to-all | bytes 262144 | tf_op jit(solution)/shard_map/all_to_all | solution.py:460
  52.9 0.0 copy-done.3
  52.9 0.8 %image.1 = f32[4,512]{1,0:T(4,128)} custom-call(bf16[8,32,512]{2,1,0:T(8,128)(2,1)S(1)} %copy-done.3, bf16[512,128]{1,0:T(8,128)(2,1)S(1)} %bitcast.7), custom_call_target="tpu_custom_call" | custom-call | tf_op jit(solution)/shard_map/image/pallas_call | solution.py:463
  (4 shorter events, 0.0 us)
Async XLA Ops:
  0.0 6.8 %copy-start.1 = (bf16[64,2,1024]{2,1,0:T(2,128)(2,1)S(1)}, bf16[64,2,1024]{2,1,0:T(2,128)(2,1)}, u32[]{:S(2)}) copy-start(bf16[64,2,1024]{2,1,0:T(2,128)(2,1)} %observed_ref.1) | copy-start | bytes 786436
  0.0 6.8 %copy-start.2 = (bf16[64,2,1024]{2,1,0:T(2,128)(2,1)S(1)}, bf16[64,2,1024]{2,1,0:T(2,128)(2,1)}, u32[]{:S(2)}) copy-start(bf16[64,2,1024]{2,1,0:T(2,128)(2,1)} %green_ref.1) | copy-start | bytes 786436
  1.0 8.0 %collective-permute-start.2 = (bf16[16,2048]{1,0:T(8,128)(2,1)S(1)}, bf16[16,2048]{1,0:T(8,128)(2,1)S(1)}, u32[]{:S(2)}, u32[]{:S(2)}) collective-permute-start(bf16[16,2048]{1,0:T(8,128)(2,1)S(1)} %get-tuple-element.35), channel_id=1, source_target_pairs={{0,3},{1,2},{2,1},{3,0},{4,7},{5,6},{6,5},{7,4},{8,11},{9,10},{10,... | collective-permute-start | bytes 196616 | tf_op jit(solution)/shard_map/ppermute | solution.py:384
  6.1 4.6 %collective-permute-start = (bf16[16,2048]{1,0:T(8,128)(2,1)S(1)}, bf16[16,2048]{1,0:T(8,128)(2,1)S(1)}, u32[]{:S(2)}, u32[]{:S(2)}) collective-permute-start(bf16[16,2048]{1,0:T(8,128)(2,1)S(1)} %get-tuple-element.36), channel_id=1, source_target_pairs={{0,1},{1,0},{2,3},{3,2},{4,5},{5,4},{6,7},{7,6},{8,9},{9,8},{10,11... | collective-permute-start | bytes 196616 | tf_op jit(solution)/shard_map/ppermute | solution.py:384
  6.1 5.6 %copy-start.4 = (f32[2,128,128]{2,1,0:T(8,128)S(1)}, f32[2,128,128]{2,1,0:T(8,128)}, u32[]{:S(2)}) copy-start(f32[2,128,128]{2,1,0:T(8,128)} %constant.29.clone.refs_5_) | copy-start | bytes 393220
  6.1 5.6 %copy-start.5 = (bf16[128,256]{1,0:T(8,128)(2,1)S(1)}, bf16[128,256]{1,0:T(8,128)(2,1)}, u32[]{:S(2)}) copy-start(bf16[128,256]{1,0:T(8,128)(2,1)} %constant.30.clone.refs_6_) | copy-start | bytes 196612
  6.1 5.6 %copy-start.6 = (bf16[256,64]{1,0:T(8,128)(2,1)S(1)}, bf16[256,64]{1,0:T(8,128)(2,1)}, u32[]{:S(2)}) copy-start(bf16[256,64]{1,0:T(8,128)(2,1)} %constant.28.clone.refs_4_) | copy-start | bytes 98308
  6.1 5.6 %collective-permute-start.1 = (bf16[16,2048]{1,0:T(8,128)(2,1)S(1)}, bf16[16,2048]{1,0:T(8,128)(2,1)S(1)}, u32[]{:S(2)}, u32[]{:S(2)}) collective-permute-start(bf16[16,2048]{1,0:T(8,128)(2,1)S(1)} %get-tuple-element.38), channel_id=1, source_target_pairs={{0,2},{1,3},{2,0},{3,1},{4,6},{5,7},{6,4},{7,5},{8,10},{9,11},{10,... | collective-permute-start | bytes 196616 | tf_op jit(solution)/shard_map/ppermute | solution.py:384
  14.6 4.4 %copy-start.8 = (s32[4,64]{1,0:T(4,128)S(1)}, s32[4,64]{1,0:T(4,128)}, u32[]{:S(2)}) copy-start(s32[4,64]{1,0:T(4,128)} %param.15) | copy-start | bytes 3076
  14.6 5.1 %copy-start.7 = (s32[64,512]{1,0:T(8,128)S(1)}, s32[64,512]{1,0:T(8,128)}, u32[]{:S(2)}) copy-start(s32[64,512]{1,0:T(8,128)} %param.13) | copy-start | bytes 393220
  14.6 14.6 %all-to-all-start = ((bf16[32,16,256]{2,1,0:T(8,128)(2,1)}), bf16[32,16,256]{2,1,0:T(8,128)(2,1)S(1)}, u32[]{:S(2)}, u32[]{:S(2)}) async-start(bf16[32,16,256]{2,1,0:T(8,128)(2,1)} %bitcast), calls=%async_computation | async-start | bytes 524288 | tf_op jit(solution)/shard_map/all_to_all | solution.py:434
  19.1 0.7 %copy-start.9 = (s32[4,64]{1,0:T(4,128)S(1)}, s32[4,64]{1,0:T(4,128)}, u32[]{:S(2)}) copy-start(s32[4,64]{1,0:T(4,128)} %param.16) | copy-start | bytes 3076
  19.8 11.0 %copy-start = (bf16[256,512]{1,0:T(8,128)(2,1)S(1)}, bf16[256,512]{1,0:T(8,128)(2,1)}, u32[]{:S(2)}) copy-start(bf16[256,512]{1,0:T(8,128)(2,1)} %constant.31.clone.refs_9_) | copy-start | bytes 786436
  19.8 7.2 %collective-permute-start.5 = (bf16[80,512]{1,0:T(8,128)(2,1)S(1)}, bf16[80,512]{1,0:T(8,128)(2,1)S(1)}, u32[]{:S(2)}, u32[]{:S(2)}) collective-permute-start(bf16[80,512]{1,0:T(8,128)(2,1)S(1)} %fusion.4.refs_0_), channel_id=1, source_target_pairs={{0,24},{4,28},{8,16},{12,20},{16,8},{20,12},{24,0},{28,4},{1,25},{... | collective-permute-start | bytes 245768 | tf_op jit(solution)/shard_map/ppermute | solution.py:384
  22.5 6.4 %collective-permute-start.4 = (bf16[80,512]{1,0:T(8,128)(2,1)S(1)}, bf16[80,512]{1,0:T(8,128)(2,1)S(1)}, u32[]{:S(2)}, u32[]{:S(2)}) collective-permute-start(bf16[80,512]{1,0:T(8,128)(2,1)S(1)} %fusion.4.refs_0_), channel_id=1, source_target_pairs={{0,16},{4,20},{8,24},{12,28},{16,0},{20,4},{24,8},{28,12},{1,17},{... | collective-permute-start | bytes 245768 | tf_op jit(solution)/shard_map/ppermute | solution.py:384
  23.1 5.8 %collective-permute-start.3 = (bf16[80,512]{1,0:T(8,128)(2,1)S(1)}, bf16[80,512]{1,0:T(8,128)(2,1)S(1)}, u32[]{:S(2)}, u32[]{:S(2)}) collective-permute-start(bf16[80,512]{1,0:T(8,128)(2,1)S(1)} %fusion.4.refs_0_), channel_id=1, source_target_pairs={{0,8},{4,12},{8,0},{12,4},{16,24},{20,28},{24,16},{28,20},{1,9},{5... | collective-permute-start | bytes 245768 | tf_op jit(solution)/shard_map/ppermute | solution.py:384
  29.2 1.6 %collective-permute-start.6 = (bf16[512,256]{1,0:T(8,128)(2,1)S(1)}, bf16[512,256]{1,0:T(8,128)(2,1)S(1)}, u32[]{:S(2)}, u32[]{:S(2)}) collective-permute-start(bf16[512,256]{1,0:T(8,128)(2,1)S(1)} %bitcast.4), channel_id=1, source_target_pairs={{0,4},{4,0},{8,12},{12,8},{16,20},{20,16},{24,28},{28,24},{1,5},{5... | collective-permute-start | bytes 786440 | tf_op jit(solution)/shard_map/ppermute | solution.py:384
  40.8 12.1 %copy-start.3 = (bf16[8,32,512]{2,1,0:T(8,128)(2,1)S(1)}, bf16[8,32,512]{2,1,0:T(8,128)(2,1)}, u32[]{:S(2)}) copy-start(bf16[8,32,512]{2,1,0:T(8,128)(2,1)} %constant.32.clone.high_ref) | copy-start | bytes 786436

commit v8 on v7

--- a/solution.py
+++ b/solution.py
@@ -250,7 +250,11 @@
 
 
 def pick_kernel(slots, *refs):
-    *packs, green_ref, picked_ref, tile_ref = refs
+    *packs, green_ref, spectra_ref, picked_ref, tile_ref, squares_ref = refs
+    widened = spectra_ref[...].astype(jnp.float32)
+    squares_ref[...] = jnp.broadcast_to(
+        jnp.sum(widened * widened, axis=0, keepdims=True), squares_ref.shape
+    )
     panel = picked_ref.shape[1] // slots
     green_ids = lax.broadcasted_iota(jnp.int32, (green_ref.shape[0], slots * panel), 0)
     tile_ids = lax.broadcasted_iota(jnp.int32, (tile_ref.shape[1], slots * panel), 0)
@@ -280,8 +284,8 @@
 
 def adjoint_kernel(panels, slots, n_src, chunk, *refs):
     packs = refs[:panels]
-    picked_ref, tile_ref, bank, spectra_ref, other_ref, low_ref, out_ref = refs[panels : panels + 7]
-    spectra, mixed, total = refs[panels + 7 :]
+    picked_ref, tile_ref, squares_ref, bank = refs[panels : panels + 4]
+    spectra_ref, other_ref, low_ref, out_ref, spectra, mixed, total = refs[panels + 4 :]
     stations = spectra_ref.shape[0]
     panel = mixed.shape[0] // panels
     class_count = bank.shape[0]
@@ -289,8 +293,9 @@
     blk_index = lax.axis_index("blk")
     spectra[:, : 2 * LANES] = spectra_ref[...]
     spectra[:, 2 * LANES :] = other_ref[...]
-    widened = spectra[...].astype(jnp.float32)
+    widened = other_ref[...].astype(jnp.float32)
     squares = jnp.sum(widened * widened, axis=0, keepdims=True)
+    squares = jnp.concatenate([squares_ref[:1], squares], axis=1)
     lanes = [slice(part * LANES, (part + 1) * LANES) for part in range(4)]
     power = []
     for real, imag in (lanes[:2], lanes[2:]):
@@ -437,15 +442,16 @@
     class_count = observed.shape[0]
     panels = n_blk // 2
     spectra, packs = lax.optimization_barrier((spectra, packs))
-    picked, tile = pl.pallas_call(
+    picked, tile, squares = pl.pallas_call(
         functools.partial(pick_kernel, slots),
         out_shape=(
             jax.ShapeDtypeStruct((panels, slots * panel, 4 * LANES), jnp.bfloat16),
             jax.ShapeDtypeStruct((panels, tiles, slots * panel), jnp.bfloat16),
+            jax.ShapeDtypeStruct((8, 2 * LANES), jnp.float32),
         ),
         compiler_params=params,
         name="pick",
-    )(*packs, banks[1])
+    )(*packs, banks[1], spectra)
     parts = pl.pallas_call(
         functools.partial(adjoint_kernel, panels, slots, n_src, 16),
         out_shape=jax.ShapeDtypeStruct((16 * devices, 2 * TILE_SIDE), PARTS_TYPE),
@@ -456,7 +462,7 @@
         ],
         compiler_params=params,
         name="adjoint",
-    )(*packs, picked, tile, banks[0], spectra, swap(spectra, "blk", 1), low)
+    )(*packs, picked, tile, squares, banks[0], spectra, swap(spectra, "blk", 1), low)
     parts = lax.all_to_all(
         parts.reshape(devices, 16, 2 * TILE_SIDE), BOTH, 0, 0, tiled=True
     ).reshape(16 * devices, 2 * TILE_SIDE)

time: 53.9 us -> 54 us (level)
  no operation moved by 1% of the time
where the time goes in v8:
time: 54 us; the launch traced here: 53.8 us
  Pallas kernels  14.5 us (27%)
  starting transfers between devices  14.1 us (26%)
  blocking collectives  12.1 us (22%)
  waiting for transfers between devices  11.2 us (21%)
  local copies, waits for them, and re-layouts  1.71 us (3%)
    all_to_all x1, blocking collectives, split_body(): lax.all_to_all(parts.reshape(devices, 16, 2 * TILE_SIDE), BOTH, 0, 0, til...  12.1 us
    ppermute x7, waiting for transfers between devices, swap(): return lax.ppermute(values, axis, [(i, i ^ distance) for i in range(size)])  10.8 us
    pallas_call x1, Pallas kernels, split_body(): pl.pallas_call(functools.partial(adjoint_kernel, panels, slots, n_src, 16...  10 us
    ppermute x7, starting transfers between devices, swap(): return lax.ppermute(values, axis, [(i, i ^ distance) for i in range(size)])  9.7 us
    all_to_all x1, starting transfers between devices, split_body(): lax.all_to_all(blocks.reshape(devices, share, 2 * LANES), BOTH, 0, 0, til...  4.42 us
    pallas_call x1, Pallas kernels, split_body(): pl.pallas_call(functools.partial(spectra_kernel, n_src), out_shape=jax.Sh...  2.83 us
  transfers between devices with their start and end apart: 8, of which 7 were waited for; matrix products, arithmetic and copies ran while one was open for 0% of the time, Pallas kernels for 2%

profile of v8, /device:TPU:0, one launch (start us, length us, event | category | flops | bytes accessed | tf_op | source)
XLA Modules:
  0.0 53.8 jit_solution(13437289323282819899)
XLA Ops:
  0.0 0.0 copy-start.1
  0.0 0.0 copy-start.2
  0.0 1.0 %constant_dynamic-slice_fusion = (bf16[16,2048]{1,0:T(8,128)(2,1)S(1)}, bf16[16,2048]{1,0:T(8,128)(2,1)S(1)}, bf16[16,2048]{1,0:T(8,128)(2,1)S(1)}, bf16[16,2048]{1,0:T(8,128)(2,1)S(1)}) fusion(bf16[64,2048]{1,0:T(8,128)(2,1)} %param.11, s32[]{:T(128)S(6)} %select_n.15, s32[]{:T(128)S(6)} %select_n.13, s32[]{:T(128)S(6)} %select_n.12, s32[]{:T(128)S(6)} %select_n.14), kind=kLoop, calls=%fused_computation.8 | loop fusion | bytes 524304 | tf_op jit(solution)/shard_map/dynamic_slice | solution.py:401
  1.0 5.1 %collective-permute-start.2 = (bf16[16,2048]{1,0:T(8,128)(2,1)S(1)}, bf16[16,2048]{1,0:T(8,128)(2,1)S(1)}, u32[]{:S(2)}, u32[]{:S(2)}) collective-permute-start(bf16[16,2048]{1,0:T(8,128)(2,1)S(1)} %get-tuple-element.37), channel_id=1, source_target_pairs={{0,3},{1,2},{2,1},{3,0},{4,7},{5,6},{6,5},{7,4},{8,11},{9,10},{10,... | collective-permute-start | bytes 196616 | tf_op jit(solution)/shard_map/ppermute | solution.py:389
  6.1 0.0 collective-permute-start
  6.1 0.0 copy-start.4
  6.1 0.0 copy-start.5
  6.1 0.0 copy-start.6
  6.1 0.6 %collective-permute-start.1 = (bf16[16,2048]{1,0:T(8,128)(2,1)S(1)}, bf16[16,2048]{1,0:T(8,128)(2,1)S(1)}, u32[]{:S(2)}, u32[]{:S(2)}) collective-permute-start(bf16[16,2048]{1,0:T(8,128)(2,1)S(1)} %get-tuple-element.40), channel_id=1, source_target_pairs={{0,2},{1,3},{2,0},{3,1},{4,6},{5,7},{6,4},{7,5},{8,10},{9,11},{10,... | collective-permute-start | bytes 196616 | tf_op jit(solution)/shard_map/ppermute | solution.py:389
  6.8 0.0 copy-done.1
  6.8 0.0 copy-done.2
  6.8 0.3 bank.1
  7.1 1.9 %collective-permute-done.2.refs_3_ = bf16[16,2048]{1,0:T(8,128)(2,1)S(1)} collective-permute-done((bf16[16,2048]{1,0:T(8,128)(2,1)S(1)}, bf16[16,2048]{1,0:T(8,128)(2,1)S(1)}, u32[]{:S(2)}, u32[]{:S(2)}) %collective-permute-start.2) | collective-permute-done | bytes 65568 | tf_op jit(solution)/shard_map/ppermute | solution.py:389
  9.0 1.7 %collective-permute-done.refs_1_ = bf16[16,2048]{1,0:T(8,128)(2,1)S(1)} collective-permute-done((bf16[16,2048]{1,0:T(8,128)(2,1)S(1)}, bf16[16,2048]{1,0:T(8,128)(2,1)S(1)}, u32[]{:S(2)}, u32[]{:S(2)}) %collective-permute-start) | collective-permute-done | bytes 65568 | tf_op jit(solution)/shard_map/ppermute | solution.py:389
  10.8 1.0 %collective-permute-done.1.refs_2_ = bf16[16,2048]{1,0:T(8,128)(2,1)S(1)} collective-permute-done((bf16[16,2048]{1,0:T(8,128)(2,1)S(1)}, bf16[16,2048]{1,0:T(8,128)(2,1)S(1)}, u32[]{:S(2)}, u32[]{:S(2)}) %collective-permute-start.1) | collective-permute-done | bytes 65568 | tf_op jit(solution)/shard_map/ppermute | solution.py:389
  11.8 0.0 copy-done.4
  11.8 0.0 copy-done.5
  11.8 0.0 copy-done.6
  11.8 2.8 %spectra.1 = bf16[512,256]{1,0:T(8,128)(2,1)} custom-call(bf16[16,2048]{1,0:T(8,128)(2,1)S(1)} %get-tuple-element.23.refs_0_, bf16[16,2048]{1,0:T(8,128)(2,1)S(1)} %collective-permute-done.refs_1_, bf16[16,2048]{1,0:T(8,128)(2,1)S(1)} %collective-permute-done.1.refs_2_, bf16[16,2048]{1,0:T(8,128)(2,1)S(1)} %collective-permute-done.2.refs_3_, ...), custom_call_target="tpu_custom_call" | custom-call | tf_op jit(solution)/shard_map/spectra/pallas_call | solution.py:428
  14.6 0.0 copy-start.8
  14.6 0.0 copy-start.7
  14.6 4.4 %all-to-all-start = ((bf16[32,16,256]{2,1,0:T(8,128)(2,1)}), bf16[32,16,256]{2,1,0:T(8,128)(2,1)S(1)}, u32[]{:S(2)}, u32[]{:S(2)}) async-start(bf16[32,16,256]{2,1,0:T(8,128)(2,1)} %bitcast), calls=%async_computation | async-start | bytes 524288 | tf_op jit(solution)/shard_map/all_to_all | solution.py:439
  19.0 0.0 copy-done.8
  19.1 0.0 copy-start.9
  19.1 0.7 %copy-done.9 = s32[4,64]{1,0:T(4,128)S(1)} copy-done((s32[4,64]{1,0:T(4,128)S(1)}, s32[4,64]{1,0:T(4,128)}, u32[]{:S(2)}) %copy-start.9) | copy-done | bytes 1048
  19.7 0.0 copy-done.7
  19.8 2.7 %collective-permute-start.5 = (bf16[80,512]{1,0:T(8,128)(2,1)S(1)}, bf16[80,512]{1,0:T(8,128)(2,1)S(1)}, u32[]{:S(2)}, u32[]{:S(2)}) collective-permute-start(bf16[80,512]{1,0:T(8,128)(2,1)S(1)} %fusion.4.refs_0_), channel_id=1, source_target_pairs={{0,24},{4,28},{8,16},{12,20},{16,8},{20,12},{24,0},{28,4},{1,25},{... | collective-permute-start | bytes 245768 | tf_op jit(solution)/shard_map/ppermute | solution.py:389
  22.5 0.6 %collective-permute-start.4 = (bf16[80,512]{1,0:T(8,128)(2,1)S(1)}, bf16[80,512]{1,0:T(8,128)(2,1)S(1)}, u32[]{:S(2)}, u32[]{:S(2)}) collective-permute-start(bf16[80,512]{1,0:T(8,128)(2,1)S(1)} %fusion.4.refs_0_), channel_id=1, source_target_pairs={{0,16},{4,20},{8,24},{12,28},{16,0},{20,4},{24,8},{28,12},{1,17},{... | collective-permute-start | bytes 245768 | tf_op jit(solution)/shard_map/ppermute | solution.py:389
  23.1 0.3 collective-permute-start.3
  23.3 3.7 %collective-permute-done.5.refs_3_ = bf16[80,512]{1,0:T(8,128)(2,1)S(1)} collective-permute-done((bf16[80,512]{1,0:T(8,128)(2,1)S(1)}, bf16[80,512]{1,0:T(8,128)(2,1)S(1)}, u32[]{:S(2)}, u32[]{:S(2)}) %collective-permute-start.5) | collective-permute-done | bytes 81952 | tf_op jit(solution)/shard_map/ppermute | solution.py:389
  27.0 1.9 %collective-permute-done.4.refs_2_ = bf16[80,512]{1,0:T(8,128)(2,1)S(1)} collective-permute-done((bf16[80,512]{1,0:T(8,128)(2,1)S(1)}, bf16[80,512]{1,0:T(8,128)(2,1)S(1)}, u32[]{:S(2)}, u32[]{:S(2)}) %collective-permute-start.4) | collective-permute-done | bytes 81952 | tf_op jit(solution)/shard_map/ppermute | solution.py:389
  28.9 0.0 collective-permute-done.3.refs_1_
  28.9 0.4 all-to-all-done
  29.2 0.0 copy-start
  29.2 0.4 collective-permute-start.6
  29.6 0.5 pick.1
  30.2 0.6 %collective-permute-done.6.refs_9_ = bf16[512,256]{1,0:T(8,128)(2,1)S(1)} collective-permute-done((bf16[512,256]{1,0:T(8,128)(2,1)S(1)}, bf16[512,256]{1,0:T(8,128)(2,1)S(1)}, u32[]{:S(2)}, u32[]{:S(2)}) %collective-permute-start.6) | collective-permute-done | bytes 262176 | tf_op jit(solution)/shard_map/ppermute | solution.py:389
  30.8 0.0 copy-done
  30.8 10.0 %adjoint.1 = bf16[512,128]{1,0:T(8,128)(2,1)S(1)} custom-call(bf16[80,512]{1,0:T(8,128)(2,1)S(1)} %fusion.4.refs_0_, bf16[80,512]{1,0:T(8,128)(2,1)S(1)} %collective-permute-done.3.refs_1_, bf16[80,512]{1,0:T(8,128)(2,1)S(1)} %collective-permute-done.4.refs_2_, bf16[80,512]{1,0:T(8,128)(2,1)S(1)} %collective-permute-done.5.refs_3_, ...), custom_call_target="tpu_custom_call" | custom-call | tf_op jit(solution)/shard_map/adjoint/pallas_call | solution.py:455
  40.8 0.0 copy-start.3
  40.8 12.1 %all_to_all.10 = bf16[32,16,128]{2,1,0:T(8,128)(2,1)S(1)} all-to-all(bf16[32,16,128]{2,1,0:T(8,128)(2,1)S(1)} %bitcast.7), channel_id=1, replica_groups=mesh['blk'=8,'src'=4] {'blk','src'}, dimensions={0} | all-to-all | bytes 262144 | tf_op jit(solution)/shard_map/all_to_all | solution.py:466
  52.9 0.0 copy-done.3
  52.9 0.8 %image.1 = f32[4,512]{1,0:T(4,128)} custom-call(bf16[8,32,512]{2,1,0:T(8,128)(2,1)S(1)} %copy-done.3, bf16[512,128]{1,0:T(8,128)(2,1)S(1)} %bitcast.8), custom_call_target="tpu_custom_call" | custom-call | tf_op jit(solution)/shard_map/image/pallas_call | solution.py:469
  (4 shorter events, 0.0 us)
Async XLA Ops:
  0.0 6.8 %copy-start.1 = (bf16[64,2,1024]{2,1,0:T(2,128)(2,1)S(1)}, bf16[64,2,1024]{2,1,0:T(2,128)(2,1)}, u32[]{:S(2)}) copy-start(bf16[64,2,1024]{2,1,0:T(2,128)(2,1)} %observed_ref.1) | copy-start | bytes 786436
  0.0 6.8 %copy-start.2 = (bf16[64,2,1024]{2,1,0:T(2,128)(2,1)S(1)}, bf16[64,2,1024]{2,1,0:T(2,128)(2,1)}, u32[]{:S(2)}) copy-start(bf16[64,2,1024]{2,1,0:T(2,128)(2,1)} %green_ref.1) | copy-start | bytes 786436
  1.0 8.0 %collective-permute-start.2 = (bf16[16,2048]{1,0:T(8,128)(2,1)S(1)}, bf16[16,2048]{1,0:T(8,128)(2,1)S(1)}, u32[]{:S(2)}, u32[]{:S(2)}) collective-permute-start(bf16[16,2048]{1,0:T(8,128)(2,1)S(1)} %get-tuple-element.37), channel_id=1, source_target_pairs={{0,3},{1,2},{2,1},{3,0},{4,7},{5,6},{6,5},{7,4},{8,11},{9,10},{10,... | collective-permute-start | bytes 196616 | tf_op jit(solution)/shard_map/ppermute | solution.py:389
  6.1 4.6 %collective-permute-start = (bf16[16,2048]{1,0:T(8,128)(2,1)S(1)}, bf16[16,2048]{1,0:T(8,128)(2,1)S(1)}, u32[]{:S(2)}, u32[]{:S(2)}) collective-permute-start(bf16[16,2048]{1,0:T(8,128)(2,1)S(1)} %get-tuple-element.38), channel_id=1, source_target_pairs={{0,1},{1,0},{2,3},{3,2},{4,5},{5,4},{6,7},{7,6},{8,9},{9,8},{10,11... | collective-permute-start | bytes 196616 | tf_op jit(solution)/shard_map/ppermute | solution.py:389
  6.1 5.6 %copy-start.4 = (f32[2,128,128]{2,1,0:T(8,128)S(1)}, f32[2,128,128]{2,1,0:T(8,128)}, u32[]{:S(2)}) copy-start(f32[2,128,128]{2,1,0:T(8,128)} %constant.29.clone.refs_5_) | copy-start | bytes 393220
  6.1 5.6 %copy-start.5 = (bf16[128,256]{1,0:T(8,128)(2,1)S(1)}, bf16[128,256]{1,0:T(8,128)(2,1)}, u32[]{:S(2)}) copy-start(bf16[128,256]{1,0:T(8,128)(2,1)} %constant.30.clone.refs_6_) | copy-start | bytes 196612
  6.1 5.6 %copy-start.6 = (bf16[256,64]{1,0:T(8,128)(2,1)S(1)}, bf16[256,64]{1,0:T(8,128)(2,1)}, u32[]{:S(2)}) copy-start(bf16[256,64]{1,0:T(8,128)(2,1)} %constant.28.clone.refs_4_) | copy-start | bytes 98308
  6.1 5.6 %collective-permute-start.1 = (bf16[16,2048]{1,0:T(8,128)(2,1)S(1)}, bf16[16,2048]{1,0:T(8,128)(2,1)S(1)}, u32[]{:S(2)}, u32[]{:S(2)}) collective-permute-start(bf16[16,2048]{1,0:T(8,128)(2,1)S(1)} %get-tuple-element.40), channel_id=1, source_target_pairs={{0,2},{1,3},{2,0},{3,1},{4,6},{5,7},{6,4},{7,5},{8,10},{9,11},{10,... | collective-permute-start | bytes 196616 | tf_op jit(solution)/shard_map/ppermute | solution.py:389
  14.6 4.4 %copy-start.8 = (s32[4,64]{1,0:T(4,128)S(1)}, s32[4,64]{1,0:T(4,128)}, u32[]{:S(2)}) copy-start(s32[4,64]{1,0:T(4,128)} %param.15) | copy-start | bytes 3076
  14.6 5.1 %copy-start.7 = (s32[64,512]{1,0:T(8,128)S(1)}, s32[64,512]{1,0:T(8,128)}, u32[]{:S(2)}) copy-start(s32[64,512]{1,0:T(8,128)} %param.13) | copy-start | bytes 393220
  14.6 14.6 %all-to-all-start = ((bf16[32,16,256]{2,1,0:T(8,128)(2,1)}), bf16[32,16,256]{2,1,0:T(8,128)(2,1)S(1)}, u32[]{:S(2)}, u32[]{:S(2)}) async-start(bf16[32,16,256]{2,1,0:T(8,128)(2,1)} %bitcast), calls=%async_computation | async-start | bytes 524288 | tf_op jit(solution)/shard_map/all_to_all | solution.py:439
  19.1 0.7 %copy-start.9 = (s32[4,64]{1,0:T(4,128)S(1)}, s32[4,64]{1,0:T(4,128)}, u32[]{:S(2)}) copy-start(s32[4,64]{1,0:T(4,128)} %param.16) | copy-start | bytes 3076
  19.8 7.2 %collective-permute-start.5 = (bf16[80,512]{1,0:T(8,128)(2,1)S(1)}, bf16[80,512]{1,0:T(8,128)(2,1)S(1)}, u32[]{:S(2)}, u32[]{:S(2)}) collective-permute-start(bf16[80,512]{1,0:T(8,128)(2,1)S(1)} %fusion.4.refs_0_), channel_id=1, source_target_pairs={{0,24},{4,28},{8,16},{12,20},{16,8},{20,12},{24,0},{28,4},{1,25},{... | collective-permute-start | bytes 245768 | tf_op jit(solution)/shard_map/ppermute | solution.py:389
  22.5 6.4 %collective-permute-start.4 = (bf16[80,512]{1,0:T(8,128)(2,1)S(1)}, bf16[80,512]{1,0:T(8,128)(2,1)S(1)}, u32[]{:S(2)}, u32[]{:S(2)}) collective-permute-start(bf16[80,512]{1,0:T(8,128)(2,1)S(1)} %fusion.4.refs_0_), channel_id=1, source_target_pairs={{0,16},{4,20},{8,24},{12,28},{16,0},{20,4},{24,8},{28,12},{1,17},{... | collective-permute-start | bytes 245768 | tf_op jit(solution)/shard_map/ppermute | solution.py:389
  23.1 5.8 %collective-permute-start.3 = (bf16[80,512]{1,0:T(8,128)(2,1)S(1)}, bf16[80,512]{1,0:T(8,128)(2,1)S(1)}, u32[]{:S(2)}, u32[]{:S(2)}) collective-permute-start(bf16[80,512]{1,0:T(8,128)(2,1)S(1)} %fusion.4.refs_0_), channel_id=1, source_target_pairs={{0,8},{4,12},{8,0},{12,4},{16,24},{20,28},{24,16},{28,20},{1,9},{5... | collective-permute-start | bytes 245768 | tf_op jit(solution)/shard_map/ppermute | solution.py:389
  29.2 1.6 %copy-start = (bf16[256,512]{1,0:T(8,128)(2,1)S(1)}, bf16[256,512]{1,0:T(8,128)(2,1)}, u32[]{:S(2)}) copy-start(bf16[256,512]{1,0:T(8,128)(2,1)} %constant.31.clone.refs_10_) | copy-start | bytes 786436
  29.2 1.6 %collective-permute-start.6 = (bf16[512,256]{1,0:T(8,128)(2,1)S(1)}, bf16[512,256]{1,0:T(8,128)(2,1)S(1)}, u32[]{:S(2)}, u32[]{:S(2)}) collective-permute-start(bf16[512,256]{1,0:T(8,128)(2,1)S(1)} %bitcast.4), channel_id=1, source_target_pairs={{0,4},{4,0},{8,12},{12,8},{16,20},{20,16},{24,28},{28,24},{1,5},{5... | collective-permute-start | bytes 786440 | tf_op jit(solution)/shard_map/ppermute | solution.py:389
  40.8 12.1 %copy-start.3 = (bf16[8,32,512]{2,1,0:T(8,128)(2,1)S(1)}, bf16[8,32,512]{2,1,0:T(8,128)(2,1)}, u32[]{:S(2)}) copy-start(bf16[8,32,512]{2,1,0:T(8,128)(2,1)} %constant.32.clone.high_ref) | copy-start | bytes 786436
